TPU v7x, 256 devices: a whole 4x4x8 slice. The times are simulated.
256 devices in a mesh: row: 16 (over z, x_hi), col: 16 (over x_lo, y, core).
Axes of the slice: x: 4 (x_hi: 2, x_lo: 2; x = x_hi * 2 + x_lo), y: 4, z: 8, core: 2. Of those that a mesh axis runs over, the one named last changes fastest.
Arguments:
- blocks: bfloat16 [16, 16, 16, 64, 1024], P('row', 'col'), may hold values from -6 to 6
- order: int32 [16, 16, 16], P('row', 'col'), may hold values from 0 to 15, each once within a row
- cross_weights: bfloat16 [6, 16, 16, 8, 128, 128], P(None, 'row', 'col'), may hold values from -0.5 to 0.5
- local_weights: bfloat16 [12, 16, 16, 8, 128, 128], P(None, 'row', 'col'), may hold values from -0.5 to 0.5
Outputs:
- result: bfloat16 [16, 16, 16, 64, 1024], P('row', 'col')
Inputs may be any that keep to these rules, and one draw needn't show every extreme that they name: Each rank's row of order is a permutation of 0 to 15.
All inputs are finite; a program needn't handle non-finite values.
Results may differ from a plain program's by a relative error of at most 0.033.
Values may be sent and summed in bfloat16 or wider, within the bound.
No kernel may reach another device: no remote copies, remote signals or barrier semaphores. Data moves between devices by JAX's collectives and lax.ppermute only.
A program may use at most 64 MiB of HBM per device.

v0:
```python
import jax
import jax.numpy as jnp
from jax import lax
from jax.sharding import PartitionSpec as P

SECTIONS = 3
LOCAL = 4


def swapped(shard, axis, distance):
    return lax.ppermute(shard, axis, [(i, i ^ 1 << distance) for i in range(lax.axis_size(axis))])


def pair_products(weight, stacked):
    return jnp.einsum("hij,hjs->his", weight, stacked, preferred_element_type=jnp.float32)


def regroup(product):
    shape = product.shape
    return product.reshape(shape[0] * 2, shape[1] // 2, shape[2]).astype(jnp.bfloat16)


def via_halves(coeffs, weight, side_flag, move_half):
    half_count = coeffs.shape[0] // 2
    upper_side = side_flag == 1
    lower, upper = (coeffs[:half_count], coeffs[half_count:])
    keeping = jnp.where(upper_side, upper, lower)
    sending = jnp.where(upper_side, lower, upper)
    arriving = move_half(sending)
    top = jnp.where(upper_side, arriving, keeping)
    bottom = jnp.where(upper_side, keeping, arriving)
    product = pair_products(weight, jnp.concatenate([top, bottom], axis=1))
    return regroup(product)


def local_level(coeffs, weight):
    half_count = coeffs.shape[0] // 2
    stacked = jnp.concatenate([coeffs[:half_count], coeffs[half_count:]], axis=1)
    return regroup(pair_products(weight, stacked))


def shards(blocks, order, cross_weights, local_weights):
    coeffs = jnp.take(blocks[0, 0], order[0, 0], axis=0)
    cross_local = cross_weights[:, 0, 0]
    local_all = local_weights[:, 0, 0]
    row_bits = lax.axis_size("row").bit_length() - 1
    col_bits = lax.axis_size("col").bit_length() - 1
    row_place = lax.axis_index("row")
    col_place = lax.axis_index("col")
    for section_index in range(SECTIONS):
        row_bit = section_index % row_bits
        col_bit = section_index % col_bits
        row_flag = row_place >> row_bit & 1
        col_flag = col_place >> col_bit & 1
        row_weight = cross_local[2 * section_index]
        col_weight = cross_local[2 * section_index + 1]
        coeffs = via_halves(
            coeffs, row_weight, row_flag, lambda piece: swapped(piece, "row", row_bit)
        )
        coeffs = via_halves(
            coeffs, col_weight, col_flag, lambda piece: swapped(piece, "col", col_bit)
        )
        for level_index in range(LOCAL):
            coeffs = local_level(coeffs, local_all[section_index * LOCAL + level_index])
    return coeffs[None, None]


def solution(mesh):
    placed = (
        P("row", "col", None, None, None),
        P("row", "col", None),
        P(None, "row", "col", None, None, None),
        P(None, "row", "col", None, None, None),
    )
    return jax.shard_map(
        shards,
        mesh=mesh,
        in_specs=placed,
        out_specs=P("row", "col", None, None, None),
        check_vma=False,
    )
```

profile of v0, /device:TPU:6, one launch (start us, length us, event | category | flops | bytes accessed | tf_op | source)
XLA Modules:
  0.0 199.3 jit_solution(14628926066098315702)
XLA Ops:
  0.0 0.0 copy-start
  0.0 0.8 fusion.145
  0.8 0.7 compare_and_fusion
  1.5 0.1 copy-done
  1.6 2.0 %gather_fusion = bf16[16,64,1024]{2,1,0:T(8,128)(2,1)} fusion(bf16[16,64,1024]{2,1,0:T(8,128)(2,1)S(1)} %bitcast.132, s32[1024]{0:T(1024)S(1)} %pad_clamp_fusion), kind=kCustom, calls=%fused_computation | custom fusion | bytes 4194368 | tf_op jit(solution)/shard_map/jit(_take)/gather | solution.py:43
  3.6 1.9 broadcast_select_fusion
  5.5 0.1 broadcast_select_fusion.4
  5.6 1.5 collective-permute-start
  7.1 25.1 %collective-permute-done = bf16[8,64,1024]{2,1,0:T(8,128)(2,1)} collective-permute-done((bf16[8,64,1024]{2,1,0:T(8,128)(2,1)S(1)}, bf16[8,64,1024]{2,1,0:T(8,128)(2,1)}, u32[]{:S(2)}, u32[]{:S(2)}) %collective-permute-start) | collective-permute-done | bytes 1048608 | tf_op jit(solution)/shard_map/ppermute | solution.py:11
  32.2 1.4 broadcast_select_fusion.2
  33.6 1.6 convert_bitcast_fusion.16
  35.2 1.1 broadcast_select_fusion.6
  36.4 0.0 collective-permute-start.1
  36.4 2.9 %collective-permute-done.1 = bf16[8,64,1024]{2,1,0:T(8,128)(2,1)S(1)} collective-permute-done((bf16[8,64,1024]{2,1,0:T(8,128)(2,1)}, bf16[8,64,1024]{2,1,0:T(8,128)(2,1)S(1)}, u32[]{:S(2)}, u32[]{:S(2)}) %collective-permute-start.1) | collective-permute-done | bytes 1048608 | tf_op jit(solution)/shard_map/ppermute | solution.py:11
  39.2 0.1 broadcast_select_fusion.8
  39.4 1.6 convert_bitcast_fusion.15
  41.0 0.2 fusion.175
  41.2 1.6 convert_bitcast_fusion.14
  42.9 0.2 fusion.174
  43.1 1.6 convert_bitcast_fusion.13
  44.7 0.2 fusion.173
  44.9 1.6 convert_bitcast_fusion.12
  46.5 0.2 fusion.172
  46.7 1.6 convert_bitcast_fusion.11
  48.4 1.1 broadcast_select_fusion.10
  49.5 1.9 collective-permute-start.2
  51.4 23.7 %collective-permute-done.2 = bf16[8,64,1024]{2,1,0:T(8,128)(2,1)S(1)} collective-permute-done((bf16[8,64,1024]{2,1,0:T(8,128)(2,1)}, bf16[8,64,1024]{2,1,0:T(8,128)(2,1)S(1)}, u32[]{:S(2)}, u32[]{:S(2)}) %collective-permute-start.2) | collective-permute-done | bytes 1048608 | tf_op jit(solution)/shard_map/ppermute | solution.py:11
  75.1 0.1 broadcast_select_fusion.12
  75.2 1.6 convert_bitcast_fusion.10
  76.9 1.1 broadcast_select_fusion.14
  78.0 1.6 collective-permute-start.3
  79.6 23.2 %collective-permute-done.3 = bf16[8,64,1024]{2,1,0:T(8,128)(2,1)S(1)} collective-permute-done((bf16[8,64,1024]{2,1,0:T(8,128)(2,1)}, bf16[8,64,1024]{2,1,0:T(8,128)(2,1)S(1)}, u32[]{:S(2)}, u32[]{:S(2)}) %collective-permute-start.3) | collective-permute-done | bytes 1048608 | tf_op jit(solution)/shard_map/ppermute | solution.py:11
  102.8 0.1 broadcast_select_fusion.16
  102.9 1.6 convert_bitcast_fusion.9
  104.6 0.2 fusion.171
  104.8 1.6 convert_bitcast_fusion.8
  106.4 0.2 fusion.170
  106.6 1.6 convert_bitcast_fusion.7
  108.2 0.2 fusion.169
  108.4 1.6 convert_bitcast_fusion.6
  110.1 0.2 fusion.168
  110.3 1.6 convert_bitcast_fusion.5
  111.9 1.1 broadcast_select_fusion.18
  113.0 3.3 %collective-permute-start.4 = (bf16[8,64,1024]{2,1,0:T(8,128)(2,1)}, bf16[8,64,1024]{2,1,0:T(8,128)(2,1)S(1)}, u32[]{:S(2)}, u32[]{:S(2)}) collective-permute-start(bf16[8,64,1024]{2,1,0:T(8,128)(2,1)} %bitcast.50), channel_id=1, source_target_pairs={{0,64},{16,80},{32,96},{48,112},{64,0},{80,16},{96,32},{112,48},{1... | collective-permute-start | bytes 3145736 | tf_op jit(solution)/shard_map/ppermute | solution.py:11
  116.3 44.6 %collective-permute-done.4 = bf16[8,64,1024]{2,1,0:T(8,128)(2,1)S(1)} collective-permute-done((bf16[8,64,1024]{2,1,0:T(8,128)(2,1)}, bf16[8,64,1024]{2,1,0:T(8,128)(2,1)S(1)}, u32[]{:S(2)}, u32[]{:S(2)}) %collective-permute-start.4) | collective-permute-done | bytes 1048608 | tf_op jit(solution)/shard_map/ppermute | solution.py:11
  160.9 0.1 broadcast_select_fusion.20
  161.0 1.6 convert_bitcast_fusion.4
  162.7 0.1 broadcast_select_fusion.22
  162.8 3.3 %collective-permute-start.5 = (bf16[8,64,1024]{2,1,0:T(8,128)(2,1)S(1)}, bf16[8,64,1024]{2,1,0:T(8,128)(2,1)S(1)}, u32[]{:S(2)}, u32[]{:S(2)}) collective-permute-start(bf16[8,64,1024]{2,1,0:T(8,128)(2,1)S(1)} %bitcast.162), channel_id=1, source_target_pairs={{0,4},{1,5},{2,6},{3,7},{4,0},{5,1},{6,2},{7,3},{8,12},{9,13},{10,... | collective-permute-start | bytes 3145736 | tf_op jit(solution)/shard_map/ppermute | solution.py:11
  166.1 22.5 %collective-permute-done.5 = bf16[8,64,1024]{2,1,0:T(8,128)(2,1)S(1)} collective-permute-done((bf16[8,64,1024]{2,1,0:T(8,128)(2,1)S(1)}, bf16[8,64,1024]{2,1,0:T(8,128)(2,1)S(1)}, u32[]{:S(2)}, u32[]{:S(2)}) %collective-permute-start.5) | collective-permute-done | bytes 1048608 | tf_op jit(solution)/shard_map/ppermute | solution.py:11
  188.6 0.1 broadcast_select_fusion.24
  188.8 1.6 convert_bitcast_fusion.3
  190.4 0.2 fusion.167
  190.6 1.6 convert_bitcast_fusion.2
  192.3 0.2 fusion.166
  192.5 1.6 convert_bitcast_fusion.1
  194.1 0.2 fusion.165
  194.3 1.6 convert_bitcast_fusion
  196.0 0.2 fusion.164
  196.1 0.0 copy-start.1
  196.1 3.1 %fusion.72 = bf16[8,1024,128]{1,2,0:T(8,128)(2,1)} fusion(bf16[8,64,1024]{2,1,0:T(8,128)(2,1)S(1)} %bitcast.161, bf16[8,64,1024]{2,1,0:T(8,128)(2,1)S(1)} %bitcast.160, bf16[12,1,1,8,128,128]{5,4,3,2,1,0:T(8,128)(2,1)} %param.7), kind=kOutput, calls=%fused_computation.91 | convolution fusion | flops 273678336 | bytes 4456448 | tf_op jit(solution)/shard_map/hij,hjs->his/dot_general | solution.py:15
  199.3 0.0 copy-done.1
  (1 shorter events, 0.0 us)
Async XLA Ops:
  0.0 1.6 copy-start
  5.6 26.6 %collective-permute-start = (bf16[8,64,1024]{2,1,0:T(8,128)(2,1)S(1)}, bf16[8,64,1024]{2,1,0:T(8,128)(2,1)}, u32[]{:S(2)}, u32[]{:S(2)}) collective-permute-start(bf16[8,64,1024]{2,1,0:T(8,128)(2,1)S(1)} %broadcast_select_fusion.4), channel_id=1, source_target_pairs={{0,16},{16,0},{32,48},{48,32},{64,80},{80,64},{96,112},{112,96},{1... | collective-permute-start | bytes 3145736 | tf_op jit(solution)/shard_map/ppermute | solution.py:11
  36.4 2.9 %collective-permute-start.1 = (bf16[8,64,1024]{2,1,0:T(8,128)(2,1)}, bf16[8,64,1024]{2,1,0:T(8,128)(2,1)S(1)}, u32[]{:S(2)}, u32[]{:S(2)}) collective-permute-start(bf16[8,64,1024]{2,1,0:T(8,128)(2,1)} %bitcast.6), channel_id=1, source_target_pairs={{0,1},{1,0},{2,3},{3,2},{4,5},{5,4},{6,7},{7,6},{8,9},{9,8},{10,11... | collective-permute-start | bytes 3145736 | tf_op jit(solution)/shard_map/ppermute | solution.py:11
  49.5 25.6 %collective-permute-start.2 = (bf16[8,64,1024]{2,1,0:T(8,128)(2,1)}, bf16[8,64,1024]{2,1,0:T(8,128)(2,1)S(1)}, u32[]{:S(2)}, u32[]{:S(2)}) collective-permute-start(bf16[8,64,1024]{2,1,0:T(8,128)(2,1)} %bitcast.26), channel_id=1, source_target_pairs={{0,32},{16,48},{32,0},{48,16},{64,96},{80,112},{96,64},{112,80},{1... | collective-permute-start | bytes 3145736 | tf_op jit(solution)/shard_map/ppermute | solution.py:11
  78.0 24.8 %collective-permute-start.3 = (bf16[8,64,1024]{2,1,0:T(8,128)(2,1)}, bf16[8,64,1024]{2,1,0:T(8,128)(2,1)S(1)}, u32[]{:S(2)}, u32[]{:S(2)}) collective-permute-start(bf16[8,64,1024]{2,1,0:T(8,128)(2,1)} %bitcast.30), channel_id=1, source_target_pairs={{0,2},{1,3},{2,0},{3,1},{4,6},{5,7},{6,4},{7,5},{8,10},{9,11},{10,... | collective-permute-start | bytes 3145736 | tf_op jit(solution)/shard_map/ppermute | solution.py:11
  113.0 47.9 %collective-permute-start.4 = (bf16[8,64,1024]{2,1,0:T(8,128)(2,1)}, bf16[8,64,1024]{2,1,0:T(8,128)(2,1)S(1)}, u32[]{:S(2)}, u32[]{:S(2)}) collective-permute-start(bf16[8,64,1024]{2,1,0:T(8,128)(2,1)} %bitcast.50), channel_id=1, source_target_pairs={{0,64},{16,80},{32,96},{48,112},{64,0},{80,16},{96,32},{112,48},{1... | collective-permute-start | bytes 3145736 | tf_op jit(solution)/shard_map/ppermute | solution.py:11
  162.8 25.8 %collective-permute-start.5 = (bf16[8,64,1024]{2,1,0:T(8,128)(2,1)S(1)}, bf16[8,64,1024]{2,1,0:T(8,128)(2,1)S(1)}, u32[]{:S(2)}, u32[]{:S(2)}) collective-permute-start(bf16[8,64,1024]{2,1,0:T(8,128)(2,1)S(1)} %bitcast.162), channel_id=1, source_target_pairs={{0,4},{1,5},{2,6},{3,7},{4,0},{5,1},{6,2},{7,3},{8,12},{9,13},{10,... | collective-permute-start | bytes 3145736 | tf_op jit(solution)/shard_map/ppermute | solution.py:11
  196.1 3.1 %copy-start.1 = (bf16[1,1,16,64,1024]{4,3,2,1,0:T(8,128)(2,1)S(1)}, bf16[1,1,16,64,1024]{4,3,2,1,0:T(8,128)(2,1)}, u32[]{:S(2)}) copy-start(bf16[1,1,16,64,1024]{4,3,2,1,0:T(8,128)(2,1)} %param.4) | copy-start | bytes 6291460
where the time goes:
time: 200 us; the launch traced here: 199 us
  waiting for transfers between devices  142 us (71%)
  matrix products  31.2 us (16%)
  starting transfers between devices  11.5 us (6%)
  other arithmetic  10.1 us (5%)
  local copies, waits for them, and re-layouts  4.21 us (2%)
    ppermute x6, waiting for transfers between devices, swapped(): lax.ppermute(shard, axis, [(i, i ^ 1 << distance) for i in range(lax.axis...  142 us
    dot_general x18, matrix products, pair_products(): jnp.einsum('hij,hjs->his', weight, stacked, preferred_element_type=jnp.fl...  31.2 us
    ppermute x6, starting transfers between devices, swapped(): lax.ppermute(shard, axis, [(i, i ^ 1 << distance) for i in range(lax.axis...  11.5 us
    select_n x6, other arithmetic, via_halves(): sending = jnp.where(upper_side, lower, upper)  4.7 us
  transfers between devices with their start and end apart: 6, of which 6 were waited for; matrix products, arithmetic and copies ran while one was open for 0% of the time, Pallas kernels for 0%

commit v1 on v0

v1 whole, which is shorter than its diff:
```python
import functools

import jax
import jax.numpy as jnp
from jax import lax
from jax.experimental import pallas as pl
from jax.experimental.pallas import tpu as pltpu
from jax.sharding import PartitionSpec as P

SECTIONS = 3
LOCAL = 4
SIZES = (256, 256, 256, 256)
ORDER = (0, 1, 0, 3, 1, 0, 2, 3, 1, 0, 2, 3, 1, 0, 2, 3, 1, 2, 3, 1, 0, 2, 3, 2)
LIMIT = 8 * 2**20

VM = pl.BlockSpec(memory_space=pltpu.VMEM)
ANY = pl.BlockSpec(memory_space=pl.ANY)


def in_vmem(shape):
    return pltpu.VMEM(shape, jnp.bfloat16)


def held(x):
    return pltpu.with_memory_space_constraint(x, pltpu.VMEM)


def outside(x):
    return pltpu.with_memory_space_constraint(x, pltpu.HBM)


def swapped(piece, axis, bit):
    return lax.ppermute(piece, axis, [(i, i ^ 1 << bit) for i in range(lax.axis_size(axis))])


def side(level):
    return lax.axis_index(("row", "col")[level % 2]) >> (level // 2) & 1


def call(kernel, name, out_shape, in_specs, out_specs, scratch=(), aliases=None):
    return pl.pallas_call(
        kernel,
        out_shape=out_shape,
        in_specs=in_specs,
        out_specs=out_specs,
        scratch_shapes=list(scratch),
        input_output_aliases=aliases or {},
        compiler_params=pltpu.CompilerParams(vmem_limit_bytes=LIMIT),
        cost_estimate=pl.CostEstimate(flops=1, bytes_accessed=1, transcendentals=0),
        name=name,
    )


def picked(source, order, first, start, columns, out):
    for j in range(8):
        out[j] = source[order[0, first + j], :, start : start + columns]


def first_kernel(columns, order_any, blocks, held_blocks, keep, send, order, sems):
    index = pltpu.make_async_copy(order_any, order, sems.at[0])
    index.start()
    copies = [
        pltpu.make_async_copy(blocks.at[pl.ds(2 * j, 2)], held_blocks.at[pl.ds(2 * j, 2)], sems.at[1 + j])
        for j in range(8)
    ]
    for copy in copies:
        copy.start()
    index.wait()
    for copy in copies:
        copy.wait()
    upper = side(0)
    picked(held_blocks, order, 8 - 8 * upper, 0, columns, send)
    picked(held_blocks, order, 8 * upper, 0, columns, keep)


def first_take(order, blocks, columns):
    half = in_vmem((8, 64, columns))
    return call(
        functools.partial(first_kernel, columns),
        "take_first",
        (in_vmem(blocks.shape), half, half),
        [ANY, ANY],
        (VM, VM, VM),
        [pltpu.SMEM((1, 16), jnp.int32), pltpu.SemaphoreType.DMA((9,))],
    )(outside(order[None]), outside(blocks))


def later_kernel(starts, sizes, order_any, blocks, token, *refs):
    outs, order, sem = refs[:-2], refs[-2], refs[-1]
    index = pltpu.make_async_copy(order_any, order, sem)
    index.start()
    index.wait()
    upper = side(0)
    for c, (start, columns) in enumerate(zip(starts, sizes)):
        picked(blocks, order, 8 - 8 * upper, start, columns, outs[2 * c + 1])
        picked(blocks, order, 8 * upper, start, columns, outs[2 * c])


def later_takes(order, blocks, token, starts, sizes):
    halves = [in_vmem((8, 64, n)) for n in sizes for _ in range(2)]
    outs = call(
        functools.partial(later_kernel, starts, sizes),
        "take_later",
        tuple(halves),
        [ANY, VM, ANY],
        (VM,) * len(halves),
        [pltpu.SMEM((1, 16), jnp.int32), pltpu.SemaphoreType.DMA],
    )(outside(order[None]), held(blocks), token)
    return list(zip(outs[::2], outs[1::2]))


def crossed(keep, arrived, weight, upper, h):
    own, other = keep[h], arrived[h]
    top = jnp.where(upper == 1, other, own)
    bottom = jnp.where(upper == 1, own, other)
    stacked = jnp.concatenate([top, bottom], axis=0)
    product = jnp.dot(weight[h], stacked, preferred_element_type=jnp.float32)
    return product.astype(jnp.bfloat16).reshape(2, 64, stacked.shape[1])


def row_kernel(level, keep, arrived, cross, token, keep_out, send_out):
    upper, later = side(level), side(level + 1)
    weight = cross.at[level]
    for p in range(4):
        send_out[2 * p : 2 * p + 2] = crossed(keep, arrived, weight, upper, 4 - 4 * later + p)
    for p in range(4):
        keep_out[2 * p : 2 * p + 2] = crossed(keep, arrived, weight, upper, 4 * later + p)


def row_level(level, keep, arrived, cross, token):
    half = in_vmem(keep.shape)
    return call(
        functools.partial(row_kernel, level),
        f"row_{level}",
        (half, half),
        [VM, VM, VM, ANY],
        (VM, VM),
    )(held(keep), held(arrived), cross, token)


def combined(first, second, upper, out):
    for j in range(4):
        halves = []
        for g in (j, 4 + j):
            weight = first[g]
            if upper is not None:
                turned = jnp.concatenate([weight[:, 64:], weight[:, :64]], axis=1)
                weight = jnp.where(upper == 1, turned, weight)
            halves.append(weight)
        for t in range(2):
            for i in range(2):
                out[j, 128 * t : 128 * t + 128, 128 * i : 128 * i + 128] = jnp.dot(
                    second[2 * j + t][:, 64 * i : 64 * i + 64],
                    halves[i][64 * t : 64 * t + 64],
                    preferred_element_type=jnp.float32,
                ).astype(jnp.bfloat16)


def combine_kernel(cross, local, token, *outs):
    for section in range(SECTIONS):
        level, k = 2 * section + 1, section * LOCAL
        combined(cross.at[level], local.at[k], side(level), outs[2 * section])
        combined(local.at[k + 1], local.at[k + 2], None, outs[2 * section + 1])


def combine(cross, local, token):
    return call(
        combine_kernel,
        "combine",
        (in_vmem((4, 256, 256)),) * (2 * SECTIONS),
        [VM, VM, ANY],
        (VM,) * (2 * SECTIONS),
    )(cross, local, token)


def four(weight, blocks):
    stacked = jnp.concatenate(blocks, axis=0)
    product = jnp.dot(weight, stacked, preferred_element_type=jnp.float32)
    return product.astype(jnp.bfloat16).reshape(4, 64, stacked.shape[1])


def mixed(buf, source, weight, h):
    stacked = jnp.concatenate([buf[source, h], buf[source, 8 + h]], axis=0)
    product = jnp.dot(weight, stacked, preferred_element_type=jnp.float32)
    return product.astype(jnp.bfloat16).reshape(2, 64, stacked.shape[1])


def col_levels(keep, arrived, early, late, buf):
    for j in range(4):
        buf[0, 4 * j : 4 * j + 4] = four(
            early[j], [keep[j], arrived[j], keep[4 + j], arrived[4 + j]]
        )
    for j in range(4):
        buf[1, 4 * j : 4 * j + 4] = four(
            late[j], [buf[0, j], buf[0, 8 + j], buf[0, 4 + j], buf[0, 12 + j]]
        )


def col_kernel(level, keep, arrived, early, late, local, token, keep_out, send_out, buf):
    col_levels(keep, arrived, early, late, buf)
    last, later = level // 2 * LOCAL + LOCAL - 1, side(level + 1)
    for first, out in ((4 - 4 * later, send_out), (4 * later, keep_out)):
        for p in range(4):
            out[2 * p : 2 * p + 2] = mixed(buf, 1, local[last, first + p], first + p)


def col_level(level, keep, arrived, weights, token):
    half = in_vmem(keep.shape)
    return call(
        functools.partial(col_kernel, level),
        f"col_{level}",
        (half, half),
        [VM, VM, VM, VM, VM, ANY],
        (VM, VM),
        [pltpu.VMEM((2, 16, 64, keep.shape[2]), jnp.bfloat16)],
    )(held(keep), held(arrived), *weights, token)


def last_kernel(level, start, columns, *refs):
    keep, arrived, early, late, local = refs[:5]
    out, buf, done, sems = refs[-4:]
    col_levels(keep, arrived, early, late, buf)
    last = level // 2 * LOCAL + LOCAL - 1
    copies = []
    for h in range(8):
        done[2 * h : 2 * h + 2] = mixed(buf, 1, local[last, h], h)
        copy = pltpu.make_async_copy(
            done.at[pl.ds(2 * h, 2)],
            out.at[pl.ds(2 * h, 2), :, pl.ds(start, columns)],
            sems.at[h],
        )
        copy.start()
        copies.append(copy)
    for copy in copies:
        copy.wait()


def last_level(level, keep, arrived, weights, token, result, start, total):
    columns = keep.shape[2]
    operands = [held(keep), held(arrived), *weights]
    in_specs = [VM] * 5
    aliases = {}
    if result is not None:
        operands.append(outside(result))
        in_specs.append(ANY)
        aliases = {5: 0}
    if token is not None:
        operands.append(token)
        in_specs.append(ANY)
    return call(
        functools.partial(last_kernel, level, start, columns),
        f"last_{start}",
        pltpu.HBM((16, 64, total), jnp.bfloat16),
        in_specs,
        ANY,
        [
            pltpu.VMEM((2, 16, 64, columns), jnp.bfloat16),
            pltpu.VMEM((16, 64, columns), jnp.bfloat16),
            pltpu.SemaphoreType.DMA((8,)),
        ],
        aliases,
    )(*operands)


def shards(blocks, order, cross_weights, local_weights):
    blocks, order = blocks[0, 0], order[0, 0]
    cross, local = held(cross_weights[:, 0, 0]), held(local_weights[:, 0, 0])
    total = blocks.shape[2]
    starts = [sum(SIZES[:c]) for c in range(len(SIZES))]
    result = None
    blocks, keep, send = first_take(order, blocks, SIZES[0])
    state = [(keep, swapped(send, "row", 0))]
    for token, send in later_takes(order, blocks, keep, starts[1:], SIZES[1:]):
        state.append((token, swapped(send, "row", 0)))
    pairs = combine(cross, local, token)
    token, stages = pairs[0], [0] * len(SIZES)
    ended = False
    for c in ORDER:
        stages[c] += 1
        stage, level = stages[c], stages[c] - 1
        keep, arrived = state[c]
        weights = (*(held(pair) for pair in pairs[level // 2 * 2 : level // 2 * 2 + 2]), local)
        if level == 2 * SECTIONS - 1:
            result = last_level(
                level, keep, arrived, weights, None if ended else token, result, starts[c], total
            )
            token, ended = outside(result), True
            continue
        ended = False
        if level % 2 == 0:
            keep, send = row_level(level, keep, arrived, cross, token)
        else:
            keep, send = col_level(level, keep, arrived, weights, token)
        state[c] = keep, swapped(send, ("row", "col")[stage % 2], stage // 2)
        token = keep
    return result[None, None]


def solution(mesh):
    placed = (
        P("row", "col", None, None, None),
        P("row", "col", None),
        P(None, "row", "col", None, None, None),
        P(None, "row", "col", None, None, None),
    )
    return jax.shard_map(
        shards,
        mesh=mesh,
        in_specs=placed,
        out_specs=P("row", "col", None, None, None),
        check_vma=False,
    )
```

time: 200 us -> 97.5 us (0.49)
  waiting for transfers between devices: 142 us -> 38.1 us
  matrix products: 31.2 us -> 0 us
  starting transfers between devices: 11.5 us -> 37.7 us
  Pallas kernels: 0 us -> 19.8 us
  other arithmetic: 10.1 us -> 0 us
  local copies, waits for them, and re-layouts: 4.21 us -> 1.42 us
    ppermute x6 -> x24, waiting for transfers between devices: 142 us -> 38.1 us  [swapped(): lax.ppermute(piece, axis, [(i, i ^ 1 << bit) for i in range(lax.axis_size...]
    dot_general x18 -> x0, matrix products: 31.2 us -> none  [pair_products(): jnp.einsum('hij,hjs->his', weight, stacked, preferred_element_type=jnp.fl...]
    ppermute x6 -> x24, starting transfers between devices: 11.5 us -> 37.7 us  [swapped(): lax.ppermute(piece, axis, [(i, i ^ 1 << bit) for i in range(lax.axis_size...]
    pallas_call x0 -> x27, Pallas kernels: none -> 19.8 us  [the longest x8 6.58 us: col_level(): call(functools.partial(col_kernel, level), f'col_{level}', (half, half),...]
    select_n x14 -> x0, other arithmetic: 9.47 us -> none  [the longest x6 4.7 us: via_halves(): sending = jnp.where(upper_side, lower, upper)]
    slice x12 -> x0, local copies, waits for them, and re-layouts: 2.07 us -> none  [local_level(): coeffs[:half_count]]
  transfers between devices with their start and end apart: 6 -> 24, of which waited for: 6 -> 11; matrix products, arithmetic and copies ran while one was open for 0% -> 0% of each run, Pallas kernels for 0% -> 17%
where the time goes in v1:
time: 97.5 us; the launch traced here: 97.4 us
  waiting for transfers between devices  38.1 us (39%)
  starting transfers between devices  37.7 us (39%)
  Pallas kernels  19.8 us (20%)
  local copies, waits for them, and re-layouts  1.42 us (1%)
    ppermute x24, waiting for transfers between devices, swapped(): lax.ppermute(piece, axis, [(i, i ^ 1 << bit) for i in range(lax.axis_size...  38.1 us
    ppermute x24, starting transfers between devices, swapped(): lax.ppermute(piece, axis, [(i, i ^ 1 << bit) for i in range(lax.axis_size...  37.7 us
    pallas_call x8, Pallas kernels, col_level(): call(functools.partial(col_kernel, level), f'col_{level}', (half, half),...  6.58 us
    pallas_call x4, Pallas kernels, last_level(): call(functools.partial(last_kernel, level, start, columns), f'last_{start...  6.01 us
    pallas_call x12, Pallas kernels, row_level(): call(functools.partial(row_kernel, level), f'row_{level}', (half, half),...  3.5 us
  transfers between devices with their start and end apart: 24, of which 11 were waited for; matrix products, arithmetic and copies ran while one was open for 0% of the time, Pallas kernels for 17%

profile of v1, /device:TPU:6, one launch (start us, length us, event | category | flops | bytes accessed | tf_op | source)
XLA Modules:
  0.0 97.4 jit_solution(495955969030531969)
XLA Ops:
  0.0 1.8 %take_first.1 = (bf16[16,64,1024]{2,1,0:T(8,128)(2,1)S(1)}, bf16[8,64,256]{2,1,0:T(8,128)(2,1)S(1)}, bf16[8,64,256]{2,1,0:T(8,128)(2,1)S(1)}) custom-call(s32[1,16]{1,0:T(1,128)} %bitcast.32, bf16[16,64,1024]{2,1,0:T(8,128)(2,1)} %bitcast.31), custom_call_target="tpu_custom_call" | custom-call | flops 1 | bytes 1 | tf_op jit(solution)/shard_map/take_first/pallas_call | solution.py:78
  1.8 1.5 %collective-permute-start.1 = (bf16[8,64,256]{2,1,0:T(8,128)(2,1)S(1)}, bf16[8,64,256]{2,1,0:T(8,128)(2,1)S(1)}, u32[]{:S(2)}, u32[]{:S(2)}) collective-permute-start(bf16[8,64,256]{2,1,0:T(8,128)(2,1)S(1)} %get-tuple-element.64), channel_id=1, source_target_pairs={{0,16},{16,0},{32,48},{48,32},{64,80},{80,64},{96,112},{112,96},{1... | collective-permute-start | bytes 786440 | tf_op jit(solution)/shard_map/ppermute | solution.py:33
  3.3 0.9 take_later.1
  4.2 2.2 %collective-permute-start.3 = (bf16[8,64,256]{2,1,0:T(8,128)(2,1)S(1)}, bf16[8,64,256]{2,1,0:T(8,128)(2,1)S(1)}, u32[]{:S(2)}, u32[]{:S(2)}) collective-permute-start(bf16[8,64,256]{2,1,0:T(8,128)(2,1)S(1)} %get-tuple-element.71), channel_id=1, source_target_pairs={{0,16},{16,0},{32,48},{48,32},{64,80},{80,64},{96,112},{112,96},{1... | collective-permute-start | bytes 786440 | tf_op jit(solution)/shard_map/ppermute | solution.py:33
  6.4 1.4 %copy-done.1 = bf16[6,1,1,8,128,128]{5,4,3,2,1,0:T(8,128)(2,1)S(1)} copy-done((bf16[6,1,1,8,128,128]{5,4,3,2,1,0:T(8,128)(2,1)S(1)}, bf16[6,1,1,8,128,128]{5,4,3,2,1,0:T(8,128)(2,1)}, u32[]{:S(2)}) %copy-start.1) | copy-done | bytes 1572888
  7.8 1.0 %combine.1 = (bf16[4,256,256]{2,1,0:T(8,128)(2,1)S(1)}, bf16[4,256,256]{2,1,0:T(8,128)(2,1)S(1)}, bf16[4,256,256]{2,1,0:T(8,128)(2,1)S(1)}, bf16[4,256,256]{2,1,...) custom-call(bf16[6,8,128,128]{3,2,1,0:T(8,128)(2,1)S(1)} %bitcast.18, ...), custom_call_target="tpu_custom_call" | custom-call | flops 1 | bytes 1 | tf_op jit(solution)/shard_map/combine/pallas_call | solution.py:167
  8.8 3.8 %collective-permute-done.1.arrived = bf16[8,64,256]{2,1,0:T(8,128)(2,1)S(1)} collective-permute-done((bf16[8,64,256]{2,1,0:T(8,128)(2,1)S(1)}, bf16[8,64,256]{2,1,0:T(8,128)(2,1)S(1)}, u32[]{:S(2)}, u32[]{:S(2)}) %collective-permute-start.1) | collective-permute-done | bytes 262176 | tf_op jit(solution)/shard_map/ppermute | solution.py:33
  12.6 0.3 row_0.4
  12.9 0.1 collective-permute-start.2
  13.0 1.5 %collective-permute-start.6 = (bf16[8,64,256]{2,1,0:T(8,128)(2,1)S(1)}, bf16[8,64,256]{2,1,0:T(8,128)(2,1)S(1)}, u32[]{:S(2)}, u32[]{:S(2)}) collective-permute-start(bf16[8,64,256]{2,1,0:T(8,128)(2,1)S(1)} %get-tuple-element.76), channel_id=1, source_target_pairs={{0,16},{16,0},{32,48},{48,32},{64,80},{80,64},{96,112},{112,96},{1... | collective-permute-start | bytes 786440 | tf_op jit(solution)/shard_map/ppermute | solution.py:33
  14.5 2.6 %collective-permute-done.3.arrived = bf16[8,64,256]{2,1,0:T(8,128)(2,1)S(1)} collective-permute-done((bf16[8,64,256]{2,1,0:T(8,128)(2,1)S(1)}, bf16[8,64,256]{2,1,0:T(8,128)(2,1)S(1)}, u32[]{:S(2)}, u32[]{:S(2)}) %collective-permute-start.3) | collective-permute-done | bytes 262176 | tf_op jit(solution)/shard_map/ppermute | solution.py:33
  17.1 0.3 row_0.5
  17.4 0.1 collective-permute-start.5
  17.5 0.8 col_1.4
  18.3 2.0 %collective-permute-start.4 = (bf16[8,64,256]{2,1,0:T(8,128)(2,1)S(1)}, bf16[8,64,256]{2,1,0:T(8,128)(2,1)S(1)}, u32[]{:S(2)}, u32[]{:S(2)}) collective-permute-start(bf16[8,64,256]{2,1,0:T(8,128)(2,1)S(1)} %get-tuple-element.74), channel_id=1, source_target_pairs={{0,32},{16,48},{32,0},{48,16},{64,96},{80,112},{96,64},{112,80},{1... | collective-permute-start | bytes 786440 | tf_op jit(solution)/shard_map/ppermute | solution.py:33
  20.3 1.4 %collective-permute-start = (bf16[8,64,256]{2,1,0:T(8,128)(2,1)S(1)}, bf16[8,64,256]{2,1,0:T(8,128)(2,1)S(1)}, u32[]{:S(2)}, u32[]{:S(2)}) collective-permute-start(bf16[8,64,256]{2,1,0:T(8,128)(2,1)S(1)} %get-tuple-element.63), channel_id=1, source_target_pairs={{0,16},{16,0},{32,48},{48,32},{64,80},{80,64},{96,112},{112,96},{1... | collective-permute-start | bytes 786440 | tf_op jit(solution)/shard_map/ppermute | solution.py:33
  21.7 1.5 %collective-permute-done.6.arrived = bf16[8,64,256]{2,1,0:T(8,128)(2,1)S(1)} collective-permute-done((bf16[8,64,256]{2,1,0:T(8,128)(2,1)S(1)}, bf16[8,64,256]{2,1,0:T(8,128)(2,1)S(1)}, u32[]{:S(2)}, u32[]{:S(2)}) %collective-permute-start.6) | collective-permute-done | bytes 262176 | tf_op jit(solution)/shard_map/ppermute | solution.py:33
  23.2 0.3 row_0.6
  23.5 0.1 collective-permute-start.10
  23.6 0.8 col_1.5
  24.5 2.1 %collective-permute-start.9 = (bf16[8,64,256]{2,1,0:T(8,128)(2,1)S(1)}, bf16[8,64,256]{2,1,0:T(8,128)(2,1)S(1)}, u32[]{:S(2)}, u32[]{:S(2)}) collective-permute-start(bf16[8,64,256]{2,1,0:T(8,128)(2,1)S(1)} %get-tuple-element.85), channel_id=1, source_target_pairs={{0,32},{16,48},{32,0},{48,16},{64,96},{80,112},{96,64},{112,80},{1... | collective-permute-start | bytes 786440 | tf_op jit(solution)/shard_map/ppermute | solution.py:33
  26.6 0.7 collective-permute-done.4.arrived
  27.3 0.3 row_2.4
  27.6 1.7 %collective-permute-start.8 = (bf16[8,64,256]{2,1,0:T(8,128)(2,1)S(1)}, bf16[8,64,256]{2,1,0:T(8,128)(2,1)S(1)}, u32[]{:S(2)}, u32[]{:S(2)}) collective-permute-start(bf16[8,64,256]{2,1,0:T(8,128)(2,1)S(1)} %get-tuple-element.82), channel_id=1, source_target_pairs={{0,2},{1,3},{2,0},{3,1},{4,6},{5,7},{6,4},{7,5},{8,10},{9,11},{10,... | collective-permute-start | bytes 786440 | tf_op jit(solution)/shard_map/ppermute | solution.py:33
  29.2 1.0 %collective-permute-done.arrived = bf16[8,64,256]{2,1,0:T(8,128)(2,1)S(1)} collective-permute-done((bf16[8,64,256]{2,1,0:T(8,128)(2,1)S(1)}, bf16[8,64,256]{2,1,0:T(8,128)(2,1)S(1)}, u32[]{:S(2)}, u32[]{:S(2)}) %collective-permute-start) | collective-permute-done | bytes 262176 | tf_op jit(solution)/shard_map/ppermute | solution.py:33
  30.2 0.3 row_0.7
  30.5 0.1 collective-permute-start.7
  30.6 0.8 col_1.6
  31.5 0.8 collective-permute-start.14
  32.3 1.2 %collective-permute-done.9.arrived = bf16[8,64,256]{2,1,0:T(8,128)(2,1)S(1)} collective-permute-done((bf16[8,64,256]{2,1,0:T(8,128)(2,1)S(1)}, bf16[8,64,256]{2,1,0:T(8,128)(2,1)S(1)}, u32[]{:S(2)}, u32[]{:S(2)}) %collective-permute-start.9) | collective-permute-done | bytes 262176 | tf_op jit(solution)/shard_map/ppermute | solution.py:33
  33.5 0.3 row_2.5
  33.8 1.8 %collective-permute-start.13 = (bf16[8,64,256]{2,1,0:T(8,128)(2,1)S(1)}, bf16[8,64,256]{2,1,0:T(8,128)(2,1)S(1)}, u32[]{:S(2)}, u32[]{:S(2)}) collective-permute-start(bf16[8,64,256]{2,1,0:T(8,128)(2,1)S(1)} %get-tuple-element.93), channel_id=1, source_target_pairs={{0,2},{1,3},{2,0},{3,1},{4,6},{5,7},{6,4},{7,5},{8,10},{9,11},{10,... | collective-permute-start | bytes 786440 | tf_op jit(solution)/shard_map/ppermute | solution.py:33
  35.6 0.0 collective-permute-done.8.arrived
  35.7 0.8 col_3.4
  36.5 3.3 %collective-permute-start.12 = (bf16[8,64,256]{2,1,0:T(8,128)(2,1)S(1)}, bf16[8,64,256]{2,1,0:T(8,128)(2,1)S(1)}, u32[]{:S(2)}, u32[]{:S(2)}) collective-permute-start(bf16[8,64,256]{2,1,0:T(8,128)(2,1)S(1)} %get-tuple-element.92), channel_id=1, source_target_pairs={{0,64},{16,80},{32,96},{48,112},{64,0},{80,16},{96,32},{112,48},{1... | collective-permute-start | bytes 786440 | tf_op jit(solution)/shard_map/ppermute | solution.py:33
  39.8 0.8 col_1.7
  40.7 1.9 %collective-permute-start.11 = (bf16[8,64,256]{2,1,0:T(8,128)(2,1)S(1)}, bf16[8,64,256]{2,1,0:T(8,128)(2,1)S(1)}, u32[]{:S(2)}, u32[]{:S(2)}) collective-permute-start(bf16[8,64,256]{2,1,0:T(8,128)(2,1)S(1)} %get-tuple-element.91), channel_id=1, source_target_pairs={{0,32},{16,48},{32,0},{48,16},{64,96},{80,112},{96,64},{112,80},{1... | collective-permute-start | bytes 786440 | tf_op jit(solution)/shard_map/ppermute | solution.py:33
  42.5 0.3 row_2.6
  42.8 3.2 %collective-permute-start.17 = (bf16[8,64,256]{2,1,0:T(8,128)(2,1)S(1)}, bf16[8,64,256]{2,1,0:T(8,128)(2,1)S(1)}, u32[]{:S(2)}, u32[]{:S(2)}) collective-permute-start(bf16[8,64,256]{2,1,0:T(8,128)(2,1)S(1)} %get-tuple-element.101), channel_id=1, source_target_pairs={{0,2},{1,3},{2,0},{3,1},{4,6},{5,7},{6,4},{7,5},{8,10},{9,11},{10,... | collective-permute-start | bytes 786440 | tf_op jit(solution)/shard_map/ppermute | solution.py:33
  46.0 0.8 col_3.5
  46.9 0.1 collective-permute-start.16
  47.0 5.7 %collective-permute-done.12.arrived = bf16[8,64,256]{2,1,0:T(8,128)(2,1)S(1)} collective-permute-done((bf16[8,64,256]{2,1,0:T(8,128)(2,1)S(1)}, bf16[8,64,256]{2,1,0:T(8,128)(2,1)S(1)}, u32[]{:S(2)}, u32[]{:S(2)}) %collective-permute-start.12) | collective-permute-done | bytes 262176 | tf_op jit(solution)/shard_map/ppermute | solution.py:33
  52.7 0.3 row_4.4
  53.0 0.3 row_2.7
  53.3 3.6 %collective-permute-start.15 = (bf16[8,64,256]{2,1,0:T(8,128)(2,1)S(1)}, bf16[8,64,256]{2,1,0:T(8,128)(2,1)S(1)}, u32[]{:S(2)}, u32[]{:S(2)}) collective-permute-start(bf16[8,64,256]{2,1,0:T(8,128)(2,1)S(1)} %get-tuple-element.99), channel_id=1, source_target_pairs={{0,2},{1,3},{2,0},{3,1},{4,6},{5,7},{6,4},{7,5},{8,10},{9,11},{10,... | collective-permute-start | bytes 786440 | tf_op jit(solution)/shard_map/ppermute | solution.py:33
  56.9 0.8 col_3.6
  57.7 0.4 collective-permute-start.21
  58.1 11.4 %collective-permute-done.16.arrived = bf16[8,64,256]{2,1,0:T(8,128)(2,1)S(1)} collective-permute-done((bf16[8,64,256]{2,1,0:T(8,128)(2,1)S(1)}, bf16[8,64,256]{2,1,0:T(8,128)(2,1)S(1)}, u32[]{:S(2)}, u32[]{:S(2)}) %collective-permute-start.16) | collective-permute-done | bytes 262176 | tf_op jit(solution)/shard_map/ppermute | solution.py:33
  69.5 0.3 row_4.5
  69.8 3.4 %collective-permute-start.20 = (bf16[8,64,256]{2,1,0:T(8,128)(2,1)S(1)}, bf16[8,64,256]{2,1,0:T(8,128)(2,1)S(1)}, u32[]{:S(2)}, u32[]{:S(2)}) collective-permute-start(bf16[8,64,256]{2,1,0:T(8,128)(2,1)S(1)} %get-tuple-element.109), channel_id=1, source_target_pairs={{0,4},{1,5},{2,6},{3,7},{4,0},{5,1},{6,2},{7,3},{8,12},{9,13},{10,... | collective-permute-start | bytes 786440 | tf_op jit(solution)/shard_map/ppermute | solution.py:33
  73.1 0.2 collective-permute-start.19
  73.4 0.8 col_3.7
  74.2 0.1 collective-permute-start.18
  74.3 0.3 row_4.6
  74.6 3.4 %collective-permute-start.23 = (bf16[8,64,256]{2,1,0:T(8,128)(2,1)S(1)}, bf16[8,64,256]{2,1,0:T(8,128)(2,1)S(1)}, u32[]{:S(2)}, u32[]{:S(2)}) collective-permute-start(bf16[8,64,256]{2,1,0:T(8,128)(2,1)S(1)} %get-tuple-element.114), channel_id=1, source_target_pairs={{0,4},{1,5},{2,6},{3,7},{4,0},{5,1},{6,2},{7,3},{8,12},{9,13},{10,... | collective-permute-start | bytes 786440 | tf_op jit(solution)/shard_map/ppermute | solution.py:33
  78.0 2.6 %collective-permute-done.20.refs_1_ = bf16[8,64,256]{2,1,0:T(8,128)(2,1)S(1)} collective-permute-done((bf16[8,64,256]{2,1,0:T(8,128)(2,1)S(1)}, bf16[8,64,256]{2,1,0:T(8,128)(2,1)S(1)}, u32[]{:S(2)}, u32[]{:S(2)}) %collective-permute-start.20) | collective-permute-done | bytes 262176 | tf_op jit(solution)/shard_map/ppermute | solution.py:33
  80.6 1.5 %last_256.1.refs_5_ = bf16[16,64,1024]{2,1,0:T(8,128)(2,1)} custom-call(bf16[8,64,256]{2,1,0:T(8,128)(2,1)S(1)} %get-tuple-element.103.token.refs_0_, bf16[8,64,256]{2,1,0:T(8,128)(2,1)S(1)} %collective-permute-done.20.refs_1_, bf16[4,256,256]{2,1,0:T(8,128)(2,1)S(1)} %get-tuple-element.107.refs_2_, bf16[4,256,256]{2,1,0:T(8,128)(2,1)S(1)} %get-tuple-element.108.refs_3_, ...), custom_call_target="tpu_custom_call" | custom-call | flops 1 | bytes 1 | tf_op jit(solution)/shard_map/last_256/pallas_call | solution.py:250
  82.1 3.8 %collective-permute-done.19.refs_1_ = bf16[8,64,256]{2,1,0:T(8,128)(2,1)S(1)} collective-permute-done((bf16[8,64,256]{2,1,0:T(8,128)(2,1)S(1)}, bf16[8,64,256]{2,1,0:T(8,128)(2,1)S(1)}, u32[]{:S(2)}, u32[]{:S(2)}) %collective-permute-start.19) | collective-permute-done | bytes 262176 | tf_op jit(solution)/shard_map/ppermute | solution.py:33
  85.9 1.5 %last_0.1.token.refs_5_ = bf16[16,64,1024]{2,1,0:T(8,128)(2,1)} custom-call(bf16[8,64,256]{2,1,0:T(8,128)(2,1)S(1)} %get-tuple-element.97.token.refs_0_, bf16[8,64,256]{2,1,0:T(8,128)(2,1)S(1)} %collective-permute-done.19.refs_1_, bf16[4,256,256]{2,1,0:T(8,128)(2,1)S(1)} %get-tuple-element.107.refs_2_, ...), custom_call_target="tpu_custom_call", output_to_operand_aliasing={{}: (5, {})} | custom-call | flops 1 | bytes 1 | tf_op jit(solution)/shard_map/last_0/pallas_call | solution.py:250
  87.4 0.3 row_4.7
  87.8 2.8 %collective-permute-start.22 = (bf16[8,64,256]{2,1,0:T(8,128)(2,1)S(1)}, bf16[8,64,256]{2,1,0:T(8,128)(2,1)S(1)}, u32[]{:S(2)}, u32[]{:S(2)}) collective-permute-start(bf16[8,64,256]{2,1,0:T(8,128)(2,1)S(1)} %get-tuple-element.113), channel_id=1, source_target_pairs={{0,4},{1,5},{2,6},{3,7},{4,0},{5,1},{6,2},{7,3},{8,12},{9,13},{10,... | collective-permute-start | bytes 786440 | tf_op jit(solution)/shard_map/ppermute | solution.py:33
  90.5 1.5 %last_768.1.refs_5_ = bf16[16,64,1024]{2,1,0:T(8,128)(2,1)} custom-call(bf16[8,64,256]{2,1,0:T(8,128)(2,1)S(1)} %get-tuple-element.111.refs_5_.refs_0_, bf16[8,64,256]{2,1,0:T(8,128)(2,1)S(1)} %collective-permute-done.23.refs_1_, bf16[4,256,256]{2,1,0:T(8,128)(2,1)S(1)} %get-tuple-element.107.refs_2_, ...), custom_call_target="tpu_custom_call", output_to_operand_aliasing={{}: (5, {})} | custom-call | flops 1 | bytes 1 | tf_op jit(solution)/shard_map/last_768/pallas_call | solution.py:250
  92.0 3.7 %collective-permute-done.22.refs_1_ = bf16[8,64,256]{2,1,0:T(8,128)(2,1)S(1)} collective-permute-done((bf16[8,64,256]{2,1,0:T(8,128)(2,1)S(1)}, bf16[8,64,256]{2,1,0:T(8,128)(2,1)S(1)}, u32[]{:S(2)}, u32[]{:S(2)}) %collective-permute-start.22) | collective-permute-done | bytes 262176 | tf_op jit(solution)/shard_map/ppermute | solution.py:33
  95.7 1.5 %last_512.1 = bf16[16,64,1024]{2,1,0:T(8,128)(2,1)} custom-call(bf16[8,64,256]{2,1,0:T(8,128)(2,1)S(1)} %get-tuple-element.112.refs_6_.refs_0_, bf16[8,64,256]{2,1,0:T(8,128)(2,1)S(1)} %collective-permute-done.22.refs_1_, bf16[4,256,256]{2,1,0:T(8,128)(2,1)S(1)} %get-tuple-element.107.refs_2_, ...), custom_call_target="tpu_custom_call", output_to_operand_aliasing={{}: (5, {})} | custom-call | flops 1 | bytes 1 | tf_op jit(solution)/shard_map/last_512/pallas_call | solution.py:250
  (17 shorter events, 0.0 us)
Async XLA Ops:
  0.0 6.4 %copy-start = (bf16[12,1,1,8,128,128]{5,4,3,2,1,0:T(8,128)(2,1)S(1)}, bf16[12,1,1,8,128,128]{5,4,3,2,1,0:T(8,128)(2,1)}, u32[]{:S(2)}) copy-start(bf16[12,1,1,8,128,128]{5,4,3,2,1,0:T(8,128)(2,1)} %param.7) | copy-start | bytes 9437188
  1.8 10.8 %collective-permute-start.1 = (bf16[8,64,256]{2,1,0:T(8,128)(2,1)S(1)}, bf16[8,64,256]{2,1,0:T(8,128)(2,1)S(1)}, u32[]{:S(2)}, u32[]{:S(2)}) collective-permute-start(bf16[8,64,256]{2,1,0:T(8,128)(2,1)S(1)} %get-tuple-element.64), channel_id=1, source_target_pairs={{0,16},{16,0},{32,48},{48,32},{64,80},{80,64},{96,112},{112,96},{1... | collective-permute-start | bytes 786440 | tf_op jit(solution)/shard_map/ppermute | solution.py:33
  4.2 12.9 %collective-permute-start.3 = (bf16[8,64,256]{2,1,0:T(8,128)(2,1)S(1)}, bf16[8,64,256]{2,1,0:T(8,128)(2,1)S(1)}, u32[]{:S(2)}, u32[]{:S(2)}) collective-permute-start(bf16[8,64,256]{2,1,0:T(8,128)(2,1)S(1)} %get-tuple-element.71), channel_id=1, source_target_pairs={{0,16},{16,0},{32,48},{48,32},{64,80},{80,64},{96,112},{112,96},{1... | collective-permute-start | bytes 786440 | tf_op jit(solution)/shard_map/ppermute | solution.py:33
  6.4 1.4 %copy-start.1 = (bf16[6,1,1,8,128,128]{5,4,3,2,1,0:T(8,128)(2,1)S(1)}, bf16[6,1,1,8,128,128]{5,4,3,2,1,0:T(8,128)(2,1)}, u32[]{:S(2)}) copy-start(bf16[6,1,1,8,128,128]{5,4,3,2,1,0:T(8,128)(2,1)} %param.6) | copy-start | bytes 4718596
  12.9 4.6 %collective-permute-start.2 = (bf16[8,64,256]{2,1,0:T(8,128)(2,1)S(1)}, bf16[8,64,256]{2,1,0:T(8,128)(2,1)S(1)}, u32[]{:S(2)}, u32[]{:S(2)}) collective-permute-start(bf16[8,64,256]{2,1,0:T(8,128)(2,1)S(1)} %get-tuple-element.68), channel_id=1, source_target_pairs={{0,1},{1,0},{2,3},{3,2},{4,5},{5,4},{6,7},{7,6},{8,9},{9,8},{10,11... | collective-permute-start | bytes 786440 | tf_op jit(solution)/shard_map/ppermute | solution.py:33
  13.0 10.2 %collective-permute-start.6 = (bf16[8,64,256]{2,1,0:T(8,128)(2,1)S(1)}, bf16[8,64,256]{2,1,0:T(8,128)(2,1)S(1)}, u32[]{:S(2)}, u32[]{:S(2)}) collective-permute-start(bf16[8,64,256]{2,1,0:T(8,128)(2,1)S(1)} %get-tuple-element.76), channel_id=1, source_target_pairs={{0,16},{16,0},{32,48},{48,32},{64,80},{80,64},{96,112},{112,96},{1... | collective-permute-start | bytes 786440 | tf_op jit(solution)/shard_map/ppermute | solution.py:33
  17.4 6.3 %collective-permute-start.5 = (bf16[8,64,256]{2,1,0:T(8,128)(2,1)S(1)}, bf16[8,64,256]{2,1,0:T(8,128)(2,1)S(1)}, u32[]{:S(2)}, u32[]{:S(2)}) collective-permute-start(bf16[8,64,256]{2,1,0:T(8,128)(2,1)S(1)} %get-tuple-element.75), channel_id=1, source_target_pairs={{0,1},{1,0},{2,3},{3,2},{4,5},{5,4},{6,7},{7,6},{8,9},{9,8},{10,11... | collective-permute-start | bytes 786440 | tf_op jit(solution)/shard_map/ppermute | solution.py:33
  18.3 9.0 %collective-permute-start.4 = (bf16[8,64,256]{2,1,0:T(8,128)(2,1)S(1)}, bf16[8,64,256]{2,1,0:T(8,128)(2,1)S(1)}, u32[]{:S(2)}, u32[]{:S(2)}) collective-permute-start(bf16[8,64,256]{2,1,0:T(8,128)(2,1)S(1)} %get-tuple-element.74), channel_id=1, source_target_pairs={{0,32},{16,48},{32,0},{48,16},{64,96},{80,112},{96,64},{112,80},{1... | collective-permute-start | bytes 786440 | tf_op jit(solution)/shard_map/ppermute | solution.py:33
  20.3 9.9 %collective-permute-start = (bf16[8,64,256]{2,1,0:T(8,128)(2,1)S(1)}, bf16[8,64,256]{2,1,0:T(8,128)(2,1)S(1)}, u32[]{:S(2)}, u32[]{:S(2)}) collective-permute-start(bf16[8,64,256]{2,1,0:T(8,128)(2,1)S(1)} %get-tuple-element.63), channel_id=1, source_target_pairs={{0,16},{16,0},{32,48},{48,32},{64,80},{80,64},{96,112},{112,96},{1... | collective-permute-start | bytes 786440 | tf_op jit(solution)/shard_map/ppermute | solution.py:33
  23.5 7.1 %collective-permute-start.10 = (bf16[8,64,256]{2,1,0:T(8,128)(2,1)S(1)}, bf16[8,64,256]{2,1,0:T(8,128)(2,1)S(1)}, u32[]{:S(2)}, u32[]{:S(2)}) collective-permute-start(bf16[8,64,256]{2,1,0:T(8,128)(2,1)S(1)} %get-tuple-element.86), channel_id=1, source_target_pairs={{0,1},{1,0},{2,3},{3,2},{4,5},{5,4},{6,7},{7,6},{8,9},{9,8},{10,11... | collective-permute-start | bytes 786440 | tf_op jit(solution)/shard_map/ppermute | solution.py:33
  23.6 3.6 %copy-start.2 = (bf16[6,1,1,8,128,128]{5,4,3,2,1,0:T(8,128)(2,1)S(1)}, bf16[6,1,1,8,128,128]{5,4,3,2,1,0:T(8,128)(2,1)}, u32[]{:S(2)}) copy-start(bf16[6,1,1,8,128,128]{5,4,3,2,1,0:T(8,128)(2,1)} %param.6) | copy-start | bytes 4718596
  24.5 9.0 %collective-permute-start.9 = (bf16[8,64,256]{2,1,0:T(8,128)(2,1)S(1)}, bf16[8,64,256]{2,1,0:T(8,128)(2,1)S(1)}, u32[]{:S(2)}, u32[]{:S(2)}) collective-permute-start(bf16[8,64,256]{2,1,0:T(8,128)(2,1)S(1)} %get-tuple-element.85), channel_id=1, source_target_pairs={{0,32},{16,48},{32,0},{48,16},{64,96},{80,112},{96,64},{112,80},{1... | collective-permute-start | bytes 786440 | tf_op jit(solution)/shard_map/ppermute | solution.py:33
  27.6 8.1 %collective-permute-start.8 = (bf16[8,64,256]{2,1,0:T(8,128)(2,1)S(1)}, bf16[8,64,256]{2,1,0:T(8,128)(2,1)S(1)}, u32[]{:S(2)}, u32[]{:S(2)}) collective-permute-start(bf16[8,64,256]{2,1,0:T(8,128)(2,1)S(1)} %get-tuple-element.82), channel_id=1, source_target_pairs={{0,2},{1,3},{2,0},{3,1},{4,6},{5,7},{6,4},{7,5},{8,10},{9,11},{10,... | collective-permute-start | bytes 786440 | tf_op jit(solution)/shard_map/ppermute | solution.py:33
  30.5 9.3 %collective-permute-start.7 = (bf16[8,64,256]{2,1,0:T(8,128)(2,1)S(1)}, bf16[8,64,256]{2,1,0:T(8,128)(2,1)S(1)}, u32[]{:S(2)}, u32[]{:S(2)}) collective-permute-start(bf16[8,64,256]{2,1,0:T(8,128)(2,1)S(1)} %get-tuple-element.81), channel_id=1, source_target_pairs={{0,1},{1,0},{2,3},{3,2},{4,5},{5,4},{6,7},{7,6},{8,9},{9,8},{10,11... | collective-permute-start | bytes 786440 | tf_op jit(solution)/shard_map/ppermute | solution.py:33
  31.5 11.1 %collective-permute-start.14 = (bf16[8,64,256]{2,1,0:T(8,128)(2,1)S(1)}, bf16[8,64,256]{2,1,0:T(8,128)(2,1)S(1)}, u32[]{:S(2)}, u32[]{:S(2)}) collective-permute-start(bf16[8,64,256]{2,1,0:T(8,128)(2,1)S(1)} %get-tuple-element.94), channel_id=1, source_target_pairs={{0,32},{16,48},{32,0},{48,16},{64,96},{80,112},{96,64},{112,80},{1... | collective-permute-start | bytes 786440 | tf_op jit(solution)/shard_map/ppermute | solution.py:33
  33.8 12.2 %collective-permute-start.13 = (bf16[8,64,256]{2,1,0:T(8,128)(2,1)S(1)}, bf16[8,64,256]{2,1,0:T(8,128)(2,1)S(1)}, u32[]{:S(2)}, u32[]{:S(2)}) collective-permute-start(bf16[8,64,256]{2,1,0:T(8,128)(2,1)S(1)} %get-tuple-element.93), channel_id=1, source_target_pairs={{0,2},{1,3},{2,0},{3,1},{4,6},{5,7},{6,4},{7,5},{8,10},{9,11},{10,... | collective-permute-start | bytes 786440 | tf_op jit(solution)/shard_map/ppermute | solution.py:33
  36.5 16.2 %collective-permute-start.12 = (bf16[8,64,256]{2,1,0:T(8,128)(2,1)S(1)}, bf16[8,64,256]{2,1,0:T(8,128)(2,1)S(1)}, u32[]{:S(2)}, u32[]{:S(2)}) collective-permute-start(bf16[8,64,256]{2,1,0:T(8,128)(2,1)S(1)} %get-tuple-element.92), channel_id=1, source_target_pairs={{0,64},{16,80},{32,96},{48,112},{64,0},{80,16},{96,32},{112,48},{1... | collective-permute-start | bytes 786440 | tf_op jit(solution)/shard_map/ppermute | solution.py:33
  40.7 12.3 %collective-permute-start.11 = (bf16[8,64,256]{2,1,0:T(8,128)(2,1)S(1)}, bf16[8,64,256]{2,1,0:T(8,128)(2,1)S(1)}, u32[]{:S(2)}, u32[]{:S(2)}) collective-permute-start(bf16[8,64,256]{2,1,0:T(8,128)(2,1)S(1)} %get-tuple-element.91), channel_id=1, source_target_pairs={{0,32},{16,48},{32,0},{48,16},{64,96},{80,112},{96,64},{112,80},{1... | collective-permute-start | bytes 786440 | tf_op jit(solution)/shard_map/ppermute | solution.py:33
  42.8 14.1 %collective-permute-start.17 = (bf16[8,64,256]{2,1,0:T(8,128)(2,1)S(1)}, bf16[8,64,256]{2,1,0:T(8,128)(2,1)S(1)}, u32[]{:S(2)}, u32[]{:S(2)}) collective-permute-start(bf16[8,64,256]{2,1,0:T(8,128)(2,1)S(1)} %get-tuple-element.101), channel_id=1, source_target_pairs={{0,2},{1,3},{2,0},{3,1},{4,6},{5,7},{6,4},{7,5},{8,10},{9,11},{10,... | collective-permute-start | bytes 786440 | tf_op jit(solution)/shard_map/ppermute | solution.py:33
  46.9 22.6 %collective-permute-start.16 = (bf16[8,64,256]{2,1,0:T(8,128)(2,1)S(1)}, bf16[8,64,256]{2,1,0:T(8,128)(2,1)S(1)}, u32[]{:S(2)}, u32[]{:S(2)}) collective-permute-start(bf16[8,64,256]{2,1,0:T(8,128)(2,1)S(1)} %get-tuple-element.100), channel_id=1, source_target_pairs={{0,64},{16,80},{32,96},{48,112},{64,0},{80,16},{96,32},{112,48},{1... | collective-permute-start | bytes 786440 | tf_op jit(solution)/shard_map/ppermute | solution.py:33
  53.3 20.1 %collective-permute-start.15 = (bf16[8,64,256]{2,1,0:T(8,128)(2,1)S(1)}, bf16[8,64,256]{2,1,0:T(8,128)(2,1)S(1)}, u32[]{:S(2)}, u32[]{:S(2)}) collective-permute-start(bf16[8,64,256]{2,1,0:T(8,128)(2,1)S(1)} %get-tuple-element.99), channel_id=1, source_target_pairs={{0,2},{1,3},{2,0},{3,1},{4,6},{5,7},{6,4},{7,5},{8,10},{9,11},{10,... | collective-permute-start | bytes 786440 | tf_op jit(solution)/shard_map/ppermute | solution.py:33
  57.7 16.6 %collective-permute-start.21 = (bf16[8,64,256]{2,1,0:T(8,128)(2,1)S(1)}, bf16[8,64,256]{2,1,0:T(8,128)(2,1)S(1)}, u32[]{:S(2)}, u32[]{:S(2)}) collective-permute-start(bf16[8,64,256]{2,1,0:T(8,128)(2,1)S(1)} %get-tuple-element.110), channel_id=1, source_target_pairs={{0,64},{16,80},{32,96},{48,112},{64,0},{80,16},{96,32},{112,48},{1... | collective-permute-start | bytes 786440 | tf_op jit(solution)/shard_map/ppermute | solution.py:33
  69.8 10.8 %collective-permute-start.20 = (bf16[8,64,256]{2,1,0:T(8,128)(2,1)S(1)}, bf16[8,64,256]{2,1,0:T(8,128)(2,1)S(1)}, u32[]{:S(2)}, u32[]{:S(2)}) collective-permute-start(bf16[8,64,256]{2,1,0:T(8,128)(2,1)S(1)} %get-tuple-element.109), channel_id=1, source_target_pairs={{0,4},{1,5},{2,6},{3,7},{4,0},{5,1},{6,2},{7,3},{8,12},{9,13},{10,... | collective-permute-start | bytes 786440 | tf_op jit(solution)/shard_map/ppermute | solution.py:33
  73.1 12.8 %collective-permute-start.19 = (bf16[8,64,256]{2,1,0:T(8,128)(2,1)S(1)}, bf16[8,64,256]{2,1,0:T(8,128)(2,1)S(1)}, u32[]{:S(2)}, u32[]{:S(2)}) collective-permute-start(bf16[8,64,256]{2,1,0:T(8,128)(2,1)S(1)} %get-tuple-element.106), channel_id=1, source_target_pairs={{0,4},{1,5},{2,6},{3,7},{4,0},{5,1},{6,2},{7,3},{8,12},{9,13},{10,... | collective-permute-start | bytes 786440 | tf_op jit(solution)/shard_map/ppermute | solution.py:33
  74.2 13.2 %collective-permute-start.18 = (bf16[8,64,256]{2,1,0:T(8,128)(2,1)S(1)}, bf16[8,64,256]{2,1,0:T(8,128)(2,1)S(1)}, u32[]{:S(2)}, u32[]{:S(2)}) collective-permute-start(bf16[8,64,256]{2,1,0:T(8,128)(2,1)S(1)} %get-tuple-element.105), channel_id=1, source_target_pairs={{0,64},{16,80},{32,96},{48,112},{64,0},{80,16},{96,32},{112,48},{1... | collective-permute-start | bytes 786440 | tf_op jit(solution)/shard_map/ppermute | solution.py:33
  74.6 15.9 %collective-permute-start.23 = (bf16[8,64,256]{2,1,0:T(8,128)(2,1)S(1)}, bf16[8,64,256]{2,1,0:T(8,128)(2,1)S(1)}, u32[]{:S(2)}, u32[]{:S(2)}) collective-permute-start(bf16[8,64,256]{2,1,0:T(8,128)(2,1)S(1)} %get-tuple-element.114), channel_id=1, source_target_pairs={{0,4},{1,5},{2,6},{3,7},{4,0},{5,1},{6,2},{7,3},{8,12},{9,13},{10,... | collective-permute-start | bytes 786440 | tf_op jit(solution)/shard_map/ppermute | solution.py:33
  87.8 8.0 %collective-permute-start.22 = (bf16[8,64,256]{2,1,0:T(8,128)(2,1)S(1)}, bf16[8,64,256]{2,1,0:T(8,128)(2,1)S(1)}, u32[]{:S(2)}, u32[]{:S(2)}) collective-permute-start(bf16[8,64,256]{2,1,0:T(8,128)(2,1)S(1)} %get-tuple-element.113), channel_id=1, source_target_pairs={{0,4},{1,5},{2,6},{3,7},{4,0},{5,1},{6,2},{7,3},{8,12},{9,13},{10,... | collective-permute-start | bytes 786440 | tf_op jit(solution)/shard_map/ppermute | solution.py:33

commit v2 on v0

v2 whole, which is shorter than its diff:
```python
import jax
import jax.numpy as jnp
from jax import lax
from jax.experimental import pallas as pl
from jax.experimental.pallas import tpu as pltpu
from jax.sharding import PartitionSpec as P

SECTIONS = 3
LOCAL = 4
SIZES = (256, 256, 256, 256)
FLOWS = ("rrc", "rcc", "rcr", "rpp")
LATER, COMBINE = -1, -2
ORDER = (0, LATER, 3, COMBINE, 1, 2, 0, 1, 0, 2, 1, 3, 2, 1, 0, 2, 1, 2, 0, 1, 3, 2, 0, 3)
LIMIT = 10 * 2**20

VM = pl.BlockSpec(memory_space=pltpu.VMEM)
ANY = pl.BlockSpec(memory_space=pl.ANY)


def in_vmem(*shape):
    return pltpu.VMEM(shape, jnp.bfloat16)


def held(x):
    return pltpu.with_memory_space_constraint(x, pltpu.VMEM)


def outside(x):
    return pltpu.with_memory_space_constraint(x, pltpu.HBM)


def row_side(section):
    return lax.axis_index("row") >> section & 1


def col_side(section):
    return lax.axis_index("col") >> section & 1


def swapped(piece, axis, section):
    size = lax.axis_size(axis)
    return lax.ppermute(piece, axis, [(i, i ^ 1 << section) for i in range(size)])


def swapped_both(piece, section):
    rows, cols, bit = lax.axis_size("row"), lax.axis_size("col"), 1 << section
    pairs = [(i * cols + j, (i ^ bit) * cols + (j ^ bit)) for i in range(rows) for j in range(cols)]
    return lax.ppermute(piece, ("row", "col"), pairs)


def call(kernel, name, out_shape, operands, token, out_specs=None, scratch=(), result=None):
    operands, specs = list(operands), [ANY if memory == "any" else VM for _, memory in operands]
    operands = [outside(x) if memory == "any" else held(x) for x, memory in operands]
    aliases = {}
    if result is not None:
        aliases = {len(operands): 0}
        operands.append(outside(result))
        specs.append(ANY)
    if token is not None:
        operands.append(token)
        specs.append(ANY)
    extra = len(operands)

    def body(*refs):
        kernel(refs[:extra], refs[extra : extra + len(out_shape)], refs[extra + len(out_shape) :])

    return pl.pallas_call(
        body,
        out_shape=tuple(out_shape),
        in_specs=specs,
        out_specs=(VM,) * len(out_shape) if out_specs is None else out_specs,
        scratch_shapes=list(scratch),
        input_output_aliases=aliases,
        compiler_params=pltpu.CompilerParams(vmem_limit_bytes=LIMIT),
        cost_estimate=pl.CostEstimate(flops=1, bytes_accessed=1, transcendentals=0),
        name=name,
    )(*operands)


def vmem(*arrays):
    return [(x, "vmem") for x in arrays]


def pieces(flow, section):
    row, col = row_side(section), col_side(section)
    if flow == "c":
        return [[(8 * row, 8)], [(8 - 8 * row, 8)]]
    own, by_col, by_row, by_both = [(8 * r + 4 * c, 4) for r in (row, 1 - row) for c in (col, 1 - col)]
    if flow == "p":
        return [[own], [by_row], [by_col], [by_both]]
    return [[own], [by_row], [by_col, by_both]]


COUNTS = {"c": (8, 8), "p": (4, 4, 4, 4), "r": (4, 4, 8)}


def shapes(flow, columns):
    return [in_vmem(count, 64, columns) for count in COUNTS[flow]]


def sent(flow, section, outs):
    if flow == "c":
        return outs[0], swapped(outs[1], "row", section)
    if flow == "p":
        return (
            outs[0],
            swapped(outs[1], "row", section),
            swapped(outs[2], "col", section),
            swapped_both(outs[3], section),
        )
    return outs[0], outs[1], swapped(outs[2], "col", section)


def picked(source, order, start, columns, outs):
    for ranges, out in zip(pieces("r", 0), outs):
        at = 0
        for first, count in ranges:
            for j in range(count):
                out[at] = source[order[0, first + j], :, start : start + columns]
                at += 1


def first_take(order, blocks, columns):
    def kernel(ins, outs, scratch):
        (order_any, source), (order_held, sems) = ins, scratch
        index = pltpu.make_async_copy(order_any, order_held, sems.at[0])
        whole = pltpu.make_async_copy(source, outs[0], sems.at[1])
        whole.start()
        index.start()
        index.wait()
        whole.wait()
        picked(outs[0], order_held, 0, columns, outs[1:])

    return call(
        kernel,
        "take_first",
        [in_vmem(*blocks.shape), *shapes("r", columns)],
        [(order, "any"), (blocks, "any")],
        None,
        scratch=[pltpu.SMEM((1, 16), jnp.int32), pltpu.SemaphoreType.DMA((2,))],
    )


def later_takes(order, blocks, cross, starts, sizes, token):
    total = sum(sizes)

    def kernel(ins, outs, scratch):
        (order_any, source, weights, _), (order_held, sem) = ins, scratch
        index = pltpu.make_async_copy(order_any, order_held, sem)
        index.start()
        for section in range(SECTIONS):
            for p in range(4):
                outs[section][p] = weights[2 * section, 4 - 4 * col_side(section) + p]
        index.wait()
        together = outs[SECTIONS]
        for c, (start, columns) in enumerate(zip(starts, sizes)):
            at = start - starts[0]
            own, by_row = outs[SECTIONS + 1 + 2 * c : SECTIONS + 3 + 2 * c]
            part = together.at[:, :, at : at + columns]
            picked(source, order_held, start, columns, (own, by_row, part))

    outs = call(
        kernel,
        "take_later",
        [in_vmem(4, 128, 128)] * SECTIONS
        + [in_vmem(8, 64, total)]
        + [in_vmem(4, 64, n) for n in sizes for _ in range(2)],
        [(order, "any"), *vmem(blocks, cross)],
        token,
        scratch=[pltpu.SMEM((1, 16), jnp.int32), pltpu.SemaphoreType.DMA],
    )
    return outs[:SECTIONS], outs[SECTIONS], list(zip(outs[SECTIONS + 1 :: 2], outs[SECTIONS + 2 :: 2]))


def combined(first, second, upper, out):
    for j in range(4):
        halves = []
        for g in (j, 4 + j):
            weight = first[g]
            if upper is not None:
                turned = jnp.concatenate([weight[:, 64:], weight[:, :64]], axis=1)
                weight = jnp.where(upper == 1, turned, weight)
            halves.append(weight)
        for t in range(2):
            for i in range(2):
                out[j, 128 * t : 128 * t + 128, 128 * i : 128 * i + 128] = jnp.dot(
                    second[2 * j + t][:, 64 * i : 64 * i + 64],
                    halves[i][64 * t : 64 * t + 64],
                    preferred_element_type=jnp.float32,
                ).astype(jnp.bfloat16)


def combine(cross, local, token):
    def kernel(ins, outs, scratch):
        cross, local = ins[:2]
        for section in range(SECTIONS):
            level, k = 2 * section + 1, section * LOCAL
            combined(cross.at[level], local.at[k], col_side(section), outs[2 * section])
            combined(local.at[k + 1], local.at[k + 2], None, outs[2 * section + 1])

    return call(kernel, "combine", [in_vmem(4, 256, 256)] * (2 * SECTIONS), vmem(cross, local), token)


def times(weight, blocks):
    stacked = jnp.concatenate(blocks, axis=0)
    product = jnp.dot(weight, stacked, preferred_element_type=jnp.float32)
    return product.astype(jnp.bfloat16).reshape(len(blocks), 64, stacked.shape[1])


def paired(weight, upper, own, other):
    return times(weight, [jnp.where(upper == 1, other, own), jnp.where(upper == 1, own, other)])


def row_step(section, keep, arrived, cross, token):
    def kernel(ins, outs, scratch):
        keep, arrived, cross = ins[:3]
        row, col = row_side(section), col_side(section)
        for first, out in ((4 - 4 * col, outs[1]), (4 * col, outs[0])):
            for p in range(4):
                h = first + p
                out[2 * p : 2 * p + 2] = paired(cross[2 * section, h], row, keep[h], arrived[h])

    shape = in_vmem(*keep.shape)
    return call(kernel, f"row_{section}", [shape, shape], vmem(keep, arrived, cross), token)


def relay_step(section, by_row, arrived, offset, token):
    columns = by_row.shape[2]

    def kernel(ins, outs, scratch):
        outs[0][:4] = ins[0][...]
        outs[0][4:] = ins[1][4:, :, offset : offset + columns]

    return call(kernel, f"relay_{section}", [in_vmem(8, 64, columns)], vmem(by_row, arrived), token)


def end_step(section, flow, after, state, weights, token, result, start, total):
    early, late, local, cross, lent = weights
    columns = state[0].shape[2]
    pieces_in, offset = state, 0
    if flow == "r":
        *pieces_in, offset = state
    operands = vmem(*pieces_in, early, late, local)
    if flow != "c":
        operands += vmem(cross, lent)
    n = len(pieces_in)

    def halves(ins, buf):
        if flow == "c":
            return (lambda j: ins[0][j]), (lambda j: ins[1][j])
        own, row, col = ins[0], row_side(section), col_side(section)
        if flow == "p":
            by_row, by_col, by_both = (lambda p: ins[1][p]), (lambda p: ins[2][p]), (lambda p: ins[3][p])
        else:
            by_col = lambda p: ins[1][p, :, offset : offset + columns]
            by_row, by_both = (lambda p: ins[2][p]), (lambda p: ins[2][4 + p])
        cross, lent = ins[n + 3], ins[n + 4]
        for p in range(4):
            buf[1, 2 * p : 2 * p + 2] = paired(cross[2 * section, 4 * col + p], row, own[p], by_row(p))
            buf[1, 8 + 2 * p : 10 + 2 * p] = paired(lent[p], row, by_col(p), by_both(p))
        return (lambda j: buf[1, j]), (lambda j: buf[1, 8 + j])

    def kernel(ins, outs, scratch):
        buf = scratch[0]
        early, late, local = ins[n : n + 3]
        mine, theirs = halves(ins, buf)
        for j in range(4):
            buf[0, 4 * j : 4 * j + 4] = times(early[j], [mine(j), theirs(j), mine(4 + j), theirs(4 + j)])
        for j in range(4):
            buf[1, 4 * j : 4 * j + 4] = times(late[j], [buf[0, j], buf[0, 8 + j], buf[0, 4 + j], buf[0, 12 + j]])
        last = section * LOCAL + LOCAL - 1

        def final(h):
            return times(local[last, h], [buf[1, h], buf[1, 8 + h]])

        if after is not None:
            for ranges, out in list(zip(pieces(after, section + 1), outs))[::-1]:
                at = 0
                for first, count in ranges:
                    for p in range(count // 2):
                        out[at : at + 2] = final(first // 2 + p)
                        at += 2
            return
        done, sems = scratch[1:]
        copies = []
        for h in range(8):
            done[2 * h : 2 * h + 2] = final(h)
            copy = pltpu.make_async_copy(
                done.at[pl.ds(2 * h, 2)],
                outs[0].at[pl.ds(2 * h, 2), :, pl.ds(start, columns)],
                sems.at[h],
            )
            copy.start()
            copies.append(copy)
        for copy in copies:
            copy.wait()

    scratch = [in_vmem(2, 16, 64, columns)]
    if after is not None:
        return call(
            kernel, f"end_{section}", shapes(after, columns), operands, token, scratch=scratch
        )
    scratch += [in_vmem(16, 64, columns), pltpu.SemaphoreType.DMA((8,))]
    return call(
        kernel,
        f"end_{section}",
        [pltpu.HBM((16, 64, total), jnp.bfloat16)],
        operands,
        token,
        out_specs=(ANY,),
        scratch=scratch,
        result=result,
    )


def shards(blocks, order, cross_weights, local_weights):
    blocks, order = blocks[0, 0], order[0]
    cross, local = cross_weights[:, 0, 0], local_weights[:, 0, 0]
    total = blocks.shape[2]
    starts = [sum(SIZES[:c]) for c in range(len(SIZES))]
    blocks, *outs = first_take(order, blocks, SIZES[0])
    states = {0: (*sent("r", 0, outs), 0)}
    token, result, ended = outs[0], None, False
    sections, halfway = [0] * len(SIZES), [False] * len(SIZES)
    for c in ORDER:
        if c == LATER:
            lend, together, rest = later_takes(order, blocks, cross, starts[1:], SIZES[1:], token)
            arrived = swapped(together, "col", 0)
            for k, pair in enumerate(rest, 1):
                states[k] = (*pair, arrived, starts[k] - starts[1])
            lent = [
                swapped(lend[s], "col", s) if any(flows[s] != "c" for flows in FLOWS) else None
                for s in range(SECTIONS)
            ]
            token = together
            continue
        if c == COMBINE:
            pairs = combine(cross, local, token)
            token = pairs[0]
            continue
        section, state = sections[c], states[c]
        flow = FLOWS[c][section]
        if flow != "p" and not halfway[c]:
            halfway[c] = True
            if flow == "c":
                keep, send = row_step(section, *state, cross, token)
                states[c] = keep, swapped(send, "col", section)
                token = keep
            else:
                own, by_row, by_col, offset = state
                (joined,) = relay_step(section, by_row, by_col, offset, token)
                states[c] = own, by_col, swapped(joined, "row", section), offset
                token = joined
            ended = False
            continue
        weights = (*pairs[2 * section : 2 * section + 2], local, cross, lent[section])
        after = FLOWS[c][section + 1] if section < SECTIONS - 1 else None
        onto = result if after is None else None
        before = None if ended and onto is not None else token
        outs = end_step(section, flow, after, state, weights, before, onto, starts[c], total)
        sections[c], halfway[c] = section + 1, False
        if after is None:
            (result,) = outs
            token, ended = outside(result), True
        else:
            state = sent(after, section + 1, outs)
            states[c] = (*state, 0) if after == "r" else state
            token, ended = outs[0], False
    return result[None, None]


def solution(mesh):
    placed = (
        P("row", "col", None, None, None),
        P("row", "col", None),
        P(None, "row", "col", None, None, None),
        P(None, "row", "col", None, None, None),
    )
    return jax.shard_map(
        shards,
        mesh=mesh,
        in_specs=placed,
        out_specs=P("row", "col", None, None, None),
        check_vma=False,
    )
```

time: 200 us -> 91.1 us (0.46)
  waiting for transfers between devices: 142 us -> 17.8 us
  starting transfers between devices: 11.5 us -> 52.2 us
  matrix products: 31.2 us -> 0 us
  Pallas kernels: 0 us -> 19.5 us
  other arithmetic: 10.1 us -> 0 us
  local copies, waits for them, and re-layouts: 4.21 us -> 0.01 us
    ppermute x6 -> x27, waiting for transfers between devices: 142 us -> 17.8 us  [the longest x25 17 us: swapped(): lax.ppermute(piece, axis, [(i, i ^ 1 << section) for i in range(size)])]
    ppermute x6 -> x27, starting transfers between devices: 11.5 us -> 52.2 us  [the longest x25 46.3 us: swapped(): lax.ppermute(piece, axis, [(i, i ^ 1 << section) for i in range(size)])]
    dot_general x18 -> x0, matrix products: 31.2 us -> none  [pair_products(): jnp.einsum('hij,hjs->his', weight, stacked, preferred_element_type=jnp.fl...]
    pallas_call x0 -> x25, Pallas kernels: none -> 19.5 us  [call(): pl.pallas_call(body, out_shape=tuple(out_shape), in_specs=specs, out_spec...]
    select_n x14 -> x0, other arithmetic: 9.47 us -> none  [the longest x6 4.7 us: via_halves(): sending = jnp.where(upper_side, lower, upper)]
    slice x12 -> x0, local copies, waits for them, and re-layouts: 2.07 us -> none  [local_level(): coeffs[:half_count]]
  transfers between devices with their start and end apart: 6 -> 27, of which waited for: 6 -> 10; matrix products, arithmetic and copies ran while one was open for 0% -> 0% of each run, Pallas kernels for 0% -> 17%
where the time goes in v2:
time: 91.1 us; the launch traced here: 90 us
  starting transfers between devices  52.2 us (57%)
  Pallas kernels  19.5 us (21%)
  waiting for transfers between devices  17.8 us (20%)
    ppermute x25, starting transfers between devices, swapped(): lax.ppermute(piece, axis, [(i, i ^ 1 << section) for i in range(size)])  46.3 us
    pallas_call x25, Pallas kernels, call(): pl.pallas_call(body, out_shape=tuple(out_shape), in_specs=specs, out_spec...  19.5 us
    ppermute x25, waiting for transfers between devices, swapped(): lax.ppermute(piece, axis, [(i, i ^ 1 << section) for i in range(size)])  17 us
    ppermute x2, starting transfers between devices, swapped_both(): return lax.ppermute(piece, ('row', 'col'), pairs)  5.95 us
  transfers between devices with their start and end apart: 27, of which 10 were waited for; matrix products, arithmetic and copies ran while one was open for 0% of the time, Pallas kernels for 17%

profile of v2, /device:TPU:6, one launch (start us, length us, event | category | flops | bytes accessed | tf_op | source)
XLA Modules:
  0.0 90.0 jit_solution(16512991377946143025)
XLA Ops:
  0.0 1.8 %take_first.1 = (bf16[16,64,1024]{2,1,0:T(8,128)(2,1)S(1)}, bf16[4,64,256]{2,1,0:T(8,128)(2,1)S(1)}, bf16[4,64,256]{2,1,0:T(8,128)(2,1)S(1)}, bf16[8,64,256]{2,1,0:T(8,128)(2,1)S(1)}) custom-call(s32[1,16]{1,0:T(1,128)} %bitcast.33, bf16[16,64,1024]{2,1,0:T(8,128)(2,1)} %bitcast.32), custom_call_target="tpu_custom_call" | custom-call | flops 1 | bytes 1 | tf_op jit(solution)/shard_map/take_first/pallas_call | solution.py:67
  1.8 0.1 collective-permute-start
  1.9 1.5 %collective-permute-done.refs_1_ = bf16[8,64,256]{2,1,0:T(8,128)(2,1)S(1)} collective-permute-done((bf16[8,64,256]{2,1,0:T(8,128)(2,1)S(1)}, bf16[8,64,256]{2,1,0:T(8,128)(2,1)S(1)}, u32[]{:S(2)}, u32[]{:S(2)}) %collective-permute-start) | collective-permute-done | bytes 262176 | tf_op jit(solution)/shard_map/ppermute | solution.py:42
  3.5 0.0 copy-start
  3.5 1.0 %take_later.1 = (bf16[4,128,128]{2,1,0:T(8,128)(2,1)S(1)}, bf16[4,128,128]{2,1,0:T(8,128)(2,1)S(1)}, bf16[4,128,128]{2,1,0:T(8,128)(2,1)S(1)}, bf16[8,64,768]{2,...) custom-call(s32[1,16]{1,0:T(1,128)} %bitcast.34, ...), custom_call_target="tpu_custom_call" | custom-call | flops 1 | bytes 1 | tf_op jit(solution)/shard_map/take_later/pallas_call | solution.py:67
  4.5 0.2 collective-permute-start.1
  4.7 1.4 %collective-permute-start.5 = (bf16[8,64,256]{2,1,0:T(8,128)(2,1)S(1)}, bf16[8,64,256]{2,1,0:T(8,128)(2,1)S(1)}, u32[]{:S(2)}, u32[]{:S(2)}) collective-permute-start(bf16[8,64,256]{2,1,0:T(8,128)(2,1)S(1)} %relay_0.4.refs_3_), channel_id=1, source_target_pairs={{0,16},{16,0},{32,48},{48,32},{64,80},{80,64},{96,112},{112,96},{1... | collective-permute-start | bytes 786440 | tf_op jit(solution)/shard_map/ppermute | solution.py:42
  6.1 0.7 collective-permute-done.1.refs_1_
  6.9 1.0 %combine.1 = (bf16[4,256,256]{2,1,0:T(8,128)(2,1)S(1)}, bf16[4,256,256]{2,1,0:T(8,128)(2,1)S(1)}, bf16[4,256,256]{2,1,0:T(8,128)(2,1)S(1)}, bf16[4,256,256]{2,1,...) custom-call(bf16[6,8,128,128]{3,2,1,0:T(8,128)(2,1)S(1)} %bitcast.19, ...), custom_call_target="tpu_custom_call" | custom-call | flops 1 | bytes 1 | tf_op jit(solution)/shard_map/combine/pallas_call | solution.py:67
  8.0 1.5 %collective-permute-start.4 = (bf16[8,64,256]{2,1,0:T(8,128)(2,1)S(1)}, bf16[8,64,256]{2,1,0:T(8,128)(2,1)S(1)}, u32[]{:S(2)}, u32[]{:S(2)}) collective-permute-start(bf16[8,64,256]{2,1,0:T(8,128)(2,1)S(1)} %relay_0.6.refs_2_), channel_id=1, source_target_pairs={{0,16},{16,0},{32,48},{48,32},{64,80},{80,64},{96,112},{112,96},{1... | collective-permute-start | bytes 786440 | tf_op jit(solution)/shard_map/ppermute | solution.py:42
  9.5 1.3 %collective-permute-done.3.refs_7_ = bf16[4,128,128]{2,1,0:T(8,128)(2,1)S(1)} collective-permute-done((bf16[4,128,128]{2,1,0:T(8,128)(2,1)S(1)}, bf16[4,128,128]{2,1,0:T(8,128)(2,1)S(1)}, u32[]{:S(2)}, u32[]{:S(2)}) %collective-permute-start.3) | collective-permute-done | bytes 131104 | tf_op jit(solution)/shard_map/ppermute | solution.py:42
  10.8 4.6 %collective-permute-done.5.refs_2_ = bf16[8,64,256]{2,1,0:T(8,128)(2,1)S(1)} collective-permute-done((bf16[8,64,256]{2,1,0:T(8,128)(2,1)S(1)}, bf16[8,64,256]{2,1,0:T(8,128)(2,1)S(1)}, u32[]{:S(2)}, u32[]{:S(2)}) %collective-permute-start.5) | collective-permute-done | bytes 262176 | tf_op jit(solution)/shard_map/ppermute | solution.py:42
  15.3 1.0 %end_0.4 = (bf16[4,64,256]{2,1,0:T(8,128)(2,1)S(1)}, bf16[4,64,256]{2,1,0:T(8,128)(2,1)S(1)}, bf16[8,64,256]{2,1,0:T(8,128)(2,1)S(1)}) custom-call(bf16[4,64,256]{2,1,0:T(8,128)(2,1)S(1)} %get-tuple-element.58.refs_2_.refs_0_, bf16[8,64,256]{2,1,0:T(8,128)(2,1)S(1)} %collective-permute-done.refs_1_, bf16[8,64,256]{2,1,0:T(8,128)(2,1)S(1)} %collective-permute-done.5.refs_2_, ...), custom_call_target="tpu_custom_call" | custom-call | flops 1 | bytes 1 | tf_op jit(solution)/shard_map/end_0/pallas_call | solution.py:67
  16.4 1.7 %collective-permute-start.8 = (bf16[8,64,256]{2,1,0:T(8,128)(2,1)S(1)}, bf16[8,64,256]{2,1,0:T(8,128)(2,1)S(1)}, u32[]{:S(2)}, u32[]{:S(2)}) collective-permute-start(bf16[8,64,256]{2,1,0:T(8,128)(2,1)S(1)} %get-tuple-element.73), channel_id=1, source_target_pairs={{0,2},{1,3},{2,0},{3,1},{4,6},{5,7},{6,4},{7,5},{8,10},{9,11},{10,... | collective-permute-start | bytes 786440 | tf_op jit(solution)/shard_map/ppermute | solution.py:42
  18.1 1.4 %collective-permute-start.7 = (bf16[8,64,256]{2,1,0:T(8,128)(2,1)S(1)}, bf16[8,64,256]{2,1,0:T(8,128)(2,1)S(1)}, u32[]{:S(2)}, u32[]{:S(2)}) collective-permute-start(bf16[8,64,256]{2,1,0:T(8,128)(2,1)S(1)} %relay_0.7.refs_8_), channel_id=1, source_target_pairs={{0,16},{16,0},{32,48},{48,32},{64,80},{80,64},{96,112},{112,96},{1... | collective-permute-start | bytes 786440 | tf_op jit(solution)/shard_map/ppermute | solution.py:42
  19.5 0.9 %collective-permute-done.4.refs_2_ = bf16[8,64,256]{2,1,0:T(8,128)(2,1)S(1)} collective-permute-done((bf16[8,64,256]{2,1,0:T(8,128)(2,1)S(1)}, bf16[8,64,256]{2,1,0:T(8,128)(2,1)S(1)}, u32[]{:S(2)}, u32[]{:S(2)}) %collective-permute-start.4) | collective-permute-done | bytes 262176 | tf_op jit(solution)/shard_map/ppermute | solution.py:42
  20.4 1.0 %end_0.5 = (bf16[8,64,256]{2,1,0:T(8,128)(2,1)S(1)}, bf16[8,64,256]{2,1,0:T(8,128)(2,1)S(1)}) custom-call(bf16[4,64,256]{2,1,0:T(8,128)(2,1)S(1)} %get-tuple-element.65.refs_0_, bf16[8,64,768]{2,1,0:T(8,128)(2,1)S(1)} %collective-permute-done.1.refs_1_, bf16[8,64,256]{2,1,0:T(8,128)(2,1)S(1)} %collective-permute-done.4.refs_2_, ...), custom_call_target="tpu_custom_call" | custom-call | flops 1 | bytes 1 | tf_op jit(solution)/shard_map/end_0/pallas_call | solution.py:67
  21.5 2.0 %collective-permute-start.6 = (bf16[8,64,256]{2,1,0:T(8,128)(2,1)S(1)}, bf16[8,64,256]{2,1,0:T(8,128)(2,1)S(1)}, u32[]{:S(2)}, u32[]{:S(2)}) collective-permute-start(bf16[8,64,256]{2,1,0:T(8,128)(2,1)S(1)} %get-tuple-element.70), channel_id=1, source_target_pairs={{0,32},{16,48},{32,0},{48,16},{64,96},{80,112},{96,64},{112,80},{1... | collective-permute-start | bytes 786440 | tf_op jit(solution)/shard_map/ppermute | solution.py:42
  23.5 1.4 %collective-permute-start.2 = (bf16[8,64,256]{2,1,0:T(8,128)(2,1)S(1)}, bf16[8,64,256]{2,1,0:T(8,128)(2,1)S(1)}, u32[]{:S(2)}, u32[]{:S(2)}) collective-permute-start(bf16[8,64,256]{2,1,0:T(8,128)(2,1)S(1)} %relay_0.5.refs_2_), channel_id=1, source_target_pairs={{0,16},{16,0},{32,48},{48,32},{64,80},{80,64},{96,112},{112,96},{1... | collective-permute-start | bytes 786440 | tf_op jit(solution)/shard_map/ppermute | solution.py:42
  24.9 0.0 collective-permute-done.8.refs_1_
  24.9 1.6 %collective-permute-done.7.refs_2_ = bf16[8,64,256]{2,1,0:T(8,128)(2,1)S(1)} collective-permute-done((bf16[8,64,256]{2,1,0:T(8,128)(2,1)S(1)}, bf16[8,64,256]{2,1,0:T(8,128)(2,1)S(1)}, u32[]{:S(2)}, u32[]{:S(2)}) %collective-permute-start.7) | collective-permute-done | bytes 262176 | tf_op jit(solution)/shard_map/ppermute | solution.py:42
  26.5 1.0 %end_0.6 = (bf16[8,64,256]{2,1,0:T(8,128)(2,1)S(1)}, bf16[8,64,256]{2,1,0:T(8,128)(2,1)S(1)}) custom-call(bf16[4,64,256]{2,1,0:T(8,128)(2,1)S(1)} %get-tuple-element.71.refs_0_, bf16[8,64,768]{2,1,0:T(8,128)(2,1)S(1)} %collective-permute-done.1.refs_1_, bf16[8,64,256]{2,1,0:T(8,128)(2,1)S(1)} %collective-permute-done.7.refs_2_, ...), custom_call_target="tpu_custom_call" | custom-call | flops 1 | bytes 1 | tf_op jit(solution)/shard_map/end_0/pallas_call | solution.py:67
  27.6 3.1 %collective-permute-start.14 = (bf16[8,64,256]{2,1,0:T(8,128)(2,1)S(1)}, bf16[8,64,256]{2,1,0:T(8,128)(2,1)S(1)}, u32[]{:S(2)}, u32[]{:S(2)}) collective-permute-start(bf16[8,64,256]{2,1,0:T(8,128)(2,1)S(1)} %get-tuple-element.84), channel_id=1, source_target_pairs={{0,32},{16,48},{32,0},{48,16},{64,96},{80,112},{96,64},{112,80},{1... | collective-permute-start | bytes 786440 | tf_op jit(solution)/shard_map/ppermute | solution.py:42
  30.7 0.1 collective-permute-done.6.refs_1_
  30.8 0.3 row_1.2
  31.1 1.4 %collective-permute-start.13 = (bf16[8,64,256]{2,1,0:T(8,128)(2,1)S(1)}, bf16[8,64,256]{2,1,0:T(8,128)(2,1)S(1)}, u32[]{:S(2)}, u32[]{:S(2)}) collective-permute-start(bf16[8,64,256]{2,1,0:T(8,128)(2,1)S(1)} %get-tuple-element.83), channel_id=1, source_target_pairs={{0,2},{1,3},{2,0},{3,1},{4,6},{5,7},{6,4},{7,5},{8,10},{9,11},{10,... | collective-permute-start | bytes 786440 | tf_op jit(solution)/shard_map/ppermute | solution.py:42
  32.5 1.7 %collective-permute-start.17 = (bf16[8,64,256]{2,1,0:T(8,128)(2,1)S(1)}, bf16[8,64,256]{2,1,0:T(8,128)(2,1)S(1)}, u32[]{:S(2)}, u32[]{:S(2)}) collective-permute-start(bf16[8,64,256]{2,1,0:T(8,128)(2,1)S(1)} %relay_1.1.refs_8_), channel_id=1, source_target_pairs={{0,32},{16,48},{32,0},{48,16},{64,96},{80,112},{96,64},{112,80},{1... | collective-permute-start | bytes 786440 | tf_op jit(solution)/shard_map/ppermute | solution.py:42
  34.2 1.1 %end_0.7 = (bf16[4,64,256]{2,1,0:T(8,128)(2,1)S(1)}, bf16[4,64,256]{2,1,0:T(8,128)(2,1)S(1)}, bf16[4,64,256]{2,1,0:T(8,128)(2,1)S(1)}, bf16[4,64,256]{2,1,0:T(8,128)(2,1)S(1)}) custom-call(bf16[4,64,256]{2,1,0:T(8,128)(2,1)S(1)} %get-tuple-element.59.refs_0_, bf16[8,64,768]{2,1,0:T(8,128)(2,1)S(1)} %collective-permute-done.1.refs_1_, ...), custom_call_target="tpu_custom_call" | custom-call | flops 1 | bytes 1 | tf_op jit(solution)/shard_map/end_0/pallas_call | solution.py:67
  35.3 2.6 %collective-permute-done.14.refs_1_ = bf16[8,64,256]{2,1,0:T(8,128)(2,1)S(1)} collective-permute-done((bf16[8,64,256]{2,1,0:T(8,128)(2,1)S(1)}, bf16[8,64,256]{2,1,0:T(8,128)(2,1)S(1)}, u32[]{:S(2)}, u32[]{:S(2)}) %collective-permute-start.14) | collective-permute-done | bytes 262176 | tf_op jit(solution)/shard_map/ppermute | solution.py:42
  37.9 0.3 row_1.3
  38.2 0.7 collective-permute-start.16
  38.9 0.8 end_1.4
  39.8 3.3 %collective-permute-start.15 = (bf16[8,64,256]{2,1,0:T(8,128)(2,1)S(1)}, bf16[8,64,256]{2,1,0:T(8,128)(2,1)S(1)}, u32[]{:S(2)}, u32[]{:S(2)}) collective-permute-start(bf16[8,64,256]{2,1,0:T(8,128)(2,1)S(1)} %get-tuple-element.87), channel_id=1, source_target_pairs={{0,64},{16,80},{32,96},{48,112},{64,0},{80,16},{96,32},{112,48},{1... | collective-permute-start | bytes 786440 | tf_op jit(solution)/shard_map/ppermute | solution.py:42
  43.1 1.4 %collective-permute-start.12 = (bf16[4,128,128]{2,1,0:T(8,128)(2,1)S(1)}, bf16[4,128,128]{2,1,0:T(8,128)(2,1)S(1)}, u32[]{:S(2)}, u32[]{:S(2)}) collective-permute-start(bf16[4,128,128]{2,1,0:T(8,128)(2,1)S(1)} %get-tuple-element.82), channel_id=1, source_target_pairs={{0,2},{1,3},{2,0},{3,1},{4,6},{5,7},{6,4},{7,5},{8,10},{9,11},{10,... | collective-permute-start | bytes 393224 | tf_op jit(solution)/shard_map/ppermute | solution.py:42
  44.5 3.6 %collective-permute-done.12.refs_7_.refs_8_ = bf16[4,128,128]{2,1,0:T(8,128)(2,1)S(1)} collective-permute-done((bf16[4,128,128]{2,1,0:T(8,128)(2,1)S(1)}, bf16[4,128,128]{2,1,0:T(8,128)(2,1)S(1)}, u32[]{:S(2)}, u32[]{:S(2)}) %collective-permute-start.12) | collective-permute-done | bytes 131104 | tf_op jit(solution)/shard_map/ppermute | solution.py:42
  48.1 0.0 collective-permute-done.17.refs_2_
  48.1 1.1 %end_1.5 = (bf16[8,64,256]{2,1,0:T(8,128)(2,1)S(1)}, bf16[8,64,256]{2,1,0:T(8,128)(2,1)S(1)}) custom-call(bf16[4,64,256]{2,1,0:T(8,128)(2,1)S(1)} %get-tuple-element.68.refs_8_.refs_0_, bf16[8,64,256]{2,1,0:T(8,128)(2,1)S(1)} %collective-permute-done.8.refs_1_, bf16[8,64,256]{2,1,0:T(8,128)(2,1)S(1)} %collective-permute-done.17.refs_2_, ...), custom_call_target="tpu_custom_call" | custom-call | flops 1 | bytes 1 | tf_op jit(solution)/shard_map/end_1/pallas_call | solution.py:67
  49.2 0.0 collective-permute-done.16.refs_1_
  49.2 0.8 end_1.6
  50.0 3.8 %collective-permute-start.20 = (bf16[8,64,256]{2,1,0:T(8,128)(2,1)S(1)}, bf16[8,64,256]{2,1,0:T(8,128)(2,1)S(1)}, u32[]{:S(2)}, u32[]{:S(2)}) collective-permute-start(bf16[8,64,256]{2,1,0:T(8,128)(2,1)S(1)} %get-tuple-element.97), channel_id=1, source_target_pairs={{0,4},{1,5},{2,6},{3,7},{4,0},{5,1},{6,2},{7,3},{8,12},{9,13},{10,... | collective-permute-start | bytes 786440 | tf_op jit(solution)/shard_map/ppermute | solution.py:42
  53.8 0.6 collective-permute-start.19
  54.4 0.0 collective-permute-done.15.refs_1_
  54.4 0.3 row_2.2
  54.7 4.7 %collective-permute-start.18 = (bf16[8,64,256]{2,1,0:T(8,128)(2,1)S(1)}, bf16[8,64,256]{2,1,0:T(8,128)(2,1)S(1)}, u32[]{:S(2)}, u32[]{:S(2)}) collective-permute-start(bf16[8,64,256]{2,1,0:T(8,128)(2,1)S(1)} %get-tuple-element.92), channel_id=1, source_target_pairs={{0,4},{1,5},{2,6},{3,7},{4,0},{5,1},{6,2},{7,3},{8,12},{9,13},{10,... | collective-permute-start | bytes 786440 | tf_op jit(solution)/shard_map/ppermute | solution.py:42
  59.5 3.5 %collective-permute-start.9 = (bf16[4,64,256]{2,1,0:T(8,128)(2,1)S(1)}, bf16[4,64,256]{2,1,0:T(8,128)(2,1)S(1)}, u32[]{:S(2)}, u32[]{:S(2)}) collective-permute-start(bf16[4,64,256]{2,1,0:T(8,128)(2,1)S(1)} %get-tuple-element.77), channel_id=1, source_target_pairs={{0,32},{16,48},{32,0},{48,16},{64,96},{80,112},{96,64},{112,80},{1... | collective-permute-start | bytes 393224 | tf_op jit(solution)/shard_map/ppermute | solution.py:42
  63.0 0.0 collective-permute-start.10
  63.0 0.0 collective-permute-done.20.refs_1_
  63.0 1.8 %collective-permute-start.11 = (bf16[4,64,256]{2,1,0:T(8,128)(2,1)S(1)}, bf16[4,64,256]{2,1,0:T(8,128)(2,1)S(1)}, u32[]{:S(2)}, u32[]{:S(2)}) collective-permute-start(bf16[4,64,256]{2,1,0:T(8,128)(2,1)S(1)} %get-tuple-element.79), channel_id=1, source_target_pairs={{0,34},{1,35},{2,32},{3,33},{4,38},{5,39},{6,36},{7,37},{8,42},{9,... | collective-permute-start | bytes 393224 | tf_op jit(solution)/shard_map/ppermute | solution.py:48
  64.8 3.6 %collective-permute-start.26 = (bf16[8,64,256]{2,1,0:T(8,128)(2,1)S(1)}, bf16[8,64,256]{2,1,0:T(8,128)(2,1)S(1)}, u32[]{:S(2)}, u32[]{:S(2)}) collective-permute-start(bf16[8,64,256]{2,1,0:T(8,128)(2,1)S(1)} %relay_2.1.refs_3_), channel_id=1, source_target_pairs={{0,64},{16,80},{32,96},{48,112},{64,0},{80,16},{96,32},{112,48},{1... | collective-permute-start | bytes 786440 | tf_op jit(solution)/shard_map/ppermute | solution.py:42
  68.4 0.3 row_2.3
  68.7 0.9 %collective-permute-start.25 = (bf16[8,64,256]{2,1,0:T(8,128)(2,1)S(1)}, bf16[8,64,256]{2,1,0:T(8,128)(2,1)S(1)}, u32[]{:S(2)}, u32[]{:S(2)}) collective-permute-start(bf16[8,64,256]{2,1,0:T(8,128)(2,1)S(1)} %get-tuple-element.104), channel_id=1, source_target_pairs={{0,4},{1,5},{2,6},{3,7},{4,0},{5,1},{6,2},{7,3},{8,12},{9,13},{10,... | collective-permute-start | bytes 786440 | tf_op jit(solution)/shard_map/ppermute | solution.py:42
  69.6 0.0 collective-permute-done.18.refs_1_
  69.6 2.7 %collective-permute-start.24 = (bf16[4,128,128]{2,1,0:T(8,128)(2,1)S(1)}, bf16[4,128,128]{2,1,0:T(8,128)(2,1)S(1)}, u32[]{:S(2)}, u32[]{:S(2)}) collective-permute-start(bf16[4,128,128]{2,1,0:T(8,128)(2,1)S(1)} %get-tuple-element.103), channel_id=1, source_target_pairs={{0,4},{1,5},{2,6},{3,7},{4,0},{5,1},{6,2},{7,3},{8,12},{9,13},{10,... | collective-permute-start | bytes 393224 | tf_op jit(solution)/shard_map/ppermute | solution.py:42
  72.3 1.5 %end_2.4.refs_9_.refs_8_ = bf16[16,64,1024]{2,1,0:T(8,128)(2,1)} custom-call(bf16[8,64,256]{2,1,0:T(8,128)(2,1)S(1)} %get-tuple-element.91.refs_2_.refs_0_, bf16[8,64,256]{2,1,0:T(8,128)(2,1)S(1)} %collective-permute-done.18.refs_1_, bf16[4,256,256]{2,1,0:T(8,128)(2,1)S(1)} %get-tuple-element.93.refs_2_.refs_3_.refs_4_, ...), custom_call_target="tpu_custom_call" | custom-call | flops 1 | bytes 1 | tf_op jit(solution)/shard_map/end_2/pallas_call | solution.py:67
  73.9 0.0 collective-permute-done.10.refs_2_
  73.9 0.0 collective-permute-done.11.refs_3_
  73.9 1.1 %end_1.7 = (bf16[4,64,256]{2,1,0:T(8,128)(2,1)S(1)}, bf16[4,64,256]{2,1,0:T(8,128)(2,1)S(1)}, bf16[4,64,256]{2,1,0:T(8,128)(2,1)S(1)}, bf16[4,64,256]{2,1,0:T(8,128)(2,1)S(1)}) custom-call(bf16[4,64,256]{2,1,0:T(8,128)(2,1)S(1)} %get-tuple-element.76.refs_3_.refs_0_, bf16[4,64,256]{2,1,0:T(8,128)(2,1)S(1)} %collective-permute-done.9.refs_1_, ...), custom_call_target="tpu_custom_call" | custom-call | flops 1 | bytes 1 | tf_op jit(solution)/shard_map/end_1/pallas_call | solution.py:67
  74.9 3.2 %collective-permute-start.21 = (bf16[4,64,256]{2,1,0:T(8,128)(2,1)S(1)}, bf16[4,64,256]{2,1,0:T(8,128)(2,1)S(1)}, u32[]{:S(2)}, u32[]{:S(2)}) collective-permute-start(bf16[4,64,256]{2,1,0:T(8,128)(2,1)S(1)} %get-tuple-element.100), channel_id=1, source_target_pairs={{0,64},{16,80},{32,96},{48,112},{64,0},{80,16},{96,32},{112,48},{1... | collective-permute-start | bytes 393224 | tf_op jit(solution)/shard_map/ppermute | solution.py:42
  78.2 1.6 %collective-permute-start.22 = (bf16[4,64,256]{2,1,0:T(8,128)(2,1)S(1)}, bf16[4,64,256]{2,1,0:T(8,128)(2,1)S(1)}, u32[]{:S(2)}, u32[]{:S(2)}) collective-permute-start(bf16[4,64,256]{2,1,0:T(8,128)(2,1)S(1)} %get-tuple-element.101), channel_id=1, source_target_pairs={{0,4},{1,5},{2,6},{3,7},{4,0},{5,1},{6,2},{7,3},{8,12},{9,13},{10,... | collective-permute-start | bytes 393224 | tf_op jit(solution)/shard_map/ppermute | solution.py:42
  79.8 4.2 %collective-permute-start.23 = (bf16[4,64,256]{2,1,0:T(8,128)(2,1)S(1)}, bf16[4,64,256]{2,1,0:T(8,128)(2,1)S(1)}, u32[]{:S(2)}, u32[]{:S(2)}) collective-permute-start(bf16[4,64,256]{2,1,0:T(8,128)(2,1)S(1)} %get-tuple-element.102), channel_id=1, source_target_pairs={{0,68},{1,69},{2,70},{3,71},{4,64},{5,65},{6,66},{7,67},{8,76},{9,... | collective-permute-start | bytes 393224 | tf_op jit(solution)/shard_map/ppermute | solution.py:48
  84.0 1.7 %end_2.5.refs_5_ = bf16[16,64,1024]{2,1,0:T(8,128)(2,1)} custom-call(bf16[4,64,256]{2,1,0:T(8,128)(2,1)S(1)} %get-tuple-element.90.refs_3_.refs_0_, bf16[8,64,256]{2,1,0:T(8,128)(2,1)S(1)} %collective-permute-done.20.refs_1_, bf16[8,64,256]{2,1,0:T(8,128)(2,1)S(1)} %collective-permute-done.26.refs_2_, ...), custom_call_target="tpu_custom_call", output_to_operand_aliasing={{}: (8, {})} | custom-call | flops 1 | bytes 1 | tf_op jit(solution)/shard_map/end_2/pallas_call | solution.py:67
  85.7 1.5 %end_2.6.refs_9_ = bf16[16,64,1024]{2,1,0:T(8,128)(2,1)} custom-call(bf16[8,64,256]{2,1,0:T(8,128)(2,1)S(1)} %get-tuple-element.98.refs_5_.refs_0_, bf16[8,64,256]{2,1,0:T(8,128)(2,1)S(1)} %collective-permute-done.25.refs_1_, bf16[4,256,256]{2,1,0:T(8,128)(2,1)S(1)} %get-tuple-element.93.refs_2_.refs_3_.refs_4_, ...), custom_call_target="tpu_custom_call", output_to_operand_aliasing={{}: (5, {})} | custom-call | flops 1 | bytes 1 | tf_op jit(solution)/shard_map/end_2/pallas_call | solution.py:67
  87.3 0.8 collective-permute-done.23.refs_3_
  88.1 1.7 %end_2.7 = bf16[16,64,1024]{2,1,0:T(8,128)(2,1)} custom-call(bf16[4,64,256]{2,1,0:T(8,128)(2,1)S(1)} %get-tuple-element.99.refs_9_.refs_0_, bf16[4,64,256]{2,1,0:T(8,128)(2,1)S(1)} %collective-permute-done.21.refs_1_, bf16[4,64,256]{2,1,0:T(8,128)(2,1)S(1)} %collective-permute-done.22.refs_2_, ...), custom_call_target="tpu_custom_call", output_to_operand_aliasing={{}: (9, {})} | custom-call | flops 1 | bytes 1 | tf_op jit(solution)/shard_map/end_2/pallas_call | solution.py:67
  (19 shorter events, 0.1 us)
Async XLA Ops:
  0.0 3.5 %copy-start.1 = (bf16[6,1,1,8,128,128]{5,4,3,2,1,0:T(8,128)(2,1)S(1)}, bf16[6,1,1,8,128,128]{5,4,3,2,1,0:T(8,128)(2,1)}, u32[]{:S(2)}) copy-start(bf16[6,1,1,8,128,128]{5,4,3,2,1,0:T(8,128)(2,1)} %param.6) | copy-start | bytes 4718596
  1.8 1.6 %collective-permute-start = (bf16[8,64,256]{2,1,0:T(8,128)(2,1)S(1)}, bf16[8,64,256]{2,1,0:T(8,128)(2,1)S(1)}, u32[]{:S(2)}, u32[]{:S(2)}) collective-permute-start(bf16[8,64,256]{2,1,0:T(8,128)(2,1)S(1)} %get-tuple-element.57), channel_id=1, source_target_pairs={{0,1},{1,0},{2,3},{3,2},{4,5},{5,4},{6,7},{7,6},{8,9},{9,8},{10,11... | collective-permute-start | bytes 786440 | tf_op jit(solution)/shard_map/ppermute | solution.py:42
  3.5 3.4 %copy-start = (bf16[12,1,1,8,128,128]{5,4,3,2,1,0:T(8,128)(2,1)S(1)}, bf16[12,1,1,8,128,128]{5,4,3,2,1,0:T(8,128)(2,1)}, u32[]{:S(2)}) copy-start(bf16[12,1,1,8,128,128]{5,4,3,2,1,0:T(8,128)(2,1)} %param.7) | copy-start | bytes 9437188
  4.5 2.4 %collective-permute-start.1 = (bf16[8,64,768]{2,1,0:T(8,128)(2,1)S(1)}, bf16[8,64,768]{2,1,0:T(8,128)(2,1)S(1)}, u32[]{:S(2)}, u32[]{:S(2)}) collective-permute-start(bf16[8,64,768]{2,1,0:T(8,128)(2,1)S(1)} %get-tuple-element.60.refs_2_), channel_id=1, source_target_pairs={{0,1},{1,0},{2,3},{3,2},{4,5},{5,4},{6,7},{7,6},{8,9},{9,8},{10,11... | collective-permute-start | bytes 2359304 | tf_op jit(solution)/shard_map/ppermute | solution.py:42
  4.7 10.6 %collective-permute-start.5 = (bf16[8,64,256]{2,1,0:T(8,128)(2,1)S(1)}, bf16[8,64,256]{2,1,0:T(8,128)(2,1)S(1)}, u32[]{:S(2)}, u32[]{:S(2)}) collective-permute-start(bf16[8,64,256]{2,1,0:T(8,128)(2,1)S(1)} %relay_0.4.refs_3_), channel_id=1, source_target_pairs={{0,16},{16,0},{32,48},{48,32},{64,80},{80,64},{96,112},{112,96},{1... | collective-permute-start | bytes 786440 | tf_op jit(solution)/shard_map/ppermute | solution.py:42
  8.0 12.5 %collective-permute-start.4 = (bf16[8,64,256]{2,1,0:T(8,128)(2,1)S(1)}, bf16[8,64,256]{2,1,0:T(8,128)(2,1)S(1)}, u32[]{:S(2)}, u32[]{:S(2)}) collective-permute-start(bf16[8,64,256]{2,1,0:T(8,128)(2,1)S(1)} %relay_0.6.refs_2_), channel_id=1, source_target_pairs={{0,16},{16,0},{32,48},{48,32},{64,80},{80,64},{96,112},{112,96},{1... | collective-permute-start | bytes 786440 | tf_op jit(solution)/shard_map/ppermute | solution.py:42
  9.4 1.3 %collective-permute-start.3 = (bf16[4,128,128]{2,1,0:T(8,128)(2,1)S(1)}, bf16[4,128,128]{2,1,0:T(8,128)(2,1)S(1)}, u32[]{:S(2)}, u32[]{:S(2)}) collective-permute-start(bf16[4,128,128]{2,1,0:T(8,128)(2,1)S(1)} %get-tuple-element.64), channel_id=1, source_target_pairs={{0,1},{1,0},{2,3},{3,2},{4,5},{5,4},{6,7},{7,6},{8,9},{9,8},{10,11... | collective-permute-start | bytes 393224 | tf_op jit(solution)/shard_map/ppermute | solution.py:42
  16.4 8.5 %collective-permute-start.8 = (bf16[8,64,256]{2,1,0:T(8,128)(2,1)S(1)}, bf16[8,64,256]{2,1,0:T(8,128)(2,1)S(1)}, u32[]{:S(2)}, u32[]{:S(2)}) collective-permute-start(bf16[8,64,256]{2,1,0:T(8,128)(2,1)S(1)} %get-tuple-element.73), channel_id=1, source_target_pairs={{0,2},{1,3},{2,0},{3,1},{4,6},{5,7},{6,4},{7,5},{8,10},{9,11},{10,... | collective-permute-start | bytes 786440 | tf_op jit(solution)/shard_map/ppermute | solution.py:42
  18.1 8.4 %collective-permute-start.7 = (bf16[8,64,256]{2,1,0:T(8,128)(2,1)S(1)}, bf16[8,64,256]{2,1,0:T(8,128)(2,1)S(1)}, u32[]{:S(2)}, u32[]{:S(2)}) collective-permute-start(bf16[8,64,256]{2,1,0:T(8,128)(2,1)S(1)} %relay_0.7.refs_8_), channel_id=1, source_target_pairs={{0,16},{16,0},{32,48},{48,32},{64,80},{80,64},{96,112},{112,96},{1... | collective-permute-start | bytes 786440 | tf_op jit(solution)/shard_map/ppermute | solution.py:42
  21.5 9.3 %collective-permute-start.6 = (bf16[8,64,256]{2,1,0:T(8,128)(2,1)S(1)}, bf16[8,64,256]{2,1,0:T(8,128)(2,1)S(1)}, u32[]{:S(2)}, u32[]{:S(2)}) collective-permute-start(bf16[8,64,256]{2,1,0:T(8,128)(2,1)S(1)} %get-tuple-element.70), channel_id=1, source_target_pairs={{0,32},{16,48},{32,0},{48,16},{64,96},{80,112},{96,64},{112,80},{1... | collective-permute-start | bytes 786440 | tf_op jit(solution)/shard_map/ppermute | solution.py:42
  23.5 10.8 %collective-permute-start.2 = (bf16[8,64,256]{2,1,0:T(8,128)(2,1)S(1)}, bf16[8,64,256]{2,1,0:T(8,128)(2,1)S(1)}, u32[]{:S(2)}, u32[]{:S(2)}) collective-permute-start(bf16[8,64,256]{2,1,0:T(8,128)(2,1)S(1)} %relay_0.5.refs_2_), channel_id=1, source_target_pairs={{0,16},{16,0},{32,48},{48,32},{64,80},{80,64},{96,112},{112,96},{1... | collective-permute-start | bytes 786440 | tf_op jit(solution)/shard_map/ppermute | solution.py:42
  27.6 10.4 %collective-permute-start.14 = (bf16[8,64,256]{2,1,0:T(8,128)(2,1)S(1)}, bf16[8,64,256]{2,1,0:T(8,128)(2,1)S(1)}, u32[]{:S(2)}, u32[]{:S(2)}) collective-permute-start(bf16[8,64,256]{2,1,0:T(8,128)(2,1)S(1)} %get-tuple-element.84), channel_id=1, source_target_pairs={{0,32},{16,48},{32,0},{48,16},{64,96},{80,112},{96,64},{112,80},{1... | collective-permute-start | bytes 786440 | tf_op jit(solution)/shard_map/ppermute | solution.py:42
  31.1 7.9 %collective-permute-start.13 = (bf16[8,64,256]{2,1,0:T(8,128)(2,1)S(1)}, bf16[8,64,256]{2,1,0:T(8,128)(2,1)S(1)}, u32[]{:S(2)}, u32[]{:S(2)}) collective-permute-start(bf16[8,64,256]{2,1,0:T(8,128)(2,1)S(1)} %get-tuple-element.83), channel_id=1, source_target_pairs={{0,2},{1,3},{2,0},{3,1},{4,6},{5,7},{6,4},{7,5},{8,10},{9,11},{10,... | collective-permute-start | bytes 786440 | tf_op jit(solution)/shard_map/ppermute | solution.py:42
  32.5 15.6 %collective-permute-start.17 = (bf16[8,64,256]{2,1,0:T(8,128)(2,1)S(1)}, bf16[8,64,256]{2,1,0:T(8,128)(2,1)S(1)}, u32[]{:S(2)}, u32[]{:S(2)}) collective-permute-start(bf16[8,64,256]{2,1,0:T(8,128)(2,1)S(1)} %relay_1.1.refs_8_), channel_id=1, source_target_pairs={{0,32},{16,48},{32,0},{48,16},{64,96},{80,112},{96,64},{112,80},{1... | collective-permute-start | bytes 786440 | tf_op jit(solution)/shard_map/ppermute | solution.py:42
  38.2 10.9 %collective-permute-start.16 = (bf16[8,64,256]{2,1,0:T(8,128)(2,1)S(1)}, bf16[8,64,256]{2,1,0:T(8,128)(2,1)S(1)}, u32[]{:S(2)}, u32[]{:S(2)}) collective-permute-start(bf16[8,64,256]{2,1,0:T(8,128)(2,1)S(1)} %get-tuple-element.88), channel_id=1, source_target_pairs={{0,2},{1,3},{2,0},{3,1},{4,6},{5,7},{6,4},{7,5},{8,10},{9,11},{10,... | collective-permute-start | bytes 786440 | tf_op jit(solution)/shard_map/ppermute | solution.py:42
  39.8 14.6 %collective-permute-start.15 = (bf16[8,64,256]{2,1,0:T(8,128)(2,1)S(1)}, bf16[8,64,256]{2,1,0:T(8,128)(2,1)S(1)}, u32[]{:S(2)}, u32[]{:S(2)}) collective-permute-start(bf16[8,64,256]{2,1,0:T(8,128)(2,1)S(1)} %get-tuple-element.87), channel_id=1, source_target_pairs={{0,64},{16,80},{32,96},{48,112},{64,0},{80,16},{96,32},{112,48},{1... | collective-permute-start | bytes 786440 | tf_op jit(solution)/shard_map/ppermute | solution.py:42
  43.1 5.0 %collective-permute-start.12 = (bf16[4,128,128]{2,1,0:T(8,128)(2,1)S(1)}, bf16[4,128,128]{2,1,0:T(8,128)(2,1)S(1)}, u32[]{:S(2)}, u32[]{:S(2)}) collective-permute-start(bf16[4,128,128]{2,1,0:T(8,128)(2,1)S(1)} %get-tuple-element.82), channel_id=1, source_target_pairs={{0,2},{1,3},{2,0},{3,1},{4,6},{5,7},{6,4},{7,5},{8,10},{9,11},{10,... | collective-permute-start | bytes 393224 | tf_op jit(solution)/shard_map/ppermute | solution.py:42
  50.0 13.0 %collective-permute-start.20 = (bf16[8,64,256]{2,1,0:T(8,128)(2,1)S(1)}, bf16[8,64,256]{2,1,0:T(8,128)(2,1)S(1)}, u32[]{:S(2)}, u32[]{:S(2)}) collective-permute-start(bf16[8,64,256]{2,1,0:T(8,128)(2,1)S(1)} %get-tuple-element.97), channel_id=1, source_target_pairs={{0,4},{1,5},{2,6},{3,7},{4,0},{5,1},{6,2},{7,3},{8,12},{9,13},{10,... | collective-permute-start | bytes 786440 | tf_op jit(solution)/shard_map/ppermute | solution.py:42
  53.8 11.0 %collective-permute-start.19 = (bf16[8,64,256]{2,1,0:T(8,128)(2,1)S(1)}, bf16[8,64,256]{2,1,0:T(8,128)(2,1)S(1)}, u32[]{:S(2)}, u32[]{:S(2)}) collective-permute-start(bf16[8,64,256]{2,1,0:T(8,128)(2,1)S(1)} %get-tuple-element.95), channel_id=1, source_target_pairs={{0,64},{16,80},{32,96},{48,112},{64,0},{80,16},{96,32},{112,48},{1... | collective-permute-start | bytes 786440 | tf_op jit(solution)/shard_map/ppermute | solution.py:42
  54.7 14.9 %collective-permute-start.18 = (bf16[8,64,256]{2,1,0:T(8,128)(2,1)S(1)}, bf16[8,64,256]{2,1,0:T(8,128)(2,1)S(1)}, u32[]{:S(2)}, u32[]{:S(2)}) collective-permute-start(bf16[8,64,256]{2,1,0:T(8,128)(2,1)S(1)} %get-tuple-element.92), channel_id=1, source_target_pairs={{0,4},{1,5},{2,6},{3,7},{4,0},{5,1},{6,2},{7,3},{8,12},{9,13},{10,... | collective-permute-start | bytes 786440 | tf_op jit(solution)/shard_map/ppermute | solution.py:42
  59.5 9.3 %collective-permute-start.9 = (bf16[4,64,256]{2,1,0:T(8,128)(2,1)S(1)}, bf16[4,64,256]{2,1,0:T(8,128)(2,1)S(1)}, u32[]{:S(2)}, u32[]{:S(2)}) collective-permute-start(bf16[4,64,256]{2,1,0:T(8,128)(2,1)S(1)} %get-tuple-element.77), channel_id=1, source_target_pairs={{0,32},{16,48},{32,0},{48,16},{64,96},{80,112},{96,64},{112,80},{1... | collective-permute-start | bytes 393224 | tf_op jit(solution)/shard_map/ppermute | solution.py:42
  63.0 10.9 %collective-permute-start.10 = (bf16[4,64,256]{2,1,0:T(8,128)(2,1)S(1)}, bf16[4,64,256]{2,1,0:T(8,128)(2,1)S(1)}, u32[]{:S(2)}, u32[]{:S(2)}) collective-permute-start(bf16[4,64,256]{2,1,0:T(8,128)(2,1)S(1)} %get-tuple-element.78), channel_id=1, source_target_pairs={{0,2},{1,3},{2,0},{3,1},{4,6},{5,7},{6,4},{7,5},{8,10},{9,11},{10,... | collective-permute-start | bytes 393224 | tf_op jit(solution)/shard_map/ppermute | solution.py:42
  63.0 10.9 %collective-permute-start.11 = (bf16[4,64,256]{2,1,0:T(8,128)(2,1)S(1)}, bf16[4,64,256]{2,1,0:T(8,128)(2,1)S(1)}, u32[]{:S(2)}, u32[]{:S(2)}) collective-permute-start(bf16[4,64,256]{2,1,0:T(8,128)(2,1)S(1)} %get-tuple-element.79), channel_id=1, source_target_pairs={{0,34},{1,35},{2,32},{3,33},{4,38},{5,39},{6,36},{7,37},{8,42},{9,... | collective-permute-start | bytes 393224 | tf_op jit(solution)/shard_map/ppermute | solution.py:48
  64.8 19.2 %collective-permute-start.26 = (bf16[8,64,256]{2,1,0:T(8,128)(2,1)S(1)}, bf16[8,64,256]{2,1,0:T(8,128)(2,1)S(1)}, u32[]{:S(2)}, u32[]{:S(2)}) collective-permute-start(bf16[8,64,256]{2,1,0:T(8,128)(2,1)S(1)} %relay_2.1.refs_3_), channel_id=1, source_target_pairs={{0,64},{16,80},{32,96},{48,112},{64,0},{80,16},{96,32},{112,48},{1... | collective-permute-start | bytes 786440 | tf_op jit(solution)/shard_map/ppermute | solution.py:42
  68.7 17.0 %collective-permute-start.25 = (bf16[8,64,256]{2,1,0:T(8,128)(2,1)S(1)}, bf16[8,64,256]{2,1,0:T(8,128)(2,1)S(1)}, u32[]{:S(2)}, u32[]{:S(2)}) collective-permute-start(bf16[8,64,256]{2,1,0:T(8,128)(2,1)S(1)} %get-tuple-element.104), channel_id=1, source_target_pairs={{0,4},{1,5},{2,6},{3,7},{4,0},{5,1},{6,2},{7,3},{8,12},{9,13},{10,... | collective-permute-start | bytes 786440 | tf_op jit(solution)/shard_map/ppermute | solution.py:42
  69.6 10.2 %collective-permute-start.24 = (bf16[4,128,128]{2,1,0:T(8,128)(2,1)S(1)}, bf16[4,128,128]{2,1,0:T(8,128)(2,1)S(1)}, u32[]{:S(2)}, u32[]{:S(2)}) collective-permute-start(bf16[4,128,128]{2,1,0:T(8,128)(2,1)S(1)} %get-tuple-element.103), channel_id=1, source_target_pairs={{0,4},{1,5},{2,6},{3,7},{4,0},{5,1},{6,2},{7,3},{8,12},{9,13},{10,... | collective-permute-start | bytes 393224 | tf_op jit(solution)/shard_map/ppermute | solution.py:42
  74.9 12.3 %collective-permute-start.21 = (bf16[4,64,256]{2,1,0:T(8,128)(2,1)S(1)}, bf16[4,64,256]{2,1,0:T(8,128)(2,1)S(1)}, u32[]{:S(2)}, u32[]{:S(2)}) collective-permute-start(bf16[4,64,256]{2,1,0:T(8,128)(2,1)S(1)} %get-tuple-element.100), channel_id=1, source_target_pairs={{0,64},{16,80},{32,96},{48,112},{64,0},{80,16},{96,32},{112,48},{1... | collective-permute-start | bytes 393224 | tf_op jit(solution)/shard_map/ppermute | solution.py:42
  78.2 9.1 %collective-permute-start.22 = (bf16[4,64,256]{2,1,0:T(8,128)(2,1)S(1)}, bf16[4,64,256]{2,1,0:T(8,128)(2,1)S(1)}, u32[]{:S(2)}, u32[]{:S(2)}) collective-permute-start(bf16[4,64,256]{2,1,0:T(8,128)(2,1)S(1)} %get-tuple-element.101), channel_id=1, source_target_pairs={{0,4},{1,5},{2,6},{3,7},{4,0},{5,1},{6,2},{7,3},{8,12},{9,13},{10,... | collective-permute-start | bytes 393224 | tf_op jit(solution)/shard_map/ppermute | solution.py:42
  79.8 8.3 %collective-permute-start.23 = (bf16[4,64,256]{2,1,0:T(8,128)(2,1)S(1)}, bf16[4,64,256]{2,1,0:T(8,128)(2,1)S(1)}, u32[]{:S(2)}, u32[]{:S(2)}) collective-permute-start(bf16[4,64,256]{2,1,0:T(8,128)(2,1)S(1)} %get-tuple-element.102), channel_id=1, source_target_pairs={{0,68},{1,69},{2,70},{3,71},{4,64},{5,65},{6,66},{7,67},{8,76},{9,... | collective-permute-start | bytes 393224 | tf_op jit(solution)/shard_map/ppermute | solution.py:48

commit v3 on v2

--- a/solution.py
+++ b/solution.py
@@ -8,9 +8,9 @@
 SECTIONS = 3
 LOCAL = 4
 SIZES = (256, 256, 256, 256)
-FLOWS = ("rrc", "rcc", "rcr", "rpp")
+FLOWS = ("rcp", "rpc", "rpp", "rpp")
 LATER, COMBINE = -1, -2
-ORDER = (0, LATER, 3, COMBINE, 1, 2, 0, 1, 0, 2, 1, 3, 2, 1, 0, 2, 1, 2, 0, 1, 3, 2, 0, 3)
+ORDER = (0, LATER, 2, COMBINE, 1, 0, 1, 0, 2, 3, 1, 3, 0, 2, 1, 0, 3, 2, 1, 3)
 LIMIT = 10 * 2**20
 
 VM = pl.BlockSpec(memory_space=pltpu.VMEM)

time: 91.1 us -> 88 us (0.966)
  waiting for transfers between devices: 17.8 us -> 16.5 us
  starting transfers between devices: 52.2 us -> 51.1 us
    ppermute x25, starting transfers between devices: 46.3 us -> 37.5 us  [swapped(): lax.ppermute(piece, axis, [(i, i ^ 1 << section) for i in range(size)])]
    ppermute x2 -> x6, starting transfers between devices: 5.95 us -> 13.6 us  [swapped_both(): return lax.ppermute(piece, ('row', 'col'), pairs)]
    ppermute x25, waiting for transfers between devices: 17 us -> 10.8 us  [swapped(): lax.ppermute(piece, axis, [(i, i ^ 1 << section) for i in range(size)])]
    ppermute x2 -> x6, waiting for transfers between devices: 0.84 us -> 5.69 us  [swapped_both(): return lax.ppermute(piece, ('row', 'col'), pairs)]
    pallas_call x25 -> x21, Pallas kernels: 19.5 us -> 19.3 us  [call(): pl.pallas_call(body, out_shape=tuple(out_shape), in_specs=specs, out_spec...]
  transfers between devices with their start and end apart: 27 -> 31, of which waited for: 10 -> 10; matrix products, arithmetic and copies ran while one was open for 0% -> 0% of each run, Pallas kernels for 17% -> 17%
where the time goes in v3:
time: 88 us; the launch traced here: 87.4 us
  starting transfers between devices  51.1 us (58%)
  Pallas kernels  19.3 us (22%)
  waiting for transfers between devices  16.5 us (19%)
    ppermute x25, starting transfers between devices, swapped(): lax.ppermute(piece, axis, [(i, i ^ 1 << section) for i in range(size)])  37.5 us
    pallas_call x21, Pallas kernels, call(): pl.pallas_call(body, out_shape=tuple(out_shape), in_specs=specs, out_spec...  19.3 us
    ppermute x6, starting transfers between devices, swapped_both(): return lax.ppermute(piece, ('row', 'col'), pairs)  13.6 us
    ppermute x25, waiting for transfers between devices, swapped(): lax.ppermute(piece, axis, [(i, i ^ 1 << section) for i in range(size)])  10.8 us
    ppermute x6, waiting for transfers between devices, swapped_both(): return lax.ppermute(piece, ('row', 'col'), pairs)  5.69 us
  transfers between devices with their start and end apart: 31, of which 10 were waited for; matrix products, arithmetic and copies ran while one was open for 0% of the time, Pallas kernels for 17%

profile of v3, /device:TPU:6, one launch (start us, length us, event | category | flops | bytes accessed | tf_op | source)
XLA Modules:
  0.0 87.4 jit_solution(11799370879187617676)
XLA Ops:
  0.0 1.8 %take_first.1 = (bf16[16,64,1024]{2,1,0:T(8,128)(2,1)S(1)}, bf16[4,64,256]{2,1,0:T(8,128)(2,1)S(1)}, bf16[4,64,256]{2,1,0:T(8,128)(2,1)S(1)}, bf16[8,64,256]{2,1,0:T(8,128)(2,1)S(1)}) custom-call(s32[1,16]{1,0:T(1,128)} %bitcast.33, bf16[16,64,1024]{2,1,0:T(8,128)(2,1)} %bitcast.32), custom_call_target="tpu_custom_call" | custom-call | flops 1 | bytes 1 | tf_op jit(solution)/shard_map/take_first/pallas_call | solution.py:67
  1.8 0.1 collective-permute-start
  1.9 1.5 %collective-permute-done.refs_1_ = bf16[8,64,256]{2,1,0:T(8,128)(2,1)S(1)} collective-permute-done((bf16[8,64,256]{2,1,0:T(8,128)(2,1)S(1)}, bf16[8,64,256]{2,1,0:T(8,128)(2,1)S(1)}, u32[]{:S(2)}, u32[]{:S(2)}) %collective-permute-start) | collective-permute-done | bytes 262176 | tf_op jit(solution)/shard_map/ppermute | solution.py:42
  3.5 0.0 copy-start
  3.5 1.0 %take_later.1 = (bf16[4,128,128]{2,1,0:T(8,128)(2,1)S(1)}, bf16[4,128,128]{2,1,0:T(8,128)(2,1)S(1)}, bf16[4,128,128]{2,1,0:T(8,128)(2,1)S(1)}, bf16[8,64,768]{2,...) custom-call(s32[1,16]{1,0:T(1,128)} %bitcast.34, ...), custom_call_target="tpu_custom_call" | custom-call | flops 1 | bytes 1 | tf_op jit(solution)/shard_map/take_later/pallas_call | solution.py:67
  4.5 0.2 collective-permute-start.1
  4.7 1.4 %collective-permute-start.4 = (bf16[8,64,256]{2,1,0:T(8,128)(2,1)S(1)}, bf16[8,64,256]{2,1,0:T(8,128)(2,1)S(1)}, u32[]{:S(2)}, u32[]{:S(2)}) collective-permute-start(bf16[8,64,256]{2,1,0:T(8,128)(2,1)S(1)} %relay_0.4.refs_3_), channel_id=1, source_target_pairs={{0,16},{16,0},{32,48},{48,32},{64,80},{80,64},{96,112},{112,96},{1... | collective-permute-start | bytes 786440 | tf_op jit(solution)/shard_map/ppermute | solution.py:42
  6.1 0.1 collective-permute-start.3
  6.2 0.6 collective-permute-done.1.refs_1_
  6.9 1.0 %combine.1 = (bf16[4,256,256]{2,1,0:T(8,128)(2,1)S(1)}, bf16[4,256,256]{2,1,0:T(8,128)(2,1)S(1)}, bf16[4,256,256]{2,1,0:T(8,128)(2,1)S(1)}, bf16[4,256,256]{2,1,...) custom-call(bf16[6,8,128,128]{3,2,1,0:T(8,128)(2,1)S(1)} %bitcast.19, ...), custom_call_target="tpu_custom_call" | custom-call | flops 1 | bytes 1 | tf_op jit(solution)/shard_map/combine/pallas_call | solution.py:67
  8.0 1.6 %collective-permute-start.6 = (bf16[8,64,256]{2,1,0:T(8,128)(2,1)S(1)}, bf16[8,64,256]{2,1,0:T(8,128)(2,1)S(1)}, u32[]{:S(2)}, u32[]{:S(2)}) collective-permute-start(bf16[8,64,256]{2,1,0:T(8,128)(2,1)S(1)} %relay_0.6.refs_8_), channel_id=1, source_target_pairs={{0,16},{16,0},{32,48},{48,32},{64,80},{80,64},{96,112},{112,96},{1... | collective-permute-start | bytes 786440 | tf_op jit(solution)/shard_map/ppermute | solution.py:42
  9.5 0.0 collective-permute-done.3.refs_7_
  9.5 5.8 %collective-permute-done.4.refs_2_ = bf16[8,64,256]{2,1,0:T(8,128)(2,1)S(1)} collective-permute-done((bf16[8,64,256]{2,1,0:T(8,128)(2,1)S(1)}, bf16[8,64,256]{2,1,0:T(8,128)(2,1)S(1)}, u32[]{:S(2)}, u32[]{:S(2)}) %collective-permute-start.4) | collective-permute-done | bytes 262176 | tf_op jit(solution)/shard_map/ppermute | solution.py:42
  15.3 1.0 %end_0.4 = (bf16[8,64,256]{2,1,0:T(8,128)(2,1)S(1)}, bf16[8,64,256]{2,1,0:T(8,128)(2,1)S(1)}) custom-call(bf16[4,64,256]{2,1,0:T(8,128)(2,1)S(1)} %get-tuple-element.60.refs_2_.refs_0_, bf16[8,64,256]{2,1,0:T(8,128)(2,1)S(1)} %collective-permute-done.refs_1_, bf16[8,64,256]{2,1,0:T(8,128)(2,1)S(1)} %collective-permute-done.4.refs_2_, ...), custom_call_target="tpu_custom_call" | custom-call | flops 1 | bytes 1 | tf_op jit(solution)/shard_map/end_0/pallas_call | solution.py:67
  16.4 2.0 %collective-permute-start.5 = (bf16[8,64,256]{2,1,0:T(8,128)(2,1)S(1)}, bf16[8,64,256]{2,1,0:T(8,128)(2,1)S(1)}, u32[]{:S(2)}, u32[]{:S(2)}) collective-permute-start(bf16[8,64,256]{2,1,0:T(8,128)(2,1)S(1)} %get-tuple-element.71), channel_id=1, source_target_pairs={{0,32},{16,48},{32,0},{48,16},{64,96},{80,112},{96,64},{112,80},{1... | collective-permute-start | bytes 786440 | tf_op jit(solution)/shard_map/ppermute | solution.py:42
  18.4 1.4 %collective-permute-start.2 = (bf16[8,64,256]{2,1,0:T(8,128)(2,1)S(1)}, bf16[8,64,256]{2,1,0:T(8,128)(2,1)S(1)}, u32[]{:S(2)}, u32[]{:S(2)}) collective-permute-start(bf16[8,64,256]{2,1,0:T(8,128)(2,1)S(1)} %relay_0.5.refs_2_), channel_id=1, source_target_pairs={{0,16},{16,0},{32,48},{48,32},{64,80},{80,64},{96,112},{112,96},{1... | collective-permute-start | bytes 786440 | tf_op jit(solution)/shard_map/ppermute | solution.py:42
  19.8 1.6 %collective-permute-start.11 = (bf16[4,128,128]{2,1,0:T(8,128)(2,1)S(1)}, bf16[4,128,128]{2,1,0:T(8,128)(2,1)S(1)}, u32[]{:S(2)}, u32[]{:S(2)}) collective-permute-start(bf16[4,128,128]{2,1,0:T(8,128)(2,1)S(1)} %get-tuple-element.81), channel_id=1, source_target_pairs={{0,2},{1,3},{2,0},{3,1},{4,6},{5,7},{6,4},{7,5},{8,10},{9,11},{10,... | collective-permute-start | bytes 393224 | tf_op jit(solution)/shard_map/ppermute | solution.py:42
  21.4 0.0 collective-permute-done.6.refs_2_
  21.4 1.0 %end_0.5 = (bf16[4,64,256]{2,1,0:T(8,128)(2,1)S(1)}, bf16[4,64,256]{2,1,0:T(8,128)(2,1)S(1)}, bf16[4,64,256]{2,1,0:T(8,128)(2,1)S(1)}, bf16[4,64,256]{2,1,0:T(8,128)(2,1)S(1)}) custom-call(bf16[4,64,256]{2,1,0:T(8,128)(2,1)S(1)} %get-tuple-element.72.refs_0_, bf16[8,64,768]{2,1,0:T(8,128)(2,1)S(1)} %collective-permute-done.1.refs_1_, ...), custom_call_target="tpu_custom_call" | custom-call | flops 1 | bytes 1 | tf_op jit(solution)/shard_map/end_0/pallas_call | solution.py:67
  22.4 1.6 %collective-permute-start.8 = (bf16[4,64,256]{2,1,0:T(8,128)(2,1)S(1)}, bf16[4,64,256]{2,1,0:T(8,128)(2,1)S(1)}, u32[]{:S(2)}, u32[]{:S(2)}) collective-permute-start(bf16[4,64,256]{2,1,0:T(8,128)(2,1)S(1)} %get-tuple-element.76), channel_id=1, source_target_pairs={{0,32},{16,48},{32,0},{48,16},{64,96},{80,112},{96,64},{112,80},{1... | collective-permute-start | bytes 393224 | tf_op jit(solution)/shard_map/ppermute | solution.py:42
  24.0 1.6 %collective-permute-start.9 = (bf16[4,64,256]{2,1,0:T(8,128)(2,1)S(1)}, bf16[4,64,256]{2,1,0:T(8,128)(2,1)S(1)}, u32[]{:S(2)}, u32[]{:S(2)}) collective-permute-start(bf16[4,64,256]{2,1,0:T(8,128)(2,1)S(1)} %get-tuple-element.77), channel_id=1, source_target_pairs={{0,2},{1,3},{2,0},{3,1},{4,6},{5,7},{6,4},{7,5},{8,10},{9,11},{10,... | collective-permute-start | bytes 393224 | tf_op jit(solution)/shard_map/ppermute | solution.py:42
  25.6 0.0 collective-permute-done.5.refs_1_
  25.6 1.0 %collective-permute-start.10 = (bf16[4,64,256]{2,1,0:T(8,128)(2,1)S(1)}, bf16[4,64,256]{2,1,0:T(8,128)(2,1)S(1)}, u32[]{:S(2)}, u32[]{:S(2)}) collective-permute-start(bf16[4,64,256]{2,1,0:T(8,128)(2,1)S(1)} %get-tuple-element.78), channel_id=1, source_target_pairs={{0,34},{1,35},{2,32},{3,33},{4,38},{5,39},{6,36},{7,37},{8,42},{9,... | collective-permute-start | bytes 393224 | tf_op jit(solution)/shard_map/ppermute | solution.py:48
  26.6 0.3 row_1.1
  26.9 0.0 collective-permute-done.2.refs_2_
  26.9 1.1 %end_0.6 = (bf16[4,64,256]{2,1,0:T(8,128)(2,1)S(1)}, bf16[4,64,256]{2,1,0:T(8,128)(2,1)S(1)}, bf16[4,64,256]{2,1,0:T(8,128)(2,1)S(1)}, bf16[4,64,256]{2,1,0:T(8,128)(2,1)S(1)}) custom-call(bf16[4,64,256]{2,1,0:T(8,128)(2,1)S(1)} %get-tuple-element.64.refs_0_, bf16[8,64,768]{2,1,0:T(8,128)(2,1)S(1)} %collective-permute-done.1.refs_1_, ...), custom_call_target="tpu_custom_call" | custom-call | flops 1 | bytes 1 | tf_op jit(solution)/shard_map/end_0/pallas_call | solution.py:67
  28.0 1.6 %collective-permute-start.7 = (bf16[8,64,256]{2,1,0:T(8,128)(2,1)S(1)}, bf16[8,64,256]{2,1,0:T(8,128)(2,1)S(1)}, u32[]{:S(2)}, u32[]{:S(2)}) collective-permute-start(bf16[8,64,256]{2,1,0:T(8,128)(2,1)S(1)} %relay_0.7.refs_9_), channel_id=1, source_target_pairs={{0,16},{16,0},{32,48},{48,32},{64,80},{80,64},{96,112},{112,96},{1... | collective-permute-start | bytes 786440 | tf_op jit(solution)/shard_map/ppermute | solution.py:42
  29.6 0.0 collective-permute-done.11.refs_8_
  29.6 1.4 %collective-permute-start.15 = (bf16[8,64,256]{2,1,0:T(8,128)(2,1)S(1)}, bf16[8,64,256]{2,1,0:T(8,128)(2,1)S(1)}, u32[]{:S(2)}, u32[]{:S(2)}) collective-permute-start(bf16[8,64,256]{2,1,0:T(8,128)(2,1)S(1)} %get-tuple-element.87), channel_id=1, source_target_pairs={{0,2},{1,3},{2,0},{3,1},{4,6},{5,7},{6,4},{7,5},{8,10},{9,11},{10,... | collective-permute-start | bytes 786440 | tf_op jit(solution)/shard_map/ppermute | solution.py:42
  31.0 0.0 collective-permute-done.8.refs_1_
  31.0 1.4 %collective-permute-done.9.refs_2_ = bf16[4,64,256]{2,1,0:T(8,128)(2,1)S(1)} collective-permute-done((bf16[4,64,256]{2,1,0:T(8,128)(2,1)S(1)}, bf16[4,64,256]{2,1,0:T(8,128)(2,1)S(1)}, u32[]{:S(2)}, u32[]{:S(2)}) %collective-permute-start.9) | collective-permute-done | bytes 131104 | tf_op jit(solution)/shard_map/ppermute | solution.py:42
  32.4 1.1 %end_1.4 = (bf16[8,64,256]{2,1,0:T(8,128)(2,1)S(1)}, bf16[8,64,256]{2,1,0:T(8,128)(2,1)S(1)}) custom-call(bf16[4,64,256]{2,1,0:T(8,128)(2,1)S(1)} %get-tuple-element.73.refs_3_.refs_0_, bf16[4,64,256]{2,1,0:T(8,128)(2,1)S(1)} %collective-permute-done.8.refs_1_, bf16[4,64,256]{2,1,0:T(8,128)(2,1)S(1)} %collective-permute-done.9.refs_2_, ...), custom_call_target="tpu_custom_call" | custom-call | flops 1 | bytes 1 | tf_op jit(solution)/shard_map/end_1/pallas_call | solution.py:67
  33.5 3.4 %collective-permute-start.20 = (bf16[8,64,256]{2,1,0:T(8,128)(2,1)S(1)}, bf16[8,64,256]{2,1,0:T(8,128)(2,1)S(1)}, u32[]{:S(2)}, u32[]{:S(2)}) collective-permute-start(bf16[8,64,256]{2,1,0:T(8,128)(2,1)S(1)} %get-tuple-element.95), channel_id=1, source_target_pairs={{0,64},{16,80},{32,96},{48,112},{64,0},{80,16},{96,32},{112,48},{1... | collective-permute-start | bytes 786440 | tf_op jit(solution)/shard_map/ppermute | solution.py:42
  36.8 0.0 collective-permute-start.21
  36.8 1.0 %collective-permute-start.22 = (bf16[4,64,256]{2,1,0:T(8,128)(2,1)S(1)}, bf16[4,64,256]{2,1,0:T(8,128)(2,1)S(1)}, u32[]{:S(2)}, u32[]{:S(2)}) collective-permute-start(bf16[4,64,256]{2,1,0:T(8,128)(2,1)S(1)} %get-tuple-element.97), channel_id=1, source_target_pairs={{0,2},{1,3},{2,0},{3,1},{4,6},{5,7},{6,4},{7,5},{8,10},{9,11},{10,... | collective-permute-start | bytes 393224 | tf_op jit(solution)/shard_map/ppermute | solution.py:42
  37.9 2.5 %collective-permute-start.23 = (bf16[4,64,256]{2,1,0:T(8,128)(2,1)S(1)}, bf16[4,64,256]{2,1,0:T(8,128)(2,1)S(1)}, u32[]{:S(2)}, u32[]{:S(2)}) collective-permute-start(bf16[4,64,256]{2,1,0:T(8,128)(2,1)S(1)} %get-tuple-element.98), channel_id=1, source_target_pairs={{0,34},{1,35},{2,32},{3,33},{4,38},{5,39},{6,36},{7,37},{8,42},{9,... | collective-permute-start | bytes 393224 | tf_op jit(solution)/shard_map/ppermute | solution.py:48
  40.3 1.0 %end_0.7 = (bf16[4,64,256]{2,1,0:T(8,128)(2,1)S(1)}, bf16[4,64,256]{2,1,0:T(8,128)(2,1)S(1)}, bf16[4,64,256]{2,1,0:T(8,128)(2,1)S(1)}, bf16[4,64,256]{2,1,0:T(8,128)(2,1)S(1)}) custom-call(bf16[4,64,256]{2,1,0:T(8,128)(2,1)S(1)} %get-tuple-element.61.refs_0_, bf16[8,64,768]{2,1,0:T(8,128)(2,1)S(1)} %collective-permute-done.1.refs_1_, ...), custom_call_target="tpu_custom_call" | custom-call | flops 1 | bytes 1 | tf_op jit(solution)/shard_map/end_0/pallas_call | solution.py:67
  41.4 3.1 %collective-permute-start.19 = (bf16[4,128,128]{2,1,0:T(8,128)(2,1)S(1)}, bf16[4,128,128]{2,1,0:T(8,128)(2,1)S(1)}, u32[]{:S(2)}, u32[]{:S(2)}) collective-permute-start(bf16[4,128,128]{2,1,0:T(8,128)(2,1)S(1)} %get-tuple-element.94), channel_id=1, source_target_pairs={{0,4},{1,5},{2,6},{3,7},{4,0},{5,1},{6,2},{7,3},{8,12},{9,13},{10,... | collective-permute-start | bytes 393224 | tf_op jit(solution)/shard_map/ppermute | solution.py:42
  44.5 0.8 end_1.5
  45.3 0.1 collective-permute-done.21.refs_1_
  45.5 2.5 %collective-permute-start.12 = (bf16[4,64,256]{2,1,0:T(8,128)(2,1)S(1)}, bf16[4,64,256]{2,1,0:T(8,128)(2,1)S(1)}, u32[]{:S(2)}, u32[]{:S(2)}) collective-permute-start(bf16[4,64,256]{2,1,0:T(8,128)(2,1)S(1)} %get-tuple-element.84), channel_id=1, source_target_pairs={{0,32},{16,48},{32,0},{48,16},{64,96},{80,112},{96,64},{112,80},{1... | collective-permute-start | bytes 393224 | tf_op jit(solution)/shard_map/ppermute | solution.py:42
  47.9 2.5 %collective-permute-done.23.refs_3_ = bf16[4,64,256]{2,1,0:T(8,128)(2,1)S(1)} collective-permute-done((bf16[4,64,256]{2,1,0:T(8,128)(2,1)S(1)}, bf16[4,64,256]{2,1,0:T(8,128)(2,1)S(1)}, u32[]{:S(2)}, u32[]{:S(2)}) %collective-permute-start.23) | collective-permute-done | bytes 131104 | tf_op jit(solution)/shard_map/ppermute | solution.py:48
  50.4 3.8 %collective-permute-start.17 = (bf16[4,64,256]{2,1,0:T(8,128)(2,1)S(1)}, bf16[4,64,256]{2,1,0:T(8,128)(2,1)S(1)}, u32[]{:S(2)}, u32[]{:S(2)}) collective-permute-start(bf16[4,64,256]{2,1,0:T(8,128)(2,1)S(1)} %get-tuple-element.90), channel_id=1, source_target_pairs={{0,4},{1,5},{2,6},{3,7},{4,0},{5,1},{6,2},{7,3},{8,12},{9,13},{10,... | collective-permute-start | bytes 393224 | tf_op jit(solution)/shard_map/ppermute | solution.py:42
  54.3 0.1 collective-permute-start.18
  54.4 1.0 %end_1.6 = (bf16[4,64,256]{2,1,0:T(8,128)(2,1)S(1)}, bf16[4,64,256]{2,1,0:T(8,128)(2,1)S(1)}, bf16[4,64,256]{2,1,0:T(8,128)(2,1)S(1)}, bf16[4,64,256]{2,1,0:T(8,128)(2,1)S(1)}) custom-call(bf16[4,64,256]{2,1,0:T(8,128)(2,1)S(1)} %get-tuple-element.75.refs_2_.refs_0_, bf16[4,64,256]{2,1,0:T(8,128)(2,1)S(1)} %collective-permute-done.21.refs_1_, ...), custom_call_target="tpu_custom_call" | custom-call | flops 1 | bytes 1 | tf_op jit(solution)/shard_map/end_1/pallas_call | solution.py:67
  55.4 0.3 row_2.1
  55.7 1.2 %collective-permute-start.13 = (bf16[4,64,256]{2,1,0:T(8,128)(2,1)S(1)}, bf16[4,64,256]{2,1,0:T(8,128)(2,1)S(1)}, u32[]{:S(2)}, u32[]{:S(2)}) collective-permute-start(bf16[4,64,256]{2,1,0:T(8,128)(2,1)S(1)} %get-tuple-element.85), channel_id=1, source_target_pairs={{0,2},{1,3},{2,0},{3,1},{4,6},{5,7},{6,4},{7,5},{8,10},{9,11},{10,... | collective-permute-start | bytes 393224 | tf_op jit(solution)/shard_map/ppermute | solution.py:42
  56.9 1.5 %collective-permute-start.14 = (bf16[4,64,256]{2,1,0:T(8,128)(2,1)S(1)}, bf16[4,64,256]{2,1,0:T(8,128)(2,1)S(1)}, u32[]{:S(2)}, u32[]{:S(2)}) collective-permute-start(bf16[4,64,256]{2,1,0:T(8,128)(2,1)S(1)} %get-tuple-element.86), channel_id=1, source_target_pairs={{0,34},{1,35},{2,32},{3,33},{4,38},{5,39},{6,36},{7,37},{8,42},{9,... | collective-permute-start | bytes 393224 | tf_op jit(solution)/shard_map/ppermute | solution.py:48
  58.5 1.3 %collective-permute-done.16.refs_1_ = bf16[4,64,256]{2,1,0:T(8,128)(2,1)S(1)} collective-permute-done((bf16[4,64,256]{2,1,0:T(8,128)(2,1)S(1)}, bf16[4,64,256]{2,1,0:T(8,128)(2,1)S(1)}, u32[]{:S(2)}, u32[]{:S(2)}) %collective-permute-start.16) | collective-permute-done | bytes 131104 | tf_op jit(solution)/shard_map/ppermute | solution.py:42
  59.7 0.0 collective-permute-start.28
  59.8 3.6 %collective-permute-start.27 = (bf16[8,64,256]{2,1,0:T(8,128)(2,1)S(1)}, bf16[8,64,256]{2,1,0:T(8,128)(2,1)S(1)}, u32[]{:S(2)}, u32[]{:S(2)}) collective-permute-start(bf16[8,64,256]{2,1,0:T(8,128)(2,1)S(1)} %get-tuple-element.105), channel_id=1, source_target_pairs={{0,4},{1,5},{2,6},{3,7},{4,0},{5,1},{6,2},{7,3},{8,12},{9,13},{10,... | collective-permute-start | bytes 786440 | tf_op jit(solution)/shard_map/ppermute | solution.py:42
  63.3 1.1 %collective-permute-done.18.refs_3_ = bf16[4,64,256]{2,1,0:T(8,128)(2,1)S(1)} collective-permute-done((bf16[4,64,256]{2,1,0:T(8,128)(2,1)S(1)}, bf16[4,64,256]{2,1,0:T(8,128)(2,1)S(1)}, u32[]{:S(2)}, u32[]{:S(2)}) %collective-permute-start.18) | collective-permute-done | bytes 131104 | tf_op jit(solution)/shard_map/ppermute | solution.py:48
  64.4 0.9 %collective-permute-start.29 = (bf16[4,64,256]{2,1,0:T(8,128)(2,1)S(1)}, bf16[4,64,256]{2,1,0:T(8,128)(2,1)S(1)}, u32[]{:S(2)}, u32[]{:S(2)}) collective-permute-start(bf16[4,64,256]{2,1,0:T(8,128)(2,1)S(1)} %get-tuple-element.107), channel_id=1, source_target_pairs={{0,4},{1,5},{2,6},{3,7},{4,0},{5,1},{6,2},{7,3},{8,12},{9,13},{10,... | collective-permute-start | bytes 393224 | tf_op jit(solution)/shard_map/ppermute | solution.py:42
  65.4 1.7 %end_2.4.refs_9_ = bf16[16,64,1024]{2,1,0:T(8,128)(2,1)} custom-call(bf16[4,64,256]{2,1,0:T(8,128)(2,1)S(1)} %get-tuple-element.88.refs_9_.refs_0_, bf16[4,64,256]{2,1,0:T(8,128)(2,1)S(1)} %collective-permute-done.16.refs_1_, bf16[4,64,256]{2,1,0:T(8,128)(2,1)S(1)} %collective-permute-done.17.refs_2_, ...), custom_call_target="tpu_custom_call" | custom-call | flops 1 | bytes 1 | tf_op jit(solution)/shard_map/end_2/pallas_call | solution.py:67
  67.1 2.8 %collective-permute-start.30 = (bf16[4,64,256]{2,1,0:T(8,128)(2,1)S(1)}, bf16[4,64,256]{2,1,0:T(8,128)(2,1)S(1)}, u32[]{:S(2)}, u32[]{:S(2)}) collective-permute-start(bf16[4,64,256]{2,1,0:T(8,128)(2,1)S(1)} %get-tuple-element.108), channel_id=1, source_target_pairs={{0,68},{1,69},{2,70},{3,71},{4,64},{5,65},{6,66},{7,67},{8,76},{9,... | collective-permute-start | bytes 393224 | tf_op jit(solution)/shard_map/ppermute | solution.py:48
  69.9 1.0 %end_1.7 = (bf16[4,64,256]{2,1,0:T(8,128)(2,1)S(1)}, bf16[4,64,256]{2,1,0:T(8,128)(2,1)S(1)}, bf16[4,64,256]{2,1,0:T(8,128)(2,1)S(1)}, bf16[4,64,256]{2,1,0:T(8,128)(2,1)S(1)}) custom-call(bf16[4,64,256]{2,1,0:T(8,128)(2,1)S(1)} %get-tuple-element.83.refs_5_.refs_0_, bf16[4,64,256]{2,1,0:T(8,128)(2,1)S(1)} %collective-permute-done.12.refs_1_, ...), custom_call_target="tpu_custom_call" | custom-call | flops 1 | bytes 1 | tf_op jit(solution)/shard_map/end_1/pallas_call | solution.py:67
  70.9 2.6 %collective-permute-start.24 = (bf16[4,64,256]{2,1,0:T(8,128)(2,1)S(1)}, bf16[4,64,256]{2,1,0:T(8,128)(2,1)S(1)}, u32[]{:S(2)}, u32[]{:S(2)}) collective-permute-start(bf16[4,64,256]{2,1,0:T(8,128)(2,1)S(1)} %get-tuple-element.102), channel_id=1, source_target_pairs={{0,64},{16,80},{32,96},{48,112},{64,0},{80,16},{96,32},{112,48},{1... | collective-permute-start | bytes 393224 | tf_op jit(solution)/shard_map/ppermute | solution.py:42
  73.5 0.9 %collective-permute-start.25 = (bf16[4,64,256]{2,1,0:T(8,128)(2,1)S(1)}, bf16[4,64,256]{2,1,0:T(8,128)(2,1)S(1)}, u32[]{:S(2)}, u32[]{:S(2)}) collective-permute-start(bf16[4,64,256]{2,1,0:T(8,128)(2,1)S(1)} %get-tuple-element.103), channel_id=1, source_target_pairs={{0,4},{1,5},{2,6},{3,7},{4,0},{5,1},{6,2},{7,3},{8,12},{9,13},{10,... | collective-permute-start | bytes 393224 | tf_op jit(solution)/shard_map/ppermute | solution.py:42
  74.4 5.7 %collective-permute-start.26 = (bf16[4,64,256]{2,1,0:T(8,128)(2,1)S(1)}, bf16[4,64,256]{2,1,0:T(8,128)(2,1)S(1)}, u32[]{:S(2)}, u32[]{:S(2)}) collective-permute-start(bf16[4,64,256]{2,1,0:T(8,128)(2,1)S(1)} %get-tuple-element.104), channel_id=1, source_target_pairs={{0,68},{1,69},{2,70},{3,71},{4,64},{5,65},{6,66},{7,67},{8,76},{9,... | collective-permute-start | bytes 393224 | tf_op jit(solution)/shard_map/ppermute | solution.py:48
  80.1 0.8 collective-permute-done.30.refs_3_
  81.0 1.7 %end_2.5.refs_5_ = bf16[16,64,1024]{2,1,0:T(8,128)(2,1)} custom-call(bf16[4,64,256]{2,1,0:T(8,128)(2,1)S(1)} %get-tuple-element.99.refs_3_.refs_0_, bf16[4,64,256]{2,1,0:T(8,128)(2,1)S(1)} %collective-permute-done.28.refs_1_, bf16[4,64,256]{2,1,0:T(8,128)(2,1)S(1)} %collective-permute-done.29.refs_2_, ...), custom_call_target="tpu_custom_call", output_to_operand_aliasing={{}: (9, {})} | custom-call | flops 1 | bytes 1 | tf_op jit(solution)/shard_map/end_2/pallas_call | solution.py:67
  82.7 1.5 %end_2.6.refs_9_ = bf16[16,64,1024]{2,1,0:T(8,128)(2,1)} custom-call(bf16[8,64,256]{2,1,0:T(8,128)(2,1)S(1)} %get-tuple-element.100.refs_9_.refs_0_, bf16[8,64,256]{2,1,0:T(8,128)(2,1)S(1)} %collective-permute-done.27.refs_1_, bf16[4,256,256]{2,1,0:T(8,128)(2,1)S(1)} %get-tuple-element.92.refs_4_.refs_2_, ...), custom_call_target="tpu_custom_call", output_to_operand_aliasing={{}: (5, {})} | custom-call | flops 1 | bytes 1 | tf_op jit(solution)/shard_map/end_2/pallas_call | solution.py:67
  84.2 1.3 %collective-permute-done.26.refs_3_ = bf16[4,64,256]{2,1,0:T(8,128)(2,1)S(1)} collective-permute-done((bf16[4,64,256]{2,1,0:T(8,128)(2,1)S(1)}, bf16[4,64,256]{2,1,0:T(8,128)(2,1)S(1)}, u32[]{:S(2)}, u32[]{:S(2)}) %collective-permute-start.26) | collective-permute-done | bytes 131104 | tf_op jit(solution)/shard_map/ppermute | solution.py:48
  85.5 1.7 %end_2.7 = bf16[16,64,1024]{2,1,0:T(8,128)(2,1)} custom-call(bf16[4,64,256]{2,1,0:T(8,128)(2,1)S(1)} %get-tuple-element.101.refs_10_.refs_0_, bf16[4,64,256]{2,1,0:T(8,128)(2,1)S(1)} %collective-permute-done.24.refs_1_, bf16[4,64,256]{2,1,0:T(8,128)(2,1)S(1)} %collective-permute-done.25.refs_2_, ...), custom_call_target="tpu_custom_call", output_to_operand_aliasing={{}: (9, {})} | custom-call | flops 1 | bytes 1 | tf_op jit(solution)/shard_map/end_2/pallas_call | solution.py:67
  (23 shorter events, 0.1 us)
Async XLA Ops:
  0.0 3.5 %copy-start.1 = (bf16[6,1,1,8,128,128]{5,4,3,2,1,0:T(8,128)(2,1)S(1)}, bf16[6,1,1,8,128,128]{5,4,3,2,1,0:T(8,128)(2,1)}, u32[]{:S(2)}) copy-start(bf16[6,1,1,8,128,128]{5,4,3,2,1,0:T(8,128)(2,1)} %param.6) | copy-start | bytes 4718596
  1.8 1.6 %collective-permute-start = (bf16[8,64,256]{2,1,0:T(8,128)(2,1)S(1)}, bf16[8,64,256]{2,1,0:T(8,128)(2,1)S(1)}, u32[]{:S(2)}, u32[]{:S(2)}) collective-permute-start(bf16[8,64,256]{2,1,0:T(8,128)(2,1)S(1)} %get-tuple-element.59), channel_id=1, source_target_pairs={{0,1},{1,0},{2,3},{3,2},{4,5},{5,4},{6,7},{7,6},{8,9},{9,8},{10,11... | collective-permute-start | bytes 786440 | tf_op jit(solution)/shard_map/ppermute | solution.py:42
  3.5 3.4 %copy-start = (bf16[12,1,1,8,128,128]{5,4,3,2,1,0:T(8,128)(2,1)S(1)}, bf16[12,1,1,8,128,128]{5,4,3,2,1,0:T(8,128)(2,1)}, u32[]{:S(2)}) copy-start(bf16[12,1,1,8,128,128]{5,4,3,2,1,0:T(8,128)(2,1)} %param.7) | copy-start | bytes 9437188
  4.5 2.4 %collective-permute-start.1 = (bf16[8,64,768]{2,1,0:T(8,128)(2,1)S(1)}, bf16[8,64,768]{2,1,0:T(8,128)(2,1)S(1)}, u32[]{:S(2)}, u32[]{:S(2)}) collective-permute-start(bf16[8,64,768]{2,1,0:T(8,128)(2,1)S(1)} %get-tuple-element.62.refs_2_), channel_id=1, source_target_pairs={{0,1},{1,0},{2,3},{3,2},{4,5},{5,4},{6,7},{7,6},{8,9},{9,8},{10,11... | collective-permute-start | bytes 2359304 | tf_op jit(solution)/shard_map/ppermute | solution.py:42
  4.7 10.6 %collective-permute-start.4 = (bf16[8,64,256]{2,1,0:T(8,128)(2,1)S(1)}, bf16[8,64,256]{2,1,0:T(8,128)(2,1)S(1)}, u32[]{:S(2)}, u32[]{:S(2)}) collective-permute-start(bf16[8,64,256]{2,1,0:T(8,128)(2,1)S(1)} %relay_0.4.refs_3_), channel_id=1, source_target_pairs={{0,16},{16,0},{32,48},{48,32},{64,80},{80,64},{96,112},{112,96},{1... | collective-permute-start | bytes 786440 | tf_op jit(solution)/shard_map/ppermute | solution.py:42
  6.1 3.4 %collective-permute-start.3 = (bf16[4,128,128]{2,1,0:T(8,128)(2,1)S(1)}, bf16[4,128,128]{2,1,0:T(8,128)(2,1)S(1)}, u32[]{:S(2)}, u32[]{:S(2)}) collective-permute-start(bf16[4,128,128]{2,1,0:T(8,128)(2,1)S(1)} %get-tuple-element.68), channel_id=1, source_target_pairs={{0,1},{1,0},{2,3},{3,2},{4,5},{5,4},{6,7},{7,6},{8,9},{9,8},{10,11... | collective-permute-start | bytes 393224 | tf_op jit(solution)/shard_map/ppermute | solution.py:42
  8.0 13.4 %collective-permute-start.6 = (bf16[8,64,256]{2,1,0:T(8,128)(2,1)S(1)}, bf16[8,64,256]{2,1,0:T(8,128)(2,1)S(1)}, u32[]{:S(2)}, u32[]{:S(2)}) collective-permute-start(bf16[8,64,256]{2,1,0:T(8,128)(2,1)S(1)} %relay_0.6.refs_8_), channel_id=1, source_target_pairs={{0,16},{16,0},{32,48},{48,32},{64,80},{80,64},{96,112},{112,96},{1... | collective-permute-start | bytes 786440 | tf_op jit(solution)/shard_map/ppermute | solution.py:42
  16.4 9.2 %collective-permute-start.5 = (bf16[8,64,256]{2,1,0:T(8,128)(2,1)S(1)}, bf16[8,64,256]{2,1,0:T(8,128)(2,1)S(1)}, u32[]{:S(2)}, u32[]{:S(2)}) collective-permute-start(bf16[8,64,256]{2,1,0:T(8,128)(2,1)S(1)} %get-tuple-element.71), channel_id=1, source_target_pairs={{0,32},{16,48},{32,0},{48,16},{64,96},{80,112},{96,64},{112,80},{1... | collective-permute-start | bytes 786440 | tf_op jit(solution)/shard_map/ppermute | solution.py:42
  18.4 8.5 %collective-permute-start.2 = (bf16[8,64,256]{2,1,0:T(8,128)(2,1)S(1)}, bf16[8,64,256]{2,1,0:T(8,128)(2,1)S(1)}, u32[]{:S(2)}, u32[]{:S(2)}) collective-permute-start(bf16[8,64,256]{2,1,0:T(8,128)(2,1)S(1)} %relay_0.5.refs_2_), channel_id=1, source_target_pairs={{0,16},{16,0},{32,48},{48,32},{64,80},{80,64},{96,112},{112,96},{1... | collective-permute-start | bytes 786440 | tf_op jit(solution)/shard_map/ppermute | solution.py:42
  19.8 9.8 %collective-permute-start.11 = (bf16[4,128,128]{2,1,0:T(8,128)(2,1)S(1)}, bf16[4,128,128]{2,1,0:T(8,128)(2,1)S(1)}, u32[]{:S(2)}, u32[]{:S(2)}) collective-permute-start(bf16[4,128,128]{2,1,0:T(8,128)(2,1)S(1)} %get-tuple-element.81), channel_id=1, source_target_pairs={{0,2},{1,3},{2,0},{3,1},{4,6},{5,7},{6,4},{7,5},{8,10},{9,11},{10,... | collective-permute-start | bytes 393224 | tf_op jit(solution)/shard_map/ppermute | solution.py:42
  22.4 8.6 %collective-permute-start.8 = (bf16[4,64,256]{2,1,0:T(8,128)(2,1)S(1)}, bf16[4,64,256]{2,1,0:T(8,128)(2,1)S(1)}, u32[]{:S(2)}, u32[]{:S(2)}) collective-permute-start(bf16[4,64,256]{2,1,0:T(8,128)(2,1)S(1)} %get-tuple-element.76), channel_id=1, source_target_pairs={{0,32},{16,48},{32,0},{48,16},{64,96},{80,112},{96,64},{112,80},{1... | collective-permute-start | bytes 393224 | tf_op jit(solution)/shard_map/ppermute | solution.py:42
  24.0 8.4 %collective-permute-start.9 = (bf16[4,64,256]{2,1,0:T(8,128)(2,1)S(1)}, bf16[4,64,256]{2,1,0:T(8,128)(2,1)S(1)}, u32[]{:S(2)}, u32[]{:S(2)}) collective-permute-start(bf16[4,64,256]{2,1,0:T(8,128)(2,1)S(1)} %get-tuple-element.77), channel_id=1, source_target_pairs={{0,2},{1,3},{2,0},{3,1},{4,6},{5,7},{6,4},{7,5},{8,10},{9,11},{10,... | collective-permute-start | bytes 393224 | tf_op jit(solution)/shard_map/ppermute | solution.py:42
  25.6 6.8 %collective-permute-start.10 = (bf16[4,64,256]{2,1,0:T(8,128)(2,1)S(1)}, bf16[4,64,256]{2,1,0:T(8,128)(2,1)S(1)}, u32[]{:S(2)}, u32[]{:S(2)}) collective-permute-start(bf16[4,64,256]{2,1,0:T(8,128)(2,1)S(1)} %get-tuple-element.78), channel_id=1, source_target_pairs={{0,34},{1,35},{2,32},{3,33},{4,38},{5,39},{6,36},{7,37},{8,42},{9,... | collective-permute-start | bytes 393224 | tf_op jit(solution)/shard_map/ppermute | solution.py:48
  28.0 9.8 %collective-permute-start.7 = (bf16[8,64,256]{2,1,0:T(8,128)(2,1)S(1)}, bf16[8,64,256]{2,1,0:T(8,128)(2,1)S(1)}, u32[]{:S(2)}, u32[]{:S(2)}) collective-permute-start(bf16[8,64,256]{2,1,0:T(8,128)(2,1)S(1)} %relay_0.7.refs_9_), channel_id=1, source_target_pairs={{0,16},{16,0},{32,48},{48,32},{64,80},{80,64},{96,112},{112,96},{1... | collective-permute-start | bytes 786440 | tf_op jit(solution)/shard_map/ppermute | solution.py:42
  29.6 11.8 %collective-permute-start.15 = (bf16[8,64,256]{2,1,0:T(8,128)(2,1)S(1)}, bf16[8,64,256]{2,1,0:T(8,128)(2,1)S(1)}, u32[]{:S(2)}, u32[]{:S(2)}) collective-permute-start(bf16[8,64,256]{2,1,0:T(8,128)(2,1)S(1)} %get-tuple-element.87), channel_id=1, source_target_pairs={{0,2},{1,3},{2,0},{3,1},{4,6},{5,7},{6,4},{7,5},{8,10},{9,11},{10,... | collective-permute-start | bytes 786440 | tf_op jit(solution)/shard_map/ppermute | solution.py:42
  33.5 20.8 %collective-permute-start.20 = (bf16[8,64,256]{2,1,0:T(8,128)(2,1)S(1)}, bf16[8,64,256]{2,1,0:T(8,128)(2,1)S(1)}, u32[]{:S(2)}, u32[]{:S(2)}) collective-permute-start(bf16[8,64,256]{2,1,0:T(8,128)(2,1)S(1)} %get-tuple-element.95), channel_id=1, source_target_pairs={{0,64},{16,80},{32,96},{48,112},{64,0},{80,16},{96,32},{112,48},{1... | collective-permute-start | bytes 786440 | tf_op jit(solution)/shard_map/ppermute | solution.py:42
  36.8 8.6 %collective-permute-start.21 = (bf16[4,64,256]{2,1,0:T(8,128)(2,1)S(1)}, bf16[4,64,256]{2,1,0:T(8,128)(2,1)S(1)}, u32[]{:S(2)}, u32[]{:S(2)}) collective-permute-start(bf16[4,64,256]{2,1,0:T(8,128)(2,1)S(1)} %get-tuple-element.96), channel_id=1, source_target_pairs={{0,32},{16,48},{32,0},{48,16},{64,96},{80,112},{96,64},{112,80},{1... | collective-permute-start | bytes 393224 | tf_op jit(solution)/shard_map/ppermute | solution.py:42
  36.8 11.1 %collective-permute-start.22 = (bf16[4,64,256]{2,1,0:T(8,128)(2,1)S(1)}, bf16[4,64,256]{2,1,0:T(8,128)(2,1)S(1)}, u32[]{:S(2)}, u32[]{:S(2)}) collective-permute-start(bf16[4,64,256]{2,1,0:T(8,128)(2,1)S(1)} %get-tuple-element.97), channel_id=1, source_target_pairs={{0,2},{1,3},{2,0},{3,1},{4,6},{5,7},{6,4},{7,5},{8,10},{9,11},{10,... | collective-permute-start | bytes 393224 | tf_op jit(solution)/shard_map/ppermute | solution.py:42
  37.9 12.5 %collective-permute-start.23 = (bf16[4,64,256]{2,1,0:T(8,128)(2,1)S(1)}, bf16[4,64,256]{2,1,0:T(8,128)(2,1)S(1)}, u32[]{:S(2)}, u32[]{:S(2)}) collective-permute-start(bf16[4,64,256]{2,1,0:T(8,128)(2,1)S(1)} %get-tuple-element.98), channel_id=1, source_target_pairs={{0,34},{1,35},{2,32},{3,33},{4,38},{5,39},{6,36},{7,37},{8,42},{9,... | collective-permute-start | bytes 393224 | tf_op jit(solution)/shard_map/ppermute | solution.py:48
  41.4 14.3 %collective-permute-start.19 = (bf16[4,128,128]{2,1,0:T(8,128)(2,1)S(1)}, bf16[4,128,128]{2,1,0:T(8,128)(2,1)S(1)}, u32[]{:S(2)}, u32[]{:S(2)}) collective-permute-start(bf16[4,128,128]{2,1,0:T(8,128)(2,1)S(1)} %get-tuple-element.94), channel_id=1, source_target_pairs={{0,4},{1,5},{2,6},{3,7},{4,0},{5,1},{6,2},{7,3},{8,12},{9,13},{10,... | collective-permute-start | bytes 393224 | tf_op jit(solution)/shard_map/ppermute | solution.py:42
  45.5 11.5 %collective-permute-start.12 = (bf16[4,64,256]{2,1,0:T(8,128)(2,1)S(1)}, bf16[4,64,256]{2,1,0:T(8,128)(2,1)S(1)}, u32[]{:S(2)}, u32[]{:S(2)}) collective-permute-start(bf16[4,64,256]{2,1,0:T(8,128)(2,1)S(1)} %get-tuple-element.84), channel_id=1, source_target_pairs={{0,32},{16,48},{32,0},{48,16},{64,96},{80,112},{96,64},{112,80},{1... | collective-permute-start | bytes 393224 | tf_op jit(solution)/shard_map/ppermute | solution.py:42
  47.9 11.8 %collective-permute-start.16 = (bf16[4,64,256]{2,1,0:T(8,128)(2,1)S(1)}, bf16[4,64,256]{2,1,0:T(8,128)(2,1)S(1)}, u32[]{:S(2)}, u32[]{:S(2)}) collective-permute-start(bf16[4,64,256]{2,1,0:T(8,128)(2,1)S(1)} %get-tuple-element.89), channel_id=1, source_target_pairs={{0,64},{16,80},{32,96},{48,112},{64,0},{80,16},{96,32},{112,48},{1... | collective-permute-start | bytes 393224 | tf_op jit(solution)/shard_map/ppermute | solution.py:42
  50.4 9.3 %collective-permute-start.17 = (bf16[4,64,256]{2,1,0:T(8,128)(2,1)S(1)}, bf16[4,64,256]{2,1,0:T(8,128)(2,1)S(1)}, u32[]{:S(2)}, u32[]{:S(2)}) collective-permute-start(bf16[4,64,256]{2,1,0:T(8,128)(2,1)S(1)} %get-tuple-element.90), channel_id=1, source_target_pairs={{0,4},{1,5},{2,6},{3,7},{4,0},{5,1},{6,2},{7,3},{8,12},{9,13},{10,... | collective-permute-start | bytes 393224 | tf_op jit(solution)/shard_map/ppermute | solution.py:42
  54.3 10.2 %collective-permute-start.18 = (bf16[4,64,256]{2,1,0:T(8,128)(2,1)S(1)}, bf16[4,64,256]{2,1,0:T(8,128)(2,1)S(1)}, u32[]{:S(2)}, u32[]{:S(2)}) collective-permute-start(bf16[4,64,256]{2,1,0:T(8,128)(2,1)S(1)} %get-tuple-element.91), channel_id=1, source_target_pairs={{0,68},{1,69},{2,70},{3,71},{4,64},{5,65},{6,66},{7,67},{8,76},{9,... | collective-permute-start | bytes 393224 | tf_op jit(solution)/shard_map/ppermute | solution.py:48
  55.7 11.3 %collective-permute-start.13 = (bf16[4,64,256]{2,1,0:T(8,128)(2,1)S(1)}, bf16[4,64,256]{2,1,0:T(8,128)(2,1)S(1)}, u32[]{:S(2)}, u32[]{:S(2)}) collective-permute-start(bf16[4,64,256]{2,1,0:T(8,128)(2,1)S(1)} %get-tuple-element.85), channel_id=1, source_target_pairs={{0,2},{1,3},{2,0},{3,1},{4,6},{5,7},{6,4},{7,5},{8,10},{9,11},{10,... | collective-permute-start | bytes 393224 | tf_op jit(solution)/shard_map/ppermute | solution.py:42
  56.9 12.9 %collective-permute-start.14 = (bf16[4,64,256]{2,1,0:T(8,128)(2,1)S(1)}, bf16[4,64,256]{2,1,0:T(8,128)(2,1)S(1)}, u32[]{:S(2)}, u32[]{:S(2)}) collective-permute-start(bf16[4,64,256]{2,1,0:T(8,128)(2,1)S(1)} %get-tuple-element.86), channel_id=1, source_target_pairs={{0,34},{1,35},{2,32},{3,33},{4,38},{5,39},{6,36},{7,37},{8,42},{9,... | collective-permute-start | bytes 393224 | tf_op jit(solution)/shard_map/ppermute | solution.py:48
  59.7 13.8 %collective-permute-start.28 = (bf16[4,64,256]{2,1,0:T(8,128)(2,1)S(1)}, bf16[4,64,256]{2,1,0:T(8,128)(2,1)S(1)}, u32[]{:S(2)}, u32[]{:S(2)}) collective-permute-start(bf16[4,64,256]{2,1,0:T(8,128)(2,1)S(1)} %get-tuple-element.106), channel_id=1, source_target_pairs={{0,64},{16,80},{32,96},{48,112},{64,0},{80,16},{96,32},{112,48},{1... | collective-permute-start | bytes 393224 | tf_op jit(solution)/shard_map/ppermute | solution.py:42
  59.8 22.9 %collective-permute-start.27 = (bf16[8,64,256]{2,1,0:T(8,128)(2,1)S(1)}, bf16[8,64,256]{2,1,0:T(8,128)(2,1)S(1)}, u32[]{:S(2)}, u32[]{:S(2)}) collective-permute-start(bf16[8,64,256]{2,1,0:T(8,128)(2,1)S(1)} %get-tuple-element.105), channel_id=1, source_target_pairs={{0,4},{1,5},{2,6},{3,7},{4,0},{5,1},{6,2},{7,3},{8,12},{9,13},{10,... | collective-permute-start | bytes 786440 | tf_op jit(solution)/shard_map/ppermute | solution.py:42
  64.4 10.0 %collective-permute-start.29 = (bf16[4,64,256]{2,1,0:T(8,128)(2,1)S(1)}, bf16[4,64,256]{2,1,0:T(8,128)(2,1)S(1)}, u32[]{:S(2)}, u32[]{:S(2)}) collective-permute-start(bf16[4,64,256]{2,1,0:T(8,128)(2,1)S(1)} %get-tuple-element.107), channel_id=1, source_target_pairs={{0,4},{1,5},{2,6},{3,7},{4,0},{5,1},{6,2},{7,3},{8,12},{9,13},{10,... | collective-permute-start | bytes 393224 | tf_op jit(solution)/shard_map/ppermute | solution.py:42
  67.1 13.9 %collective-permute-start.30 = (bf16[4,64,256]{2,1,0:T(8,128)(2,1)S(1)}, bf16[4,64,256]{2,1,0:T(8,128)(2,1)S(1)}, u32[]{:S(2)}, u32[]{:S(2)}) collective-permute-start(bf16[4,64,256]{2,1,0:T(8,128)(2,1)S(1)} %get-tuple-element.108), channel_id=1, source_target_pairs={{0,68},{1,69},{2,70},{3,71},{4,64},{5,65},{6,66},{7,67},{8,76},{9,... | collective-permute-start | bytes 393224 | tf_op jit(solution)/shard_map/ppermute | solution.py:48
  70.9 13.3 %collective-permute-start.24 = (bf16[4,64,256]{2,1,0:T(8,128)(2,1)S(1)}, bf16[4,64,256]{2,1,0:T(8,128)(2,1)S(1)}, u32[]{:S(2)}, u32[]{:S(2)}) collective-permute-start(bf16[4,64,256]{2,1,0:T(8,128)(2,1)S(1)} %get-tuple-element.102), channel_id=1, source_target_pairs={{0,64},{16,80},{32,96},{48,112},{64,0},{80,16},{96,32},{112,48},{1... | collective-permute-start | bytes 393224 | tf_op jit(solution)/shard_map/ppermute | solution.py:42
  73.5 10.7 %collective-permute-start.25 = (bf16[4,64,256]{2,1,0:T(8,128)(2,1)S(1)}, bf16[4,64,256]{2,1,0:T(8,128)(2,1)S(1)}, u32[]{:S(2)}, u32[]{:S(2)}) collective-permute-start(bf16[4,64,256]{2,1,0:T(8,128)(2,1)S(1)} %get-tuple-element.103), channel_id=1, source_target_pairs={{0,4},{1,5},{2,6},{3,7},{4,0},{5,1},{6,2},{7,3},{8,12},{9,13},{10,... | collective-permute-start | bytes 393224 | tf_op jit(solution)/shard_map/ppermute | solution.py:42
  74.4 11.0 %collective-permute-start.26 = (bf16[4,64,256]{2,1,0:T(8,128)(2,1)S(1)}, bf16[4,64,256]{2,1,0:T(8,128)(2,1)S(1)}, u32[]{:S(2)}, u32[]{:S(2)}) collective-permute-start(bf16[4,64,256]{2,1,0:T(8,128)(2,1)S(1)} %get-tuple-element.104), channel_id=1, source_target_pairs={{0,68},{1,69},{2,70},{3,71},{4,64},{5,65},{6,66},{7,67},{8,76},{9,... | collective-permute-start | bytes 393224 | tf_op jit(solution)/shard_map/ppermute | solution.py:48

commit v4 on v3

--- a/solution.py
+++ b/solution.py
@@ -234,7 +234,7 @@
     return call(kernel, f"relay_{section}", [in_vmem(8, 64, columns)], vmem(by_row, arrived), token)
 
 
-def end_step(section, flow, after, state, weights, token, result, start, total):
+def end_step(section, flow, after, state, weights, token, kept, start, total):
     early, late, local, cross, lent = weights
     columns = state[0].shape[2]
     pieces_in, offset = state, 0
@@ -243,7 +243,10 @@
     operands = vmem(*pieces_in, early, late, local)
     if flow != "c":
         operands += vmem(cross, lent)
-    n = len(pieces_in)
+    n, m = len(pieces_in), len(operands)
+    whole = after is None and sum(part.shape[2] for _, part in kept) + columns == total
+    if whole:
+        operands += vmem(*(part for _, part in kept))
 
     def halves(ins, buf):
         if flow == "c":
@@ -261,7 +264,13 @@
         return (lambda j: buf[1, j]), (lambda j: buf[1, 8 + j])
 
     def kernel(ins, outs, scratch):
-        buf = scratch[0]
+        buf, copies = scratch[0], []
+        if whole:
+            for i, (at, part) in enumerate(kept):
+                there = outs[0].at[:, :, pl.ds(at, part.shape[2])]
+                copies.append(pltpu.make_async_copy(ins[m + i], there, scratch[2].at[8 + i]))
+            for copy in copies:
+                copy.start()
         early, late, local = ins[n : n + 3]
         mine, theirs = halves(ins, buf)
         for j in range(4):
@@ -281,8 +290,11 @@
                         out[at : at + 2] = final(first // 2 + p)
                         at += 2
             return
+        if not whole:
+            for h in range(8):
+                outs[0][2 * h : 2 * h + 2] = final(h)
+            return
         done, sems = scratch[1:]
-        copies = []
         for h in range(8):
             done[2 * h : 2 * h + 2] = final(h)
             copy = pltpu.make_async_copy(
@@ -300,7 +312,10 @@
         return call(
             kernel, f"end_{section}", shapes(after, columns), operands, token, scratch=scratch
         )
-    scratch += [in_vmem(16, 64, columns), pltpu.SemaphoreType.DMA((8,))]
+    if not whole:
+        shape = [in_vmem(16, 64, columns)]
+        return call(kernel, f"end_{section}", shape, operands, token, scratch=scratch)
+    scratch += [in_vmem(16, 64, columns), pltpu.SemaphoreType.DMA((8 + len(kept),))]
     return call(
         kernel,
         f"end_{section}",
@@ -309,7 +324,6 @@
         token,
         out_specs=(ANY,),
         scratch=scratch,
-        result=result,
     )
 
 
@@ -320,7 +334,7 @@
     starts = [sum(SIZES[:c]) for c in range(len(SIZES))]
     blocks, *outs = first_take(order, blocks, SIZES[0])
     states = {0: (*sent("r", 0, outs), 0)}
-    token, result, ended = outs[0], None, False
+    token, kept = outs[0], []
     sections, halfway = [0] * len(SIZES), [False] * len(SIZES)
     for c in ORDER:
         if c == LATER:
@@ -351,22 +365,18 @@
                 (joined,) = relay_step(section, by_row, by_col, offset, token)
                 states[c] = own, by_col, swapped(joined, "row", section), offset
                 token = joined
-            ended = False
             continue
         weights = (*pairs[2 * section : 2 * section + 2], local, cross, lent[section])
         after = FLOWS[c][section + 1] if section < SECTIONS - 1 else None
-        onto = result if after is None else None
-        before = None if ended and onto is not None else token
-        outs = end_step(section, flow, after, state, weights, before, onto, starts[c], total)
+        outs = end_step(section, flow, after, state, weights, token, kept, starts[c], total)
         sections[c], halfway[c] = section + 1, False
+        token = outs[0]
         if after is None:
-            (result,) = outs
-            token, ended = outside(result), True
+            kept.append((starts[c], token))
         else:
             state = sent(after, section + 1, outs)
             states[c] = (*state, 0) if after == "r" else state
-            token, ended = outs[0], False
-    return result[None, None]
+    return token[None, None]
 
 
 def solution(mesh):

time: 88 us -> 87.8 us (level)
  waiting for transfers between devices: 16.5 us -> 19.7 us
  Pallas kernels: 19.3 us -> 17.1 us
  starting transfers between devices: 51.1 us -> 49.7 us
    ppermute x6, waiting for transfers between devices: 5.69 us -> 8.21 us  [swapped_both(): return lax.ppermute(piece, ('row', 'col'), pairs)]
    pallas_call x21, Pallas kernels: 19.3 us -> 17.1 us  [call(): pl.pallas_call(body, out_shape=tuple(out_shape), in_specs=specs, out_spec...]
    ppermute x25, starting transfers between devices: 37.5 us -> 36.3 us  [swapped(): lax.ppermute(piece, axis, [(i, i ^ 1 << section) for i in range(size)])]
  transfers between devices with their start and end apart: 31 -> 31, of which waited for: 10 -> 12; matrix products, arithmetic and copies ran while one was open for 0% -> 0% of each run, Pallas kernels for 17% -> 14%
where the time goes in v4:
time: 87.8 us; the launch traced here: 87.1 us
  starting transfers between devices  49.7 us (57%)
  waiting for transfers between devices  19.7 us (22%)
  Pallas kernels  17.1 us (19%)
    ppermute x25, starting transfers between devices, swapped(): lax.ppermute(piece, axis, [(i, i ^ 1 << section) for i in range(size)])  36.3 us
    pallas_call x21, Pallas kernels, call(): pl.pallas_call(body, out_shape=tuple(out_shape), in_specs=specs, out_spec...  17.1 us
    ppermute x6, starting transfers between devices, swapped_both(): return lax.ppermute(piece, ('row', 'col'), pairs)  13.4 us
    ppermute x25, waiting for transfers between devices, swapped(): lax.ppermute(piece, axis, [(i, i ^ 1 << section) for i in range(size)])  11.5 us
    ppermute x6, waiting for transfers between devices, swapped_both(): return lax.ppermute(piece, ('row', 'col'), pairs)  8.21 us
  transfers between devices with their start and end apart: 31, of which 12 were waited for; matrix products, arithmetic and copies ran while one was open for 0% of the time, Pallas kernels for 14%

profile of v4, /device:TPU:6, one launch (start us, length us, event | category | flops | bytes accessed | tf_op | source)
XLA Modules:
  0.0 87.1 jit_solution(4764392025146809996)
XLA Ops:
  0.0 1.8 %take_first.1 = (bf16[16,64,1024]{2,1,0:T(8,128)(2,1)S(1)}, bf16[4,64,256]{2,1,0:T(8,128)(2,1)S(1)}, bf16[4,64,256]{2,1,0:T(8,128)(2,1)S(1)}, bf16[8,64,256]{2,1,0:T(8,128)(2,1)S(1)}) custom-call(s32[1,16]{1,0:T(1,128)} %bitcast.33, bf16[16,64,1024]{2,1,0:T(8,128)(2,1)} %bitcast.32), custom_call_target="tpu_custom_call" | custom-call | flops 1 | bytes 1 | tf_op jit(solution)/shard_map/take_first/pallas_call | solution.py:67
  1.8 0.1 collective-permute-start
  1.9 1.5 %collective-permute-done.refs_1_ = bf16[8,64,256]{2,1,0:T(8,128)(2,1)S(1)} collective-permute-done((bf16[8,64,256]{2,1,0:T(8,128)(2,1)S(1)}, bf16[8,64,256]{2,1,0:T(8,128)(2,1)S(1)}, u32[]{:S(2)}, u32[]{:S(2)}) %collective-permute-start) | collective-permute-done | bytes 262176 | tf_op jit(solution)/shard_map/ppermute | solution.py:42
  3.5 0.0 copy-start
  3.5 1.0 %take_later.1 = (bf16[4,128,128]{2,1,0:T(8,128)(2,1)S(1)}, bf16[4,128,128]{2,1,0:T(8,128)(2,1)S(1)}, bf16[4,128,128]{2,1,0:T(8,128)(2,1)S(1)}, bf16[8,64,768]{2,...) custom-call(s32[1,16]{1,0:T(1,128)} %bitcast.34, ...), custom_call_target="tpu_custom_call" | custom-call | flops 1 | bytes 1 | tf_op jit(solution)/shard_map/take_later/pallas_call | solution.py:67
  4.5 0.2 collective-permute-start.1
  4.7 1.4 %collective-permute-start.4 = (bf16[8,64,256]{2,1,0:T(8,128)(2,1)S(1)}, bf16[8,64,256]{2,1,0:T(8,128)(2,1)S(1)}, u32[]{:S(2)}, u32[]{:S(2)}) collective-permute-start(bf16[8,64,256]{2,1,0:T(8,128)(2,1)S(1)} %relay_0.4.refs_3_), channel_id=1, source_target_pairs={{0,16},{16,0},{32,48},{48,32},{64,80},{80,64},{96,112},{112,96},{1... | collective-permute-start | bytes 786440 | tf_op jit(solution)/shard_map/ppermute | solution.py:42
  6.1 0.1 collective-permute-start.3
  6.2 0.6 collective-permute-done.1.refs_1_
  6.9 1.0 %combine.1 = (bf16[4,256,256]{2,1,0:T(8,128)(2,1)S(1)}, bf16[4,256,256]{2,1,0:T(8,128)(2,1)S(1)}, bf16[4,256,256]{2,1,0:T(8,128)(2,1)S(1)}, bf16[4,256,256]{2,1,...) custom-call(bf16[6,8,128,128]{3,2,1,0:T(8,128)(2,1)S(1)} %bitcast.19, ...), custom_call_target="tpu_custom_call" | custom-call | flops 1 | bytes 1 | tf_op jit(solution)/shard_map/combine/pallas_call | solution.py:67
  8.0 1.6 %collective-permute-start.6 = (bf16[8,64,256]{2,1,0:T(8,128)(2,1)S(1)}, bf16[8,64,256]{2,1,0:T(8,128)(2,1)S(1)}, u32[]{:S(2)}, u32[]{:S(2)}) collective-permute-start(bf16[8,64,256]{2,1,0:T(8,128)(2,1)S(1)} %relay_0.6.refs_8_), channel_id=1, source_target_pairs={{0,16},{16,0},{32,48},{48,32},{64,80},{80,64},{96,112},{112,96},{1... | collective-permute-start | bytes 786440 | tf_op jit(solution)/shard_map/ppermute | solution.py:42
  9.5 5.8 %collective-permute-done.4.refs_2_ = bf16[8,64,256]{2,1,0:T(8,128)(2,1)S(1)} collective-permute-done((bf16[8,64,256]{2,1,0:T(8,128)(2,1)S(1)}, bf16[8,64,256]{2,1,0:T(8,128)(2,1)S(1)}, u32[]{:S(2)}, u32[]{:S(2)}) %collective-permute-start.4) | collective-permute-done | bytes 262176 | tf_op jit(solution)/shard_map/ppermute | solution.py:42
  15.3 1.0 %end_0.4 = (bf16[8,64,256]{2,1,0:T(8,128)(2,1)S(1)}, bf16[8,64,256]{2,1,0:T(8,128)(2,1)S(1)}) custom-call(bf16[4,64,256]{2,1,0:T(8,128)(2,1)S(1)} %get-tuple-element.60.refs_2_.refs_0_, bf16[8,64,256]{2,1,0:T(8,128)(2,1)S(1)} %collective-permute-done.refs_1_, bf16[8,64,256]{2,1,0:T(8,128)(2,1)S(1)} %collective-permute-done.4.refs_2_, ...), custom_call_target="tpu_custom_call" | custom-call | flops 1 | bytes 1 | tf_op jit(solution)/shard_map/end_0/pallas_call | solution.py:67
  16.4 2.0 %collective-permute-start.5 = (bf16[8,64,256]{2,1,0:T(8,128)(2,1)S(1)}, bf16[8,64,256]{2,1,0:T(8,128)(2,1)S(1)}, u32[]{:S(2)}, u32[]{:S(2)}) collective-permute-start(bf16[8,64,256]{2,1,0:T(8,128)(2,1)S(1)} %get-tuple-element.71), channel_id=1, source_target_pairs={{0,32},{16,48},{32,0},{48,16},{64,96},{80,112},{96,64},{112,80},{1... | collective-permute-start | bytes 786440 | tf_op jit(solution)/shard_map/ppermute | solution.py:42
  18.4 1.4 %collective-permute-start.2 = (bf16[8,64,256]{2,1,0:T(8,128)(2,1)S(1)}, bf16[8,64,256]{2,1,0:T(8,128)(2,1)S(1)}, u32[]{:S(2)}, u32[]{:S(2)}) collective-permute-start(bf16[8,64,256]{2,1,0:T(8,128)(2,1)S(1)} %relay_0.5.refs_2_), channel_id=1, source_target_pairs={{0,16},{16,0},{32,48},{48,32},{64,80},{80,64},{96,112},{112,96},{1... | collective-permute-start | bytes 786440 | tf_op jit(solution)/shard_map/ppermute | solution.py:42
  19.8 1.6 %collective-permute-start.11 = (bf16[4,128,128]{2,1,0:T(8,128)(2,1)S(1)}, bf16[4,128,128]{2,1,0:T(8,128)(2,1)S(1)}, u32[]{:S(2)}, u32[]{:S(2)}) collective-permute-start(bf16[4,128,128]{2,1,0:T(8,128)(2,1)S(1)} %get-tuple-element.81), channel_id=1, source_target_pairs={{0,2},{1,3},{2,0},{3,1},{4,6},{5,7},{6,4},{7,5},{8,10},{9,11},{10,... | collective-permute-start | bytes 393224 | tf_op jit(solution)/shard_map/ppermute | solution.py:42
  21.4 1.0 %end_0.5 = (bf16[4,64,256]{2,1,0:T(8,128)(2,1)S(1)}, bf16[4,64,256]{2,1,0:T(8,128)(2,1)S(1)}, bf16[4,64,256]{2,1,0:T(8,128)(2,1)S(1)}, bf16[4,64,256]{2,1,0:T(8,128)(2,1)S(1)}) custom-call(bf16[4,64,256]{2,1,0:T(8,128)(2,1)S(1)} %get-tuple-element.72.refs_0_, bf16[8,64,768]{2,1,0:T(8,128)(2,1)S(1)} %collective-permute-done.1.refs_1_, ...), custom_call_target="tpu_custom_call" | custom-call | flops 1 | bytes 1 | tf_op jit(solution)/shard_map/end_0/pallas_call | solution.py:67
  22.4 1.6 %collective-permute-start.8 = (bf16[4,64,256]{2,1,0:T(8,128)(2,1)S(1)}, bf16[4,64,256]{2,1,0:T(8,128)(2,1)S(1)}, u32[]{:S(2)}, u32[]{:S(2)}) collective-permute-start(bf16[4,64,256]{2,1,0:T(8,128)(2,1)S(1)} %get-tuple-element.76), channel_id=1, source_target_pairs={{0,32},{16,48},{32,0},{48,16},{64,96},{80,112},{96,64},{112,80},{1... | collective-permute-start | bytes 393224 | tf_op jit(solution)/shard_map/ppermute | solution.py:42
  24.0 1.6 %collective-permute-start.9 = (bf16[4,64,256]{2,1,0:T(8,128)(2,1)S(1)}, bf16[4,64,256]{2,1,0:T(8,128)(2,1)S(1)}, u32[]{:S(2)}, u32[]{:S(2)}) collective-permute-start(bf16[4,64,256]{2,1,0:T(8,128)(2,1)S(1)} %get-tuple-element.77), channel_id=1, source_target_pairs={{0,2},{1,3},{2,0},{3,1},{4,6},{5,7},{6,4},{7,5},{8,10},{9,11},{10,... | collective-permute-start | bytes 393224 | tf_op jit(solution)/shard_map/ppermute | solution.py:42
  25.6 1.0 %collective-permute-start.10 = (bf16[4,64,256]{2,1,0:T(8,128)(2,1)S(1)}, bf16[4,64,256]{2,1,0:T(8,128)(2,1)S(1)}, u32[]{:S(2)}, u32[]{:S(2)}) collective-permute-start(bf16[4,64,256]{2,1,0:T(8,128)(2,1)S(1)} %get-tuple-element.78), channel_id=1, source_target_pairs={{0,34},{1,35},{2,32},{3,33},{4,38},{5,39},{6,36},{7,37},{8,42},{9,... | collective-permute-start | bytes 393224 | tf_op jit(solution)/shard_map/ppermute | solution.py:48
  26.6 0.3 row_1.1
  26.9 1.1 %end_0.6 = (bf16[4,64,256]{2,1,0:T(8,128)(2,1)S(1)}, bf16[4,64,256]{2,1,0:T(8,128)(2,1)S(1)}, bf16[4,64,256]{2,1,0:T(8,128)(2,1)S(1)}, bf16[4,64,256]{2,1,0:T(8,128)(2,1)S(1)}) custom-call(bf16[4,64,256]{2,1,0:T(8,128)(2,1)S(1)} %get-tuple-element.64.refs_0_, bf16[8,64,768]{2,1,0:T(8,128)(2,1)S(1)} %collective-permute-done.1.refs_1_, ...), custom_call_target="tpu_custom_call" | custom-call | flops 1 | bytes 1 | tf_op jit(solution)/shard_map/end_0/pallas_call | solution.py:67
  28.0 1.6 %collective-permute-start.7 = (bf16[8,64,256]{2,1,0:T(8,128)(2,1)S(1)}, bf16[8,64,256]{2,1,0:T(8,128)(2,1)S(1)}, u32[]{:S(2)}, u32[]{:S(2)}) collective-permute-start(bf16[8,64,256]{2,1,0:T(8,128)(2,1)S(1)} %relay_0.7.refs_9_), channel_id=1, source_target_pairs={{0,16},{16,0},{32,48},{48,32},{64,80},{80,64},{96,112},{112,96},{1... | collective-permute-start | bytes 786440 | tf_op jit(solution)/shard_map/ppermute | solution.py:42
  29.6 1.4 %collective-permute-start.15 = (bf16[8,64,256]{2,1,0:T(8,128)(2,1)S(1)}, bf16[8,64,256]{2,1,0:T(8,128)(2,1)S(1)}, u32[]{:S(2)}, u32[]{:S(2)}) collective-permute-start(bf16[8,64,256]{2,1,0:T(8,128)(2,1)S(1)} %get-tuple-element.87), channel_id=1, source_target_pairs={{0,2},{1,3},{2,0},{3,1},{4,6},{5,7},{6,4},{7,5},{8,10},{9,11},{10,... | collective-permute-start | bytes 786440 | tf_op jit(solution)/shard_map/ppermute | solution.py:42
  31.0 0.0 collective-permute-done.8.refs_1_
  31.0 1.4 %collective-permute-done.9.refs_2_ = bf16[4,64,256]{2,1,0:T(8,128)(2,1)S(1)} collective-permute-done((bf16[4,64,256]{2,1,0:T(8,128)(2,1)S(1)}, bf16[4,64,256]{2,1,0:T(8,128)(2,1)S(1)}, u32[]{:S(2)}, u32[]{:S(2)}) %collective-permute-start.9) | collective-permute-done | bytes 131104 | tf_op jit(solution)/shard_map/ppermute | solution.py:42
  32.4 0.0 collective-permute-done.10.refs_3_
  32.4 1.1 %end_1.4 = (bf16[8,64,256]{2,1,0:T(8,128)(2,1)S(1)}, bf16[8,64,256]{2,1,0:T(8,128)(2,1)S(1)}) custom-call(bf16[4,64,256]{2,1,0:T(8,128)(2,1)S(1)} %get-tuple-element.73.refs_3_.refs_0_, bf16[4,64,256]{2,1,0:T(8,128)(2,1)S(1)} %collective-permute-done.8.refs_1_, bf16[4,64,256]{2,1,0:T(8,128)(2,1)S(1)} %collective-permute-done.9.refs_2_, ...), custom_call_target="tpu_custom_call" | custom-call | flops 1 | bytes 1 | tf_op jit(solution)/shard_map/end_1/pallas_call | solution.py:67
  33.5 3.4 %collective-permute-start.20 = (bf16[8,64,256]{2,1,0:T(8,128)(2,1)S(1)}, bf16[8,64,256]{2,1,0:T(8,128)(2,1)S(1)}, u32[]{:S(2)}, u32[]{:S(2)}) collective-permute-start(bf16[8,64,256]{2,1,0:T(8,128)(2,1)S(1)} %get-tuple-element.95), channel_id=1, source_target_pairs={{0,64},{16,80},{32,96},{48,112},{64,0},{80,16},{96,32},{112,48},{1... | collective-permute-start | bytes 786440 | tf_op jit(solution)/shard_map/ppermute | solution.py:42
  36.8 1.0 %collective-permute-start.22 = (bf16[4,64,256]{2,1,0:T(8,128)(2,1)S(1)}, bf16[4,64,256]{2,1,0:T(8,128)(2,1)S(1)}, u32[]{:S(2)}, u32[]{:S(2)}) collective-permute-start(bf16[4,64,256]{2,1,0:T(8,128)(2,1)S(1)} %get-tuple-element.97), channel_id=1, source_target_pairs={{0,2},{1,3},{2,0},{3,1},{4,6},{5,7},{6,4},{7,5},{8,10},{9,11},{10,... | collective-permute-start | bytes 393224 | tf_op jit(solution)/shard_map/ppermute | solution.py:42
  37.9 0.0 collective-permute-done.7.refs_2_
  37.9 2.5 %collective-permute-start.23 = (bf16[4,64,256]{2,1,0:T(8,128)(2,1)S(1)}, bf16[4,64,256]{2,1,0:T(8,128)(2,1)S(1)}, u32[]{:S(2)}, u32[]{:S(2)}) collective-permute-start(bf16[4,64,256]{2,1,0:T(8,128)(2,1)S(1)} %get-tuple-element.98), channel_id=1, source_target_pairs={{0,34},{1,35},{2,32},{3,33},{4,38},{5,39},{6,36},{7,37},{8,42},{9,... | collective-permute-start | bytes 393224 | tf_op jit(solution)/shard_map/ppermute | solution.py:48
  40.3 1.0 %end_0.7 = (bf16[4,64,256]{2,1,0:T(8,128)(2,1)S(1)}, bf16[4,64,256]{2,1,0:T(8,128)(2,1)S(1)}, bf16[4,64,256]{2,1,0:T(8,128)(2,1)S(1)}, bf16[4,64,256]{2,1,0:T(8,128)(2,1)S(1)}) custom-call(bf16[4,64,256]{2,1,0:T(8,128)(2,1)S(1)} %get-tuple-element.61.refs_0_, bf16[8,64,768]{2,1,0:T(8,128)(2,1)S(1)} %collective-permute-done.1.refs_1_, ...), custom_call_target="tpu_custom_call" | custom-call | flops 1 | bytes 1 | tf_op jit(solution)/shard_map/end_0/pallas_call | solution.py:67
  41.4 3.1 %collective-permute-start.19 = (bf16[4,128,128]{2,1,0:T(8,128)(2,1)S(1)}, bf16[4,128,128]{2,1,0:T(8,128)(2,1)S(1)}, u32[]{:S(2)}, u32[]{:S(2)}) collective-permute-start(bf16[4,128,128]{2,1,0:T(8,128)(2,1)S(1)} %get-tuple-element.94), channel_id=1, source_target_pairs={{0,4},{1,5},{2,6},{3,7},{4,0},{5,1},{6,2},{7,3},{8,12},{9,13},{10,... | collective-permute-start | bytes 393224 | tf_op jit(solution)/shard_map/ppermute | solution.py:42
  44.5 0.8 end_1.5
  45.3 0.1 collective-permute-done.21.refs_1_
  45.5 2.5 %collective-permute-start.12 = (bf16[4,64,256]{2,1,0:T(8,128)(2,1)S(1)}, bf16[4,64,256]{2,1,0:T(8,128)(2,1)S(1)}, u32[]{:S(2)}, u32[]{:S(2)}) collective-permute-start(bf16[4,64,256]{2,1,0:T(8,128)(2,1)S(1)} %get-tuple-element.84), channel_id=1, source_target_pairs={{0,32},{16,48},{32,0},{48,16},{64,96},{80,112},{96,64},{112,80},{1... | collective-permute-start | bytes 393224 | tf_op jit(solution)/shard_map/ppermute | solution.py:42
  47.9 0.0 collective-permute-done.22.refs_2_
  47.9 2.5 %collective-permute-done.23.refs_3_ = bf16[4,64,256]{2,1,0:T(8,128)(2,1)S(1)} collective-permute-done((bf16[4,64,256]{2,1,0:T(8,128)(2,1)S(1)}, bf16[4,64,256]{2,1,0:T(8,128)(2,1)S(1)}, u32[]{:S(2)}, u32[]{:S(2)}) %collective-permute-start.23) | collective-permute-done | bytes 131104 | tf_op jit(solution)/shard_map/ppermute | solution.py:48
  50.4 3.8 %collective-permute-start.17 = (bf16[4,64,256]{2,1,0:T(8,128)(2,1)S(1)}, bf16[4,64,256]{2,1,0:T(8,128)(2,1)S(1)}, u32[]{:S(2)}, u32[]{:S(2)}) collective-permute-start(bf16[4,64,256]{2,1,0:T(8,128)(2,1)S(1)} %get-tuple-element.90), channel_id=1, source_target_pairs={{0,4},{1,5},{2,6},{3,7},{4,0},{5,1},{6,2},{7,3},{8,12},{9,13},{10,... | collective-permute-start | bytes 393224 | tf_op jit(solution)/shard_map/ppermute | solution.py:42
  54.3 0.1 collective-permute-start.18
  54.4 1.0 %end_1.6 = (bf16[4,64,256]{2,1,0:T(8,128)(2,1)S(1)}, bf16[4,64,256]{2,1,0:T(8,128)(2,1)S(1)}, bf16[4,64,256]{2,1,0:T(8,128)(2,1)S(1)}, bf16[4,64,256]{2,1,0:T(8,128)(2,1)S(1)}) custom-call(bf16[4,64,256]{2,1,0:T(8,128)(2,1)S(1)} %get-tuple-element.75.refs_2_.refs_0_, bf16[4,64,256]{2,1,0:T(8,128)(2,1)S(1)} %collective-permute-done.21.refs_1_, ...), custom_call_target="tpu_custom_call" | custom-call | flops 1 | bytes 1 | tf_op jit(solution)/shard_map/end_1/pallas_call | solution.py:67
  55.4 0.3 row_2.1
  55.7 1.2 %collective-permute-start.13 = (bf16[4,64,256]{2,1,0:T(8,128)(2,1)S(1)}, bf16[4,64,256]{2,1,0:T(8,128)(2,1)S(1)}, u32[]{:S(2)}, u32[]{:S(2)}) collective-permute-start(bf16[4,64,256]{2,1,0:T(8,128)(2,1)S(1)} %get-tuple-element.85), channel_id=1, source_target_pairs={{0,2},{1,3},{2,0},{3,1},{4,6},{5,7},{6,4},{7,5},{8,10},{9,11},{10,... | collective-permute-start | bytes 393224 | tf_op jit(solution)/shard_map/ppermute | solution.py:42
  56.9 1.5 %collective-permute-start.14 = (bf16[4,64,256]{2,1,0:T(8,128)(2,1)S(1)}, bf16[4,64,256]{2,1,0:T(8,128)(2,1)S(1)}, u32[]{:S(2)}, u32[]{:S(2)}) collective-permute-start(bf16[4,64,256]{2,1,0:T(8,128)(2,1)S(1)} %get-tuple-element.86), channel_id=1, source_target_pairs={{0,34},{1,35},{2,32},{3,33},{4,38},{5,39},{6,36},{7,37},{8,42},{9,... | collective-permute-start | bytes 393224 | tf_op jit(solution)/shard_map/ppermute | solution.py:48
  58.5 1.3 %collective-permute-done.16.refs_1_ = bf16[4,64,256]{2,1,0:T(8,128)(2,1)S(1)} collective-permute-done((bf16[4,64,256]{2,1,0:T(8,128)(2,1)S(1)}, bf16[4,64,256]{2,1,0:T(8,128)(2,1)S(1)}, u32[]{:S(2)}, u32[]{:S(2)}) %collective-permute-start.16) | collective-permute-done | bytes 131104 | tf_op jit(solution)/shard_map/ppermute | solution.py:42
  59.7 0.0 collective-permute-start.27
  59.8 0.0 collective-permute-done.17.refs_2_
  59.8 3.6 %collective-permute-start.30 = (bf16[8,64,256]{2,1,0:T(8,128)(2,1)S(1)}, bf16[8,64,256]{2,1,0:T(8,128)(2,1)S(1)}, u32[]{:S(2)}, u32[]{:S(2)}) collective-permute-start(bf16[8,64,256]{2,1,0:T(8,128)(2,1)S(1)} %get-tuple-element.108), channel_id=1, source_target_pairs={{0,4},{1,5},{2,6},{3,7},{4,0},{5,1},{6,2},{7,3},{8,12},{9,13},{10,... | collective-permute-start | bytes 786440 | tf_op jit(solution)/shard_map/ppermute | solution.py:42
  63.3 1.1 %collective-permute-done.18.refs_3_ = bf16[4,64,256]{2,1,0:T(8,128)(2,1)S(1)} collective-permute-done((bf16[4,64,256]{2,1,0:T(8,128)(2,1)S(1)}, bf16[4,64,256]{2,1,0:T(8,128)(2,1)S(1)}, u32[]{:S(2)}, u32[]{:S(2)}) %collective-permute-start.18) | collective-permute-done | bytes 131104 | tf_op jit(solution)/shard_map/ppermute | solution.py:48
  64.4 0.9 %collective-permute-start.28 = (bf16[4,64,256]{2,1,0:T(8,128)(2,1)S(1)}, bf16[4,64,256]{2,1,0:T(8,128)(2,1)S(1)}, u32[]{:S(2)}, u32[]{:S(2)}) collective-permute-start(bf16[4,64,256]{2,1,0:T(8,128)(2,1)S(1)} %get-tuple-element.106), channel_id=1, source_target_pairs={{0,4},{1,5},{2,6},{3,7},{4,0},{5,1},{6,2},{7,3},{8,12},{9,13},{10,... | collective-permute-start | bytes 393224 | tf_op jit(solution)/shard_map/ppermute | solution.py:42
  65.4 1.0 %end_2.4.refs_9_ = bf16[16,64,256]{2,1,0:T(8,128)(2,1)S(1)} custom-call(bf16[4,64,256]{2,1,0:T(8,128)(2,1)S(1)} %get-tuple-element.88.refs_9_.refs_0_, bf16[4,64,256]{2,1,0:T(8,128)(2,1)S(1)} %collective-permute-done.16.refs_1_, bf16[4,64,256]{2,1,0:T(8,128)(2,1)S(1)} %collective-permute-done.17.refs_2_, ...), custom_call_target="tpu_custom_call" | custom-call | flops 1 | bytes 1 | tf_op jit(solution)/shard_map/end_2/pallas_call | solution.py:67
  66.3 0.2 collective-permute-done.13.refs_2_
  66.6 3.7 %collective-permute-start.29 = (bf16[4,64,256]{2,1,0:T(8,128)(2,1)S(1)}, bf16[4,64,256]{2,1,0:T(8,128)(2,1)S(1)}, u32[]{:S(2)}, u32[]{:S(2)}) collective-permute-start(bf16[4,64,256]{2,1,0:T(8,128)(2,1)S(1)} %get-tuple-element.107), channel_id=1, source_target_pairs={{0,68},{1,69},{2,70},{3,71},{4,64},{5,65},{6,66},{7,67},{8,76},{9,... | collective-permute-start | bytes 393224 | tf_op jit(solution)/shard_map/ppermute | solution.py:48
  70.3 1.0 %end_1.7 = (bf16[4,64,256]{2,1,0:T(8,128)(2,1)S(1)}, bf16[4,64,256]{2,1,0:T(8,128)(2,1)S(1)}, bf16[4,64,256]{2,1,0:T(8,128)(2,1)S(1)}, bf16[4,64,256]{2,1,0:T(8,128)(2,1)S(1)}) custom-call(bf16[4,64,256]{2,1,0:T(8,128)(2,1)S(1)} %get-tuple-element.83.refs_5_.refs_0_, bf16[4,64,256]{2,1,0:T(8,128)(2,1)S(1)} %collective-permute-done.12.refs_1_, ...), custom_call_target="tpu_custom_call" | custom-call | flops 1 | bytes 1 | tf_op jit(solution)/shard_map/end_1/pallas_call | solution.py:67
  71.3 1.8 %collective-permute-start.24 = (bf16[4,64,256]{2,1,0:T(8,128)(2,1)S(1)}, bf16[4,64,256]{2,1,0:T(8,128)(2,1)S(1)}, u32[]{:S(2)}, u32[]{:S(2)}) collective-permute-start(bf16[4,64,256]{2,1,0:T(8,128)(2,1)S(1)} %get-tuple-element.102), channel_id=1, source_target_pairs={{0,64},{16,80},{32,96},{48,112},{64,0},{80,16},{96,32},{112,48},{1... | collective-permute-start | bytes 393224 | tf_op jit(solution)/shard_map/ppermute | solution.py:42
  73.2 0.5 collective-permute-start.25
  73.7 0.4 collective-permute-done.28.refs_2_
  74.1 4.6 %collective-permute-start.26 = (bf16[4,64,256]{2,1,0:T(8,128)(2,1)S(1)}, bf16[4,64,256]{2,1,0:T(8,128)(2,1)S(1)}, u32[]{:S(2)}, u32[]{:S(2)}) collective-permute-start(bf16[4,64,256]{2,1,0:T(8,128)(2,1)S(1)} %get-tuple-element.104), channel_id=1, source_target_pairs={{0,68},{1,69},{2,70},{3,71},{4,64},{5,65},{6,66},{7,67},{8,76},{9,... | collective-permute-start | bytes 393224 | tf_op jit(solution)/shard_map/ppermute | solution.py:48
  78.7 2.0 %collective-permute-done.29.refs_3_ = bf16[4,64,256]{2,1,0:T(8,128)(2,1)S(1)} collective-permute-done((bf16[4,64,256]{2,1,0:T(8,128)(2,1)S(1)}, bf16[4,64,256]{2,1,0:T(8,128)(2,1)S(1)}, u32[]{:S(2)}, u32[]{:S(2)}) %collective-permute-start.29) | collective-permute-done | bytes 131104 | tf_op jit(solution)/shard_map/ppermute | solution.py:48
  80.7 1.0 %end_2.5.refs_5_.refs_10_ = bf16[16,64,256]{2,1,0:T(8,128)(2,1)S(1)} custom-call(bf16[4,64,256]{2,1,0:T(8,128)(2,1)S(1)} %get-tuple-element.99.refs_3_.refs_0_, bf16[4,64,256]{2,1,0:T(8,128)(2,1)S(1)} %collective-permute-done.27.refs_1_, bf16[4,64,256]{2,1,0:T(8,128)(2,1)S(1)} %collective-permute-done.28.refs_2_, ...), custom_call_target="tpu_custom_call" | custom-call | flops 1 | bytes 1 | tf_op jit(solution)/shard_map/end_2/pallas_call | solution.py:67
  81.7 0.8 end_2.6.refs_11_.refs_12_
  82.5 2.6 %collective-permute-done.26.refs_3_ = bf16[4,64,256]{2,1,0:T(8,128)(2,1)S(1)} collective-permute-done((bf16[4,64,256]{2,1,0:T(8,128)(2,1)S(1)}, bf16[4,64,256]{2,1,0:T(8,128)(2,1)S(1)}, u32[]{:S(2)}, u32[]{:S(2)}) %collective-permute-start.26) | collective-permute-done | bytes 131104 | tf_op jit(solution)/shard_map/ppermute | solution.py:48
  85.1 1.7 %end_2.7 = bf16[16,64,1024]{2,1,0:T(8,128)(2,1)} custom-call(bf16[4,64,256]{2,1,0:T(8,128)(2,1)S(1)} %get-tuple-element.101.refs_9_.refs_0_, bf16[4,64,256]{2,1,0:T(8,128)(2,1)S(1)} %collective-permute-done.24.refs_1_, bf16[4,64,256]{2,1,0:T(8,128)(2,1)S(1)} %collective-permute-done.25.refs_2_, bf16[4,64,256]{2,1,0:T(8,128)(2,1)S(1)} %collective-permute-done.26.refs_3_, ...), custom_call_target="tpu_custom_call" | custom-call | flops 1 | bytes 1 | tf_op jit(solution)/shard_map/end_2/pallas_call | solution.py:67
  (23 shorter events, 0.1 us)
Async XLA Ops:
  0.0 3.5 %copy-start.1 = (bf16[6,1,1,8,128,128]{5,4,3,2,1,0:T(8,128)(2,1)S(1)}, bf16[6,1,1,8,128,128]{5,4,3,2,1,0:T(8,128)(2,1)}, u32[]{:S(2)}) copy-start(bf16[6,1,1,8,128,128]{5,4,3,2,1,0:T(8,128)(2,1)} %param.6) | copy-start | bytes 4718596
  1.8 1.6 %collective-permute-start = (bf16[8,64,256]{2,1,0:T(8,128)(2,1)S(1)}, bf16[8,64,256]{2,1,0:T(8,128)(2,1)S(1)}, u32[]{:S(2)}, u32[]{:S(2)}) collective-permute-start(bf16[8,64,256]{2,1,0:T(8,128)(2,1)S(1)} %get-tuple-element.59), channel_id=1, source_target_pairs={{0,1},{1,0},{2,3},{3,2},{4,5},{5,4},{6,7},{7,6},{8,9},{9,8},{10,11... | collective-permute-start | bytes 786440 | tf_op jit(solution)/shard_map/ppermute | solution.py:42
  3.5 3.4 %copy-start = (bf16[12,1,1,8,128,128]{5,4,3,2,1,0:T(8,128)(2,1)S(1)}, bf16[12,1,1,8,128,128]{5,4,3,2,1,0:T(8,128)(2,1)}, u32[]{:S(2)}) copy-start(bf16[12,1,1,8,128,128]{5,4,3,2,1,0:T(8,128)(2,1)} %param.7) | copy-start | bytes 9437188
  4.5 2.4 %collective-permute-start.1 = (bf16[8,64,768]{2,1,0:T(8,128)(2,1)S(1)}, bf16[8,64,768]{2,1,0:T(8,128)(2,1)S(1)}, u32[]{:S(2)}, u32[]{:S(2)}) collective-permute-start(bf16[8,64,768]{2,1,0:T(8,128)(2,1)S(1)} %get-tuple-element.62.refs_2_), channel_id=1, source_target_pairs={{0,1},{1,0},{2,3},{3,2},{4,5},{5,4},{6,7},{7,6},{8,9},{9,8},{10,11... | collective-permute-start | bytes 2359304 | tf_op jit(solution)/shard_map/ppermute | solution.py:42
  4.7 10.6 %collective-permute-start.4 = (bf16[8,64,256]{2,1,0:T(8,128)(2,1)S(1)}, bf16[8,64,256]{2,1,0:T(8,128)(2,1)S(1)}, u32[]{:S(2)}, u32[]{:S(2)}) collective-permute-start(bf16[8,64,256]{2,1,0:T(8,128)(2,1)S(1)} %relay_0.4.refs_3_), channel_id=1, source_target_pairs={{0,16},{16,0},{32,48},{48,32},{64,80},{80,64},{96,112},{112,96},{1... | collective-permute-start | bytes 786440 | tf_op jit(solution)/shard_map/ppermute | solution.py:42
  6.1 3.4 %collective-permute-start.3 = (bf16[4,128,128]{2,1,0:T(8,128)(2,1)S(1)}, bf16[4,128,128]{2,1,0:T(8,128)(2,1)S(1)}, u32[]{:S(2)}, u32[]{:S(2)}) collective-permute-start(bf16[4,128,128]{2,1,0:T(8,128)(2,1)S(1)} %get-tuple-element.68), channel_id=1, source_target_pairs={{0,1},{1,0},{2,3},{3,2},{4,5},{5,4},{6,7},{7,6},{8,9},{9,8},{10,11... | collective-permute-start | bytes 393224 | tf_op jit(solution)/shard_map/ppermute | solution.py:42
  8.0 13.4 %collective-permute-start.6 = (bf16[8,64,256]{2,1,0:T(8,128)(2,1)S(1)}, bf16[8,64,256]{2,1,0:T(8,128)(2,1)S(1)}, u32[]{:S(2)}, u32[]{:S(2)}) collective-permute-start(bf16[8,64,256]{2,1,0:T(8,128)(2,1)S(1)} %relay_0.6.refs_8_), channel_id=1, source_target_pairs={{0,16},{16,0},{32,48},{48,32},{64,80},{80,64},{96,112},{112,96},{1... | collective-permute-start | bytes 786440 | tf_op jit(solution)/shard_map/ppermute | solution.py:42
  16.4 9.2 %collective-permute-start.5 = (bf16[8,64,256]{2,1,0:T(8,128)(2,1)S(1)}, bf16[8,64,256]{2,1,0:T(8,128)(2,1)S(1)}, u32[]{:S(2)}, u32[]{:S(2)}) collective-permute-start(bf16[8,64,256]{2,1,0:T(8,128)(2,1)S(1)} %get-tuple-element.71), channel_id=1, source_target_pairs={{0,32},{16,48},{32,0},{48,16},{64,96},{80,112},{96,64},{112,80},{1... | collective-permute-start | bytes 786440 | tf_op jit(solution)/shard_map/ppermute | solution.py:42
  18.4 8.5 %collective-permute-start.2 = (bf16[8,64,256]{2,1,0:T(8,128)(2,1)S(1)}, bf16[8,64,256]{2,1,0:T(8,128)(2,1)S(1)}, u32[]{:S(2)}, u32[]{:S(2)}) collective-permute-start(bf16[8,64,256]{2,1,0:T(8,128)(2,1)S(1)} %relay_0.5.refs_2_), channel_id=1, source_target_pairs={{0,16},{16,0},{32,48},{48,32},{64,80},{80,64},{96,112},{112,96},{1... | collective-permute-start | bytes 786440 | tf_op jit(solution)/shard_map/ppermute | solution.py:42
  19.8 9.8 %collective-permute-start.11 = (bf16[4,128,128]{2,1,0:T(8,128)(2,1)S(1)}, bf16[4,128,128]{2,1,0:T(8,128)(2,1)S(1)}, u32[]{:S(2)}, u32[]{:S(2)}) collective-permute-start(bf16[4,128,128]{2,1,0:T(8,128)(2,1)S(1)} %get-tuple-element.81), channel_id=1, source_target_pairs={{0,2},{1,3},{2,0},{3,1},{4,6},{5,7},{6,4},{7,5},{8,10},{9,11},{10,... | collective-permute-start | bytes 393224 | tf_op jit(solution)/shard_map/ppermute | solution.py:42
  22.4 8.6 %collective-permute-start.8 = (bf16[4,64,256]{2,1,0:T(8,128)(2,1)S(1)}, bf16[4,64,256]{2,1,0:T(8,128)(2,1)S(1)}, u32[]{:S(2)}, u32[]{:S(2)}) collective-permute-start(bf16[4,64,256]{2,1,0:T(8,128)(2,1)S(1)} %get-tuple-element.76), channel_id=1, source_target_pairs={{0,32},{16,48},{32,0},{48,16},{64,96},{80,112},{96,64},{112,80},{1... | collective-permute-start | bytes 393224 | tf_op jit(solution)/shard_map/ppermute | solution.py:42
  24.0 8.4 %collective-permute-start.9 = (bf16[4,64,256]{2,1,0:T(8,128)(2,1)S(1)}, bf16[4,64,256]{2,1,0:T(8,128)(2,1)S(1)}, u32[]{:S(2)}, u32[]{:S(2)}) collective-permute-start(bf16[4,64,256]{2,1,0:T(8,128)(2,1)S(1)} %get-tuple-element.77), channel_id=1, source_target_pairs={{0,2},{1,3},{2,0},{3,1},{4,6},{5,7},{6,4},{7,5},{8,10},{9,11},{10,... | collective-permute-start | bytes 393224 | tf_op jit(solution)/shard_map/ppermute | solution.py:42
  25.6 6.8 %collective-permute-start.10 = (bf16[4,64,256]{2,1,0:T(8,128)(2,1)S(1)}, bf16[4,64,256]{2,1,0:T(8,128)(2,1)S(1)}, u32[]{:S(2)}, u32[]{:S(2)}) collective-permute-start(bf16[4,64,256]{2,1,0:T(8,128)(2,1)S(1)} %get-tuple-element.78), channel_id=1, source_target_pairs={{0,34},{1,35},{2,32},{3,33},{4,38},{5,39},{6,36},{7,37},{8,42},{9,... | collective-permute-start | bytes 393224 | tf_op jit(solution)/shard_map/ppermute | solution.py:48
  28.0 9.8 %collective-permute-start.7 = (bf16[8,64,256]{2,1,0:T(8,128)(2,1)S(1)}, bf16[8,64,256]{2,1,0:T(8,128)(2,1)S(1)}, u32[]{:S(2)}, u32[]{:S(2)}) collective-permute-start(bf16[8,64,256]{2,1,0:T(8,128)(2,1)S(1)} %relay_0.7.refs_9_), channel_id=1, source_target_pairs={{0,16},{16,0},{32,48},{48,32},{64,80},{80,64},{96,112},{112,96},{1... | collective-permute-start | bytes 786440 | tf_op jit(solution)/shard_map/ppermute | solution.py:42
  29.6 11.8 %collective-permute-start.15 = (bf16[8,64,256]{2,1,0:T(8,128)(2,1)S(1)}, bf16[8,64,256]{2,1,0:T(8,128)(2,1)S(1)}, u32[]{:S(2)}, u32[]{:S(2)}) collective-permute-start(bf16[8,64,256]{2,1,0:T(8,128)(2,1)S(1)} %get-tuple-element.87), channel_id=1, source_target_pairs={{0,2},{1,3},{2,0},{3,1},{4,6},{5,7},{6,4},{7,5},{8,10},{9,11},{10,... | collective-permute-start | bytes 786440 | tf_op jit(solution)/shard_map/ppermute | solution.py:42
  33.5 20.8 %collective-permute-start.20 = (bf16[8,64,256]{2,1,0:T(8,128)(2,1)S(1)}, bf16[8,64,256]{2,1,0:T(8,128)(2,1)S(1)}, u32[]{:S(2)}, u32[]{:S(2)}) collective-permute-start(bf16[8,64,256]{2,1,0:T(8,128)(2,1)S(1)} %get-tuple-element.95), channel_id=1, source_target_pairs={{0,64},{16,80},{32,96},{48,112},{64,0},{80,16},{96,32},{112,48},{1... | collective-permute-start | bytes 786440 | tf_op jit(solution)/shard_map/ppermute | solution.py:42
  36.8 8.6 %collective-permute-start.21 = (bf16[4,64,256]{2,1,0:T(8,128)(2,1)S(1)}, bf16[4,64,256]{2,1,0:T(8,128)(2,1)S(1)}, u32[]{:S(2)}, u32[]{:S(2)}) collective-permute-start(bf16[4,64,256]{2,1,0:T(8,128)(2,1)S(1)} %get-tuple-element.96), channel_id=1, source_target_pairs={{0,32},{16,48},{32,0},{48,16},{64,96},{80,112},{96,64},{112,80},{1... | collective-permute-start | bytes 393224 | tf_op jit(solution)/shard_map/ppermute | solution.py:42
  36.8 11.1 %collective-permute-start.22 = (bf16[4,64,256]{2,1,0:T(8,128)(2,1)S(1)}, bf16[4,64,256]{2,1,0:T(8,128)(2,1)S(1)}, u32[]{:S(2)}, u32[]{:S(2)}) collective-permute-start(bf16[4,64,256]{2,1,0:T(8,128)(2,1)S(1)} %get-tuple-element.97), channel_id=1, source_target_pairs={{0,2},{1,3},{2,0},{3,1},{4,6},{5,7},{6,4},{7,5},{8,10},{9,11},{10,... | collective-permute-start | bytes 393224 | tf_op jit(solution)/shard_map/ppermute | solution.py:42
  37.9 12.5 %collective-permute-start.23 = (bf16[4,64,256]{2,1,0:T(8,128)(2,1)S(1)}, bf16[4,64,256]{2,1,0:T(8,128)(2,1)S(1)}, u32[]{:S(2)}, u32[]{:S(2)}) collective-permute-start(bf16[4,64,256]{2,1,0:T(8,128)(2,1)S(1)} %get-tuple-element.98), channel_id=1, source_target_pairs={{0,34},{1,35},{2,32},{3,33},{4,38},{5,39},{6,36},{7,37},{8,42},{9,... | collective-permute-start | bytes 393224 | tf_op jit(solution)/shard_map/ppermute | solution.py:48
  41.4 14.3 %collective-permute-start.19 = (bf16[4,128,128]{2,1,0:T(8,128)(2,1)S(1)}, bf16[4,128,128]{2,1,0:T(8,128)(2,1)S(1)}, u32[]{:S(2)}, u32[]{:S(2)}) collective-permute-start(bf16[4,128,128]{2,1,0:T(8,128)(2,1)S(1)} %get-tuple-element.94), channel_id=1, source_target_pairs={{0,4},{1,5},{2,6},{3,7},{4,0},{5,1},{6,2},{7,3},{8,12},{9,13},{10,... | collective-permute-start | bytes 393224 | tf_op jit(solution)/shard_map/ppermute | solution.py:42
  45.5 11.5 %collective-permute-start.12 = (bf16[4,64,256]{2,1,0:T(8,128)(2,1)S(1)}, bf16[4,64,256]{2,1,0:T(8,128)(2,1)S(1)}, u32[]{:S(2)}, u32[]{:S(2)}) collective-permute-start(bf16[4,64,256]{2,1,0:T(8,128)(2,1)S(1)} %get-tuple-element.84), channel_id=1, source_target_pairs={{0,32},{16,48},{32,0},{48,16},{64,96},{80,112},{96,64},{112,80},{1... | collective-permute-start | bytes 393224 | tf_op jit(solution)/shard_map/ppermute | solution.py:42
  47.9 11.8 %collective-permute-start.16 = (bf16[4,64,256]{2,1,0:T(8,128)(2,1)S(1)}, bf16[4,64,256]{2,1,0:T(8,128)(2,1)S(1)}, u32[]{:S(2)}, u32[]{:S(2)}) collective-permute-start(bf16[4,64,256]{2,1,0:T(8,128)(2,1)S(1)} %get-tuple-element.89), channel_id=1, source_target_pairs={{0,64},{16,80},{32,96},{48,112},{64,0},{80,16},{96,32},{112,48},{1... | collective-permute-start | bytes 393224 | tf_op jit(solution)/shard_map/ppermute | solution.py:42
  50.4 9.3 %collective-permute-start.17 = (bf16[4,64,256]{2,1,0:T(8,128)(2,1)S(1)}, bf16[4,64,256]{2,1,0:T(8,128)(2,1)S(1)}, u32[]{:S(2)}, u32[]{:S(2)}) collective-permute-start(bf16[4,64,256]{2,1,0:T(8,128)(2,1)S(1)} %get-tuple-element.90), channel_id=1, source_target_pairs={{0,4},{1,5},{2,6},{3,7},{4,0},{5,1},{6,2},{7,3},{8,12},{9,13},{10,... | collective-permute-start | bytes 393224 | tf_op jit(solution)/shard_map/ppermute | solution.py:42
  54.3 10.2 %collective-permute-start.18 = (bf16[4,64,256]{2,1,0:T(8,128)(2,1)S(1)}, bf16[4,64,256]{2,1,0:T(8,128)(2,1)S(1)}, u32[]{:S(2)}, u32[]{:S(2)}) collective-permute-start(bf16[4,64,256]{2,1,0:T(8,128)(2,1)S(1)} %get-tuple-element.91), channel_id=1, source_target_pairs={{0,68},{1,69},{2,70},{3,71},{4,64},{5,65},{6,66},{7,67},{8,76},{9,... | collective-permute-start | bytes 393224 | tf_op jit(solution)/shard_map/ppermute | solution.py:48
  55.7 10.9 %collective-permute-start.13 = (bf16[4,64,256]{2,1,0:T(8,128)(2,1)S(1)}, bf16[4,64,256]{2,1,0:T(8,128)(2,1)S(1)}, u32[]{:S(2)}, u32[]{:S(2)}) collective-permute-start(bf16[4,64,256]{2,1,0:T(8,128)(2,1)S(1)} %get-tuple-element.85), channel_id=1, source_target_pairs={{0,2},{1,3},{2,0},{3,1},{4,6},{5,7},{6,4},{7,5},{8,10},{9,11},{10,... | collective-permute-start | bytes 393224 | tf_op jit(solution)/shard_map/ppermute | solution.py:42
  56.9 13.3 %collective-permute-start.14 = (bf16[4,64,256]{2,1,0:T(8,128)(2,1)S(1)}, bf16[4,64,256]{2,1,0:T(8,128)(2,1)S(1)}, u32[]{:S(2)}, u32[]{:S(2)}) collective-permute-start(bf16[4,64,256]{2,1,0:T(8,128)(2,1)S(1)} %get-tuple-element.86), channel_id=1, source_target_pairs={{0,34},{1,35},{2,32},{3,33},{4,38},{5,39},{6,36},{7,37},{8,42},{9,... | collective-permute-start | bytes 393224 | tf_op jit(solution)/shard_map/ppermute | solution.py:48
  59.7 13.4 %collective-permute-start.27 = (bf16[4,64,256]{2,1,0:T(8,128)(2,1)S(1)}, bf16[4,64,256]{2,1,0:T(8,128)(2,1)S(1)}, u32[]{:S(2)}, u32[]{:S(2)}) collective-permute-start(bf16[4,64,256]{2,1,0:T(8,128)(2,1)S(1)} %get-tuple-element.105), channel_id=1, source_target_pairs={{0,64},{16,80},{32,96},{48,112},{64,0},{80,16},{96,32},{112,48},{1... | collective-permute-start | bytes 393224 | tf_op jit(solution)/shard_map/ppermute | solution.py:42
  59.8 21.9 %collective-permute-start.30 = (bf16[8,64,256]{2,1,0:T(8,128)(2,1)S(1)}, bf16[8,64,256]{2,1,0:T(8,128)(2,1)S(1)}, u32[]{:S(2)}, u32[]{:S(2)}) collective-permute-start(bf16[8,64,256]{2,1,0:T(8,128)(2,1)S(1)} %get-tuple-element.108), channel_id=1, source_target_pairs={{0,4},{1,5},{2,6},{3,7},{4,0},{5,1},{6,2},{7,3},{8,12},{9,13},{10,... | collective-permute-start | bytes 786440 | tf_op jit(solution)/shard_map/ppermute | solution.py:42
  64.4 9.7 %collective-permute-start.28 = (bf16[4,64,256]{2,1,0:T(8,128)(2,1)S(1)}, bf16[4,64,256]{2,1,0:T(8,128)(2,1)S(1)}, u32[]{:S(2)}, u32[]{:S(2)}) collective-permute-start(bf16[4,64,256]{2,1,0:T(8,128)(2,1)S(1)} %get-tuple-element.106), channel_id=1, source_target_pairs={{0,4},{1,5},{2,6},{3,7},{4,0},{5,1},{6,2},{7,3},{8,12},{9,13},{10,... | collective-permute-start | bytes 393224 | tf_op jit(solution)/shard_map/ppermute | solution.py:42
  66.6 14.1 %collective-permute-start.29 = (bf16[4,64,256]{2,1,0:T(8,128)(2,1)S(1)}, bf16[4,64,256]{2,1,0:T(8,128)(2,1)S(1)}, u32[]{:S(2)}, u32[]{:S(2)}) collective-permute-start(bf16[4,64,256]{2,1,0:T(8,128)(2,1)S(1)} %get-tuple-element.107), channel_id=1, source_target_pairs={{0,68},{1,69},{2,70},{3,71},{4,64},{5,65},{6,66},{7,67},{8,76},{9,... | collective-permute-start | bytes 393224 | tf_op jit(solution)/shard_map/ppermute | solution.py:48
  71.3 11.2 %collective-permute-start.24 = (bf16[4,64,256]{2,1,0:T(8,128)(2,1)S(1)}, bf16[4,64,256]{2,1,0:T(8,128)(2,1)S(1)}, u32[]{:S(2)}, u32[]{:S(2)}) collective-permute-start(bf16[4,64,256]{2,1,0:T(8,128)(2,1)S(1)} %get-tuple-element.102), channel_id=1, source_target_pairs={{0,64},{16,80},{32,96},{48,112},{64,0},{80,16},{96,32},{112,48},{1... | collective-permute-start | bytes 393224 | tf_op jit(solution)/shard_map/ppermute | solution.py:42
  73.2 9.3 %collective-permute-start.25 = (bf16[4,64,256]{2,1,0:T(8,128)(2,1)S(1)}, bf16[4,64,256]{2,1,0:T(8,128)(2,1)S(1)}, u32[]{:S(2)}, u32[]{:S(2)}) collective-permute-start(bf16[4,64,256]{2,1,0:T(8,128)(2,1)S(1)} %get-tuple-element.103), channel_id=1, source_target_pairs={{0,4},{1,5},{2,6},{3,7},{4,0},{5,1},{6,2},{7,3},{8,12},{9,13},{10,... | collective-permute-start | bytes 393224 | tf_op jit(solution)/shard_map/ppermute | solution.py:42
  74.1 11.0 %collective-permute-start.26 = (bf16[4,64,256]{2,1,0:T(8,128)(2,1)S(1)}, bf16[4,64,256]{2,1,0:T(8,128)(2,1)S(1)}, u32[]{:S(2)}, u32[]{:S(2)}) collective-permute-start(bf16[4,64,256]{2,1,0:T(8,128)(2,1)S(1)} %get-tuple-element.104), channel_id=1, source_target_pairs={{0,68},{1,69},{2,70},{3,71},{4,64},{5,65},{6,66},{7,67},{8,76},{9,... | collective-permute-start | bytes 393224 | tf_op jit(solution)/shard_map/ppermute | solution.py:48
